TPU v7x, 512 devices: a whole 4x8x8 slice. The times are simulated.
512 devices in a mesh: ctx: 32 (over z, x), tp: 16 (over y, core).
Axes of the slice: x: 4, y: 8, z: 8, core: 2. Of those that a mesh axis runs over, the one named last changes fastest.
Arguments:
- x_heads: bfloat16 [4, 8192, 4096], P(None, ('ctx', 'tp')), may hold values from -6 to 6
- b_keys: bfloat16 [4, 8192, 2048], P(None, ('ctx', 'tp')), may hold values from -6 to 6
- c_queries: bfloat16 [4, 8192, 2048], P(None, ('ctx', 'tp')), may hold values from -0.005859375 to 0.005859375
- log_decay: float32 [4, 8192, 64], P(None, ('ctx', 'tp')), may hold values from -1 to 0, as said below
- level_log: float32 [4, 8192, 896], P(None, ('ctx', 'tp')), may hold values from -1 to 1
- skip_gain: float32 [64], P('tp'), may hold values from 0.1 to 1.9
Outputs:
- mixed: bfloat16 [4, 8192, 4096], P(None, ('ctx', 'tp'))
Inputs may be any that keep to these rules, and one draw needn't show every extreme that they name: `log_decay`: log-decay of each position and head; negative.
All inputs are finite; a program needn't handle non-finite values.
Results may differ from a plain program's by a relative error of at most 0.0036.
Values may be sent and summed in bfloat16 or wider, within the bound.
No kernel may reach another device: no remote copies, remote signals or barrier semaphores. Data moves between devices by JAX's collectives and lax.ppermute only.
A program may use at most 128 MiB of HBM per device.

v0:
```python
import jax
import jax.numpy as jnp
from jax import lax
from jax.sharding import PartitionSpec as P

HEAD_COUNT = 64
STATE = 128
GROUPS = 16


def from_partner(value, axis, bit):
    mask = 2**bit
    pairs = [(source, source ^ mask) for source in range(lax.axis_size(axis))]
    return lax.ppermute(value, axis, pairs)


def level_matrix(length):
    token_position = jnp.arange(length, dtype=jnp.int32)
    xor_bits = jnp.bitwise_xor(token_position[:, None], token_position[None, :])
    levels_of = jnp.zeros((length, length), jnp.int32)
    for bit_power in range(length.bit_length()):
        levels_of = levels_of + (xor_bits >= 1 << bit_power).astype(jnp.int32)
    return levels_of


def local_terms(x_vals, b_vals, c_vals, cum_log, gate_vals, per_group):
    length = x_vals.shape[1]
    dot_scores = jnp.einsum("stgn,sugn->sgtu", c_vals, b_vals, preferred_element_type=jnp.float32)
    dot_heads = jnp.repeat(dot_scores, per_group, axis=1)
    cum_heads = jnp.swapaxes(cum_log, 1, 2)
    log_gap = cum_heads[:, :, :, None] - cum_heads[:, :, None, :]
    token_position = jnp.arange(length, dtype=jnp.int32)
    causal = token_position[:, None] >= token_position[None, :]
    decay_mat = jnp.where(causal, jnp.exp(jnp.where(causal, log_gap, 0.0)), 0.0)
    levels_of = level_matrix(length)
    gate_heads = jnp.transpose(gate_vals, (0, 2, 1, 3))
    picked = jnp.where(levels_of == 0, gate_heads[:, :, :, 0][..., None], 0.0)
    for level_id in range(1, length.bit_length()):
        picked = picked + jnp.where(
            levels_of == level_id, gate_heads[:, :, :, level_id][..., None], 0.0
        )
    scores = (dot_heads * decay_mat * picked).astype(jnp.bfloat16)
    near_part = jnp.einsum("shtu,suhp->sthp", scores, x_vals, preferred_element_type=jnp.float32)
    key_decay = jnp.exp(cum_log[:, -1:, :] - cum_log)
    b_heads = jnp.repeat(b_vals, per_group, axis=2)
    keys_scaled = (b_heads * key_decay[..., None]).astype(jnp.bfloat16)
    states = jnp.einsum("sthn,sthp->shnp", keys_scaled, x_vals, preferred_element_type=jnp.float32)
    return (near_part, states)


def per_device(x_heads, b_keys, c_queries, log_decay, level_log, skip_gain):
    x_local, b_local, c_local = (
        lax.all_to_all(x_heads, "tp", split_axis=2, concat_axis=1, tiled=True),
        lax.all_to_all(b_keys, "tp", split_axis=2, concat_axis=1, tiled=True),
        lax.all_to_all(c_queries, "tp", split_axis=2, concat_axis=1, tiled=True),
    )
    decay_local, gate_local = (
        lax.all_to_all(log_decay, "tp", split_axis=2, concat_axis=1, tiled=True),
        lax.all_to_all(level_log, "tp", split_axis=2, concat_axis=1, tiled=True),
    )
    seq_count, length, width_here = x_local.shape
    heads_here = decay_local.shape[2]
    head_dim = width_here // heads_here
    state_dim = STATE
    groups_here = b_local.shape[2] // state_dim
    per_group = HEAD_COUNT // GROUPS
    levels_all = gate_local.shape[2] // heads_here
    x_vals = x_local.reshape(seq_count, length, heads_here, head_dim)
    b_vals = b_local.reshape(seq_count, length, groups_here, state_dim)
    c_vals = c_local.reshape(seq_count, length, groups_here, state_dim)
    gate_vals = jnp.exp(gate_local.reshape(seq_count, length, heads_here, levels_all))
    cum_log = jnp.cumsum(decay_local, axis=1)
    near_part, states = local_terms(x_vals, b_vals, c_vals, cum_log, gate_vals, per_group)
    totals = cum_log[:, -1, :]
    ctx_size = lax.axis_size("ctx")
    ctx_bits = ctx_size.bit_length() - 1
    near_levels = length.bit_length()
    block_index = lax.axis_index("ctx")
    aggregate, block_log = (states, totals)
    prefix_log = jnp.zeros_like(totals)
    collected = []
    for bit_pos in range(ctx_bits):
        partner, partner_log = from_partner((aggregate, block_log), "ctx", bit_pos)
        upper_half = block_index >> bit_pos & 1 == 1
        collected.append(
            jnp.where(upper_half, jnp.exp(prefix_log)[:, :, None, None] * partner, 0.0).astype(
                jnp.bfloat16
            )
        )
        aggregate = jnp.where(
            upper_half,
            jnp.exp(block_log)[:, :, None, None] * partner + aggregate,
            jnp.exp(partner_log)[:, :, None, None] * aggregate + partner,
        )
        prefix_log = jnp.where(upper_half, prefix_log + partner_log, prefix_log)
        block_log = block_log + partner_log
    level_states = jnp.stack(collected, axis=2)
    c_heads = jnp.repeat(c_vals, per_group, axis=2)
    raw_part = jnp.einsum(
        "sthn,shbnp->sthbp", c_heads, level_states, preferred_element_type=jnp.float32
    )
    far_weight = gate_vals[..., near_levels : near_levels + ctx_bits] * jnp.exp(cum_log)[..., None]
    far_part = jnp.sum(far_weight[..., None] * raw_part, axis=3)
    mixed_out = near_part + far_part + skip_gain[None, None, :, None] * x_vals
    mixed_out = mixed_out.astype(jnp.bfloat16).reshape(seq_count, length, width_here)
    return lax.all_to_all(mixed_out, "tp", split_axis=1, concat_axis=2, tiled=True)


def solution(mesh):
    in_specs = (
        P(None, ("ctx", "tp"), None),
        P(None, ("ctx", "tp"), None),
        P(None, ("ctx", "tp"), None),
        P(None, ("ctx", "tp"), None),
        P(None, ("ctx", "tp"), None),
        P("tp"),
    )
    out_specs = P(None, ("ctx", "tp"), None)
    return jax.shard_map(
        per_device, mesh=mesh, in_specs=in_specs, out_specs=out_specs, check_vma=False
    )
```

profile of v0, /device:TPU:1, one launch (start us, length us, event | category | flops | bytes accessed | tf_op | source)
XLA Modules:
  0.0 239.5 jit_solution(17070430891512451601)
XLA Ops:
  0.0 0.9 copy.141
  0.9 0.7 reshape.117
  1.7 10.2 %all-to-all-start.2 = ((f32[16,1,256]{2,1,0:T(1,128)}), f32[16,1,256]{2,1,0:T(1,128)S(1)}, u32[]{:S(2)}, u32[]{:S(2)}) async-start(f32[16,1,256]{2,1,0:T(1,128)} %reshape.117), calls=%async_computation.2 | async-start | bytes 32768 | tf_op jit(solution)/shard_map/all_to_all | solution.py:58
  11.8 2.7 %copy.138 = bf16[4,16,2048]{1,0,2:T(4,128)(2,1)S(1)} copy(bf16[4,16,2048]{2,1,0:T(8,128)(2,1)} %param.7) | data formatting | bytes 524288 | tf_op args[1]
  14.6 2.8 %reshape.121 = bf16[16,2,4096]{2,1,0:T(2,128)(2,1)} reshape(bf16[2048,4,16]{2,1,0:T(4,128)(2,1)S(1)} %bitcast.117) | data formatting | bytes 524288
  17.4 1.9 all-to-all-done.2
  19.2 5.4 %all-to-all-start.1 = ((bf16[16,2,4096]{2,1,0:T(2,128)(2,1)}), bf16[16,2,4096]{2,1,0:T(2,128)(2,1)S(1)}, u32[]{:S(2)}, u32[]{:S(2)}) async-start(bf16[16,2,4096]{2,1,0:T(2,128)(2,1)} %reshape.121), calls=%async_computation.1 | async-start | bytes 524288 | tf_op jit(solution)/shard_map/all_to_all | solution.py:54
  24.7 1.2 copy.146
  25.9 2.1 reshape.115
  28.0 4.6 %copy.157 = bf16[4,16,4096]{1,0,2:T(4,128)(2,1)} copy(bf16[4,16,4096]{2,1,0:T(8,128)(2,1)S(1)} %copy-done.1) | data formatting | bytes 1048576 | tf_op args[0]
  32.6 6.4 %reshape.119 = bf16[16,2,8192]{2,1,0:T(2,128)(2,1)} reshape(bf16[4096,4,16]{2,1,0:T(4,128)(2,1)} %bitcast.113) | data formatting | bytes 1048576
  39.0 0.8 broadcast_compare_fusion.5
  39.8 0.8 iota_compare_fusion
  41.1 0.7 reduce.3
  42.1 4.8 %reduce-window.6 = f32[4,4,2,128]{3,2,1,0:T(2,128)S(1)} reduce-window(f32[4,4,2,128]{3,2,1,0:T(2,128)S(1)} %reshape.91, f32[]{:T(128)} %constant.17.clone.1), window={size=1x1x1x128 pad=0_0x0_0x0_0x127_0}, to_apply=%region_0.0 | reduce-window | flops 520192 | bytes 32772 | tf_op jit(solution)/shard_map/reduce-window
  47.3 7.2 %all-to-all-start.4 = ((bf16[16,2,8192]{2,1,0:T(2,128)(2,1)}), bf16[16,2,8192]{2,1,0:T(2,128)(2,1)S(1)}, u32[]{:S(2)}, u32[]{:S(2)}) async-start(bf16[16,2,8192]{2,1,0:T(2,128)(2,1)} %reshape.119), calls=%async_computation.4 | async-start | bytes 1048576 | tf_op jit(solution)/shard_map/all_to_all | solution.py:53
  54.8 1.9 collective-permute-start.1
  56.8 2.3 collective-permute-done.1
  59.1 3.1 %collective-permute-start.3 = (f32[4,4]{1,0:T(4,128)S(1)}, f32[4,4]{1,0:T(4,128)S(1)}, u32[]{:S(2)}, u32[]{:S(2)}) collective-permute-start(f32[4,4]{1,0:T(4,128)S(1)} %get-tuple-element.12), channel_id=1, source_target_pairs={{0,32},{16,48},{32,0},{48,16},{64,96},{80,112},{96,64},{112,80},{1... | collective-permute-start | bytes 200 | tf_op jit(solution)/shard_map/ppermute | solution.py:14
  62.2 1.4 reshape.122
  63.7 1.2 copy.172
  64.9 6.9 %all-to-all-done.4 = bf16[16,2,8192]{2,1,0:T(2,128)(2,1)S(1)} async-done(((bf16[16,2,8192]{2,1,0:T(2,128)(2,1)}), bf16[16,2,8192]{2,1,0:T(2,128)(2,1)S(1)}, u32[]{:S(2)}, u32[]{:S(2)}) %all-to-all-start.4) | async-done | bytes 524320 | tf_op jit(solution)/shard_map/all_to_all | solution.py:53
  71.8 4.1 %all-to-all-start.3 = ((f32[16,1,3584]{2,1,0:T(1,128)}), f32[16,1,3584]{2,1,0:T(1,128)}, u32[]{:S(2)}, u32[]{:S(2)}) async-start(f32[16,1,3584]{2,1,0:T(1,128)} %reshape.115), calls=%async_computation.3 | async-start | bytes 458752 | tf_op jit(solution)/shard_map/all_to_all | solution.py:59
  75.9 4.1 %reshape.120 = bf16[4096,4,16]{2,1,0:T(4,128)(2,1)} reshape(bf16[16,2,8192]{2,1,0:T(2,128)(2,1)S(1)} %all-to-all-done.4) | data formatting | bytes 1048576
  80.0 5.5 %copy.158 = bf16[4,16,16,256]{3,1,2,0:T(8,128)(2,1)S(1)} copy(bf16[4,16,16,256]{1,0,3,2:T(4,128)(2,1)} %bitcast.112) | data formatting | bytes 1048576 | tf_op jit(solution)/shard_map/all_to_all | solution.py:53
  86.5 1.0 fusion.30
  87.5 1.9 collective-permute-start
  89.5 3.6 %collective-permute-start.5 = (f32[4,4]{1,0:T(4,128)S(1)}, f32[4,4]{1,0:T(4,128)S(1)}, u32[]{:S(2)}, u32[]{:S(2)}) collective-permute-start(f32[4,4]{1,0:T(4,128)S(1)} %get-tuple-element.10), channel_id=1, source_target_pairs={{0,64},{16,80},{32,96},{48,112},{64,0},{80,16},{96,32},{112,48},{1... | collective-permute-start | bytes 200 | tf_op jit(solution)/shard_map/ppermute | solution.py:14
  93.1 2.7 %copy.135 = bf16[4,16,2048]{1,0,2:T(4,128)(2,1)S(1)} copy(bf16[4,16,2048]{2,1,0:T(8,128)(2,1)} %param.8) | data formatting | bytes 524288 | tf_op args[2]
  96.4 5.8 %collective-permute-start.7 = (f32[4,4]{1,0:T(4,128)S(1)}, f32[4,4]{1,0:T(4,128)S(1)}, u32[]{:S(2)}, u32[]{:S(2)}) collective-permute-start(f32[4,4]{1,0:T(4,128)S(1)} %get-tuple-element.8), channel_id=1, source_target_pairs={{0,128},{16,144},{32,160},{48,176},{64,192},{80,208},{96,224},{112... | collective-permute-start | bytes 200 | tf_op jit(solution)/shard_map/ppermute | solution.py:14
  102.2 2.8 %reshape.123 = bf16[16,2,4096]{2,1,0:T(2,128)(2,1)} reshape(bf16[2048,4,16]{2,1,0:T(4,128)(2,1)S(1)} %bitcast.114) | data formatting | bytes 524288
  105.6 2.0 add_select_fusion.3
  107.6 4.3 %collective-permute-start.2 = (f32[4,4,128,64]{2,3,1,0:T(8,128)}, f32[4,4,128,64]{2,3,1,0:T(8,128)S(1)}, u32[]{:S(2)}, u32[]{:S(2)}) collective-permute-start(f32[4,4,128,64]{2,3,1,0:T(8,128)} %add_select_fusion.3), channel_id=1, source_target_pairs={{0,32},{16,48},{32,0},{48,16},{64,96},{80,112},{96,64},{112,80},{1... | collective-permute-start | bytes 1572872 | tf_op jit(solution)/shard_map/ppermute | solution.py:14
  111.9 0.8 broadcast_compare_fusion.1
  112.7 0.8 broadcast_compare_fusion.3
  113.5 0.8 broadcast_compare_fusion.7
  114.9 7.2 %all-to-all-start = ((bf16[16,2,4096]{2,1,0:T(2,128)(2,1)}), bf16[16,2,4096]{2,1,0:T(2,128)(2,1)}, u32[]{:S(2)}, u32[]{:S(2)}) async-start(bf16[16,2,4096]{2,1,0:T(2,128)(2,1)} %reshape.123), calls=%async_computation | async-start | bytes 524288 | tf_op jit(solution)/shard_map/all_to_all | solution.py:55
  122.0 2.1 reduce.2
  124.2 1.3 reshape.116
  125.5 2.0 add_select_fusion.2
  127.5 2.5 %collective-permute-start.4 = (f32[4,4,128,64]{2,3,1,0:T(8,128)}, f32[4,4,128,64]{2,3,1,0:T(8,128)}, u32[]{:S(2)}, u32[]{:S(2)}) collective-permute-start(f32[4,4,128,64]{2,3,1,0:T(8,128)} %add_select_fusion.2), channel_id=1, source_target_pairs={{0,64},{16,80},{32,96},{48,112},{64,0},{80,16},{96,32},{112,48},{1... | collective-permute-start | bytes 1572872 | tf_op jit(solution)/shard_map/ppermute | solution.py:14
  130.4 1.1 copy.177
  131.5 0.7 exp.65
  132.3 10.8 %collective-permute-done.4 = f32[4,4,128,64]{2,3,1,0:T(8,128)} collective-permute-done((f32[4,4,128,64]{2,3,1,0:T(8,128)}, f32[4,4,128,64]{2,3,1,0:T(8,128)}, u32[]{:S(2)}, u32[]{:S(2)}) %collective-permute-start.4) | collective-permute-done | bytes 524320 | tf_op jit(solution)/shard_map/ppermute | solution.py:14
  143.0 2.2 add_select_fusion.1
  145.2 3.3 %collective-permute-start.6 = (f32[4,4,128,64]{2,3,1,0:T(8,128)}, f32[4,4,128,64]{2,3,1,0:T(8,128)}, u32[]{:S(2)}, u32[]{:S(2)}) collective-permute-start(f32[4,4,128,64]{2,3,1,0:T(8,128)} %add_select_fusion.1), channel_id=1, source_target_pairs={{0,128},{16,144},{32,160},{48,176},{64,192},{80,208},{96,224},{112... | collective-permute-start | bytes 1572872 | tf_op jit(solution)/shard_map/ppermute | solution.py:14
  149.2 0.6 copy.155
  149.8 0.6 copy.154
  150.4 0.6 copy.153
  152.8 0.6 copy.149
  154.0 4.2 %reshape.124 = bf16[2048,4,16]{2,1,0:T(4,128)(2,1)S(1)} reshape(bf16[16,2,4096]{2,1,0:T(2,128)(2,1)} %all-to-all-done) | data formatting | bytes 524288
  158.2 2.1 copy.170
  160.4 1.3 fusion.62
  161.8 11.3 %collective-permute-done.6 = f32[4,4,128,64]{2,3,1,0:T(8,128)} collective-permute-done((f32[4,4,128,64]{2,3,1,0:T(8,128)}, f32[4,4,128,64]{2,3,1,0:T(8,128)}, u32[]{:S(2)}, u32[]{:S(2)}) %collective-permute-start.6) | collective-permute-done | bytes 524320 | tf_op jit(solution)/shard_map/ppermute | solution.py:14
  173.0 1.4 add_select_fusion
  174.6 8.1 %collective-permute-start.8 = (f32[4,4,128,64]{2,3,1,0:T(8,128)S(1)}, f32[4,4,128,64]{2,3,1,0:T(8,128)S(1)}, u32[]{:S(2)}, u32[]{:S(2)}) collective-permute-start(f32[4,4,128,64]{2,3,1,0:T(8,128)S(1)} %add_select_fusion), channel_id=1, source_target_pairs={{0,256},{16,272},{32,288},{48,304},{64,320},{80,336},{96,352},{112... | collective-permute-start | bytes 1572872 | tf_op jit(solution)/shard_map/ppermute | solution.py:14
  182.7 0.8 fusion.38
  183.5 1.2 fusion.40
  184.7 1.2 fusion.42
  185.9 19.6 %collective-permute-done.8 = f32[4,4,128,64]{2,3,1,0:T(8,128)S(1)} collective-permute-done((f32[4,4,128,64]{2,3,1,0:T(8,128)S(1)}, f32[4,4,128,64]{2,3,1,0:T(8,128)S(1)}, u32[]{:S(2)}, u32[]{:S(2)}) %collective-permute-start.8) | collective-permute-done | bytes 524320 | tf_op jit(solution)/shard_map/ppermute | solution.py:14
  205.6 0.9 fusion
  206.7 6.4 %fusion.29 = bf16[4,256,4,64]{1,3,2,0:T(8,128)(2,1)S(1)} fusion(f32[4,256,4,64]{1,3,2,0:T(8,128)S(1)} %fusion, bf16[4,256,4,64]{1,3,2,0:T(8,128)(2,1)S(1)} %copy.159, f32[4,4,256]{2,1,0:T(4,128)S(1)} %copy-done.13, f32[4,4,256]{2,1,0:T(4,128)S(1)} %copy-done.14, f32[4,4,256]{2,1,0:T(4,128)S(1)} %copy-done.15, f32[4,4,256]{2,1,0:T(4,128)S(1)} %copy-done.16, ...), kind=kOutput, calls=%fused_computation.33 | convolution fusion | flops 159645696 | bytes 3964944 | tf_op jit(solution)/shard_map/shtu,suhp->sthp/dot_general | solution.py:43
  213.4 25.2 %all_to_all.90 = bf16[4,256,256]{2,0,1:T(4,128)(2,1)S(1)} all-to-all(bf16[4,256,256]{2,0,1:T(4,128)(2,1)S(1)} %copy.165), channel_id=1, replica_groups=mesh['ctx'=32,'tp'=16] {'tp'}, dimensions={1} | all-to-all | bytes 1048576 | tf_op jit(solution)/shard_map/all_to_all | solution.py:106
  238.7 0.8 copy.173
  (97 shorter events, 8.6 us)
Async XLA Ops:
  0.0 24.6 %copy-start.2 = (f32[4,16,896]{2,1,0:T(8,128)S(1)}, f32[4,16,896]{2,1,0:T(8,128)}, u32[]{:S(2)}) copy-start(f32[4,16,896]{2,1,0:T(8,128)} %param.10) | copy-start | bytes 688132
  1.7 17.6 %all-to-all-start.2 = ((f32[16,1,256]{2,1,0:T(1,128)}), f32[16,1,256]{2,1,0:T(1,128)S(1)}, u32[]{:S(2)}, u32[]{:S(2)}) async-start(f32[16,1,256]{2,1,0:T(1,128)} %reshape.117), calls=%async_computation.2 | async-start | bytes 32768 | tf_op jit(solution)/shard_map/all_to_all | solution.py:58
  11.8 16.1 %copy-start.1 = (bf16[4,16,4096]{2,1,0:T(8,128)(2,1)S(1)}, bf16[4,16,4096]{2,1,0:T(8,128)(2,1)}, u32[]{:S(2)}) copy-start(bf16[4,16,4096]{2,1,0:T(8,128)(2,1)} %param.6) | copy-start | bytes 1572868
  19.2 28.1 %all-to-all-start.1 = ((bf16[16,2,4096]{2,1,0:T(2,128)(2,1)}), bf16[16,2,4096]{2,1,0:T(2,128)(2,1)S(1)}, u32[]{:S(2)}, u32[]{:S(2)}) async-start(bf16[16,2,4096]{2,1,0:T(2,128)(2,1)} %reshape.121), calls=%async_computation.1 | async-start | bytes 524288 | tf_op jit(solution)/shard_map/all_to_all | solution.py:54
  47.3 24.6 %all-to-all-start.4 = ((bf16[16,2,8192]{2,1,0:T(2,128)(2,1)}), bf16[16,2,8192]{2,1,0:T(2,128)(2,1)S(1)}, u32[]{:S(2)}, u32[]{:S(2)}) async-start(bf16[16,2,8192]{2,1,0:T(2,128)(2,1)} %reshape.119), calls=%async_computation.4 | async-start | bytes 1048576 | tf_op jit(solution)/shard_map/all_to_all | solution.py:53
  54.8 4.3 %collective-permute-start.1 = (f32[4,4]{1,0:T(4,128)S(1)}, f32[4,4]{1,0:T(4,128)S(1)}, u32[]{:S(2)}, u32[]{:S(2)}) collective-permute-start(f32[4,4]{1,0:T(4,128)S(1)} %slice_reduce_fusion), channel_id=1, source_target_pairs={{0,16},{16,0},{32,48},{48,32},{64,80},{80,64},{96,112},{112,96},{1... | collective-permute-start | bytes 200 | tf_op jit(solution)/shard_map/ppermute | solution.py:14
  59.1 30.3 %collective-permute-start.3 = (f32[4,4]{1,0:T(4,128)S(1)}, f32[4,4]{1,0:T(4,128)S(1)}, u32[]{:S(2)}, u32[]{:S(2)}) collective-permute-start(f32[4,4]{1,0:T(4,128)S(1)} %get-tuple-element.12), channel_id=1, source_target_pairs={{0,32},{16,48},{32,0},{48,16},{64,96},{80,112},{96,64},{112,80},{1... | collective-permute-start | bytes 200 | tf_op jit(solution)/shard_map/ppermute | solution.py:14
  71.8 43.0 %all-to-all-start.3 = ((f32[16,1,3584]{2,1,0:T(1,128)}), f32[16,1,3584]{2,1,0:T(1,128)}, u32[]{:S(2)}, u32[]{:S(2)}) async-start(f32[16,1,3584]{2,1,0:T(1,128)} %reshape.115), calls=%async_computation.3 | async-start | bytes 458752 | tf_op jit(solution)/shard_map/all_to_all | solution.py:59
  87.5 18.1 %collective-permute-start = (f32[4,4,128,64]{2,3,1,0:T(8,128)S(1)}, f32[4,4,128,64]{2,3,1,0:T(8,128)}, u32[]{:S(2)}, u32[]{:S(2)}) collective-permute-start(f32[4,4,128,64]{2,3,1,0:T(8,128)S(1)} %fusion.30), channel_id=1, source_target_pairs={{0,16},{16,0},{32,48},{48,32},{64,80},{80,64},{96,112},{112,96},{1... | collective-permute-start | bytes 1572872 | tf_op jit(solution)/shard_map/ppermute | solution.py:14
  89.5 6.3 %collective-permute-start.5 = (f32[4,4]{1,0:T(4,128)S(1)}, f32[4,4]{1,0:T(4,128)S(1)}, u32[]{:S(2)}, u32[]{:S(2)}) collective-permute-start(f32[4,4]{1,0:T(4,128)S(1)} %get-tuple-element.10), channel_id=1, source_target_pairs={{0,64},{16,80},{32,96},{48,112},{64,0},{80,16},{96,32},{112,48},{1... | collective-permute-start | bytes 200 | tf_op jit(solution)/shard_map/ppermute | solution.py:14
  96.4 8.6 %collective-permute-start.7 = (f32[4,4]{1,0:T(4,128)S(1)}, f32[4,4]{1,0:T(4,128)S(1)}, u32[]{:S(2)}, u32[]{:S(2)}) collective-permute-start(f32[4,4]{1,0:T(4,128)S(1)} %get-tuple-element.8), channel_id=1, source_target_pairs={{0,128},{16,144},{32,160},{48,176},{64,192},{80,208},{96,224},{112... | collective-permute-start | bytes 200 | tf_op jit(solution)/shard_map/ppermute | solution.py:14
  107.6 17.9 %collective-permute-start.2 = (f32[4,4,128,64]{2,3,1,0:T(8,128)}, f32[4,4,128,64]{2,3,1,0:T(8,128)S(1)}, u32[]{:S(2)}, u32[]{:S(2)}) collective-permute-start(f32[4,4,128,64]{2,3,1,0:T(8,128)} %add_select_fusion.3), channel_id=1, source_target_pairs={{0,32},{16,48},{32,0},{48,16},{64,96},{80,112},{96,64},{112,80},{1... | collective-permute-start | bytes 1572872 | tf_op jit(solution)/shard_map/ppermute | solution.py:14
  114.9 39.1 %all-to-all-start = ((bf16[16,2,4096]{2,1,0:T(2,128)(2,1)}), bf16[16,2,4096]{2,1,0:T(2,128)(2,1)}, u32[]{:S(2)}, u32[]{:S(2)}) async-start(bf16[16,2,4096]{2,1,0:T(2,128)(2,1)} %reshape.123), calls=%async_computation | async-start | bytes 524288 | tf_op jit(solution)/shard_map/all_to_all | solution.py:55
  127.5 15.6 %collective-permute-start.4 = (f32[4,4,128,64]{2,3,1,0:T(8,128)}, f32[4,4,128,64]{2,3,1,0:T(8,128)}, u32[]{:S(2)}, u32[]{:S(2)}) collective-permute-start(f32[4,4,128,64]{2,3,1,0:T(8,128)} %add_select_fusion.2), channel_id=1, source_target_pairs={{0,64},{16,80},{32,96},{48,112},{64,0},{80,16},{96,32},{112,48},{1... | collective-permute-start | bytes 1572872 | tf_op jit(solution)/shard_map/ppermute | solution.py:14
  145.2 27.8 %collective-permute-start.6 = (f32[4,4,128,64]{2,3,1,0:T(8,128)}, f32[4,4,128,64]{2,3,1,0:T(8,128)}, u32[]{:S(2)}, u32[]{:S(2)}) collective-permute-start(f32[4,4,128,64]{2,3,1,0:T(8,128)} %add_select_fusion.1), channel_id=1, source_target_pairs={{0,128},{16,144},{32,160},{48,176},{64,192},{80,208},{96,224},{112... | collective-permute-start | bytes 1572872 | tf_op jit(solution)/shard_map/ppermute | solution.py:14
  160.4 23.1 %copy-start.24 = (f32[4,4]{1,0:T(4,128)S(1)}, f32[4,4]{1,0:T(4,128)}, u32[]{:S(2)}) copy-start(f32[4,4]{1,0:T(4,128)} %get-tuple-element.30) | copy-start | bytes 196
  160.4 24.3 %copy-start.23 = (f32[4,4]{1,0:T(4,128)S(1)}, f32[4,4]{1,0:T(4,128)}, u32[]{:S(2)}) copy-start(f32[4,4]{1,0:T(4,128)} %get-tuple-element.29) | copy-start | bytes 196
  160.4 45.1 %copy-start.22 = (f32[4,4]{1,0:T(4,128)S(1)}, f32[4,4]{1,0:T(4,128)}, u32[]{:S(2)}) copy-start(f32[4,4]{1,0:T(4,128)} %get-tuple-element.5) | copy-start | bytes 196
  160.4 45.3 %copy-start = (bf16[4,16,16,128]{3,1,2,0:T(8,128)(2,1)S(1)}, bf16[4,16,16,128]{3,1,2,0:T(8,128)(2,1)}, u32[]{:S(2)}) copy-start(bf16[4,16,16,128]{3,1,2,0:T(8,128)(2,1)} %copy.170) | copy-start | bytes 786436
  174.4 32.1 %copy-start.3 = (pred[256,256]{1,0:T(8,128)(4,1)S(1)}, pred[256,256]{1,0:T(8,128)(4,1)}, u32[]{:S(2)}) copy-start(pred[256,256]{1,0:T(8,128)(4,1)} %get-tuple-element.38) | copy-start | bytes 196612
  174.4 32.1 %copy-start.4 = (pred[256,256]{1,0:T(8,128)(4,1)S(1)}, pred[256,256]{1,0:T(8,128)(4,1)}, u32[]{:S(2)}) copy-start(pred[256,256]{1,0:T(8,128)(4,1)} %get-tuple-element.39) | copy-start | bytes 196612
  174.4 32.1 %copy-start.5 = (pred[256,256]{1,0:T(8,128)(4,1)S(1)}, pred[256,256]{1,0:T(8,128)(4,1)}, u32[]{:S(2)}) copy-start(pred[256,256]{1,0:T(8,128)(4,1)} %get-tuple-element.32) | copy-start | bytes 196612
  174.4 32.1 %copy-start.6 = (pred[256,256]{1,0:T(8,128)(4,1)S(1)}, pred[256,256]{1,0:T(8,128)(4,1)}, u32[]{:S(2)}) copy-start(pred[256,256]{1,0:T(8,128)(4,1)} %get-tuple-element.33) | copy-start | bytes 196612
  174.4 32.1 %copy-start.7 = (pred[256,256]{1,0:T(8,128)(4,1)S(1)}, pred[256,256]{1,0:T(8,128)(4,1)}, u32[]{:S(2)}) copy-start(pred[256,256]{1,0:T(8,128)(4,1)} %get-tuple-element.34) | copy-start | bytes 196612
  174.4 32.1 %copy-start.8 = (pred[256,256]{1,0:T(8,128)(4,1)S(1)}, pred[256,256]{1,0:T(8,128)(4,1)}, u32[]{:S(2)}) copy-start(pred[256,256]{1,0:T(8,128)(4,1)} %get-tuple-element.35) | copy-start | bytes 196612
  174.5 32.1 %copy-start.9 = (pred[256,256]{1,0:T(8,128)(4,1)S(1)}, pred[256,256]{1,0:T(8,128)(4,1)}, u32[]{:S(2)}) copy-start(pred[256,256]{1,0:T(8,128)(4,1)} %get-tuple-element.36) | copy-start | bytes 196612
  174.5 32.1 %copy-start.10 = (pred[256,256]{1,0:T(8,128)(4,1)S(1)}, pred[256,256]{1,0:T(8,128)(4,1)}, u32[]{:S(2)}) copy-start(pred[256,256]{1,0:T(8,128)(4,1)} %get-tuple-element.37) | copy-start | bytes 196612
  174.5 32.1 %copy-start.11 = (pred[256,256]{1,0:T(8,128)(4,1)S(1)}, pred[256,256]{1,0:T(8,128)(4,1)}, u32[]{:S(2)}) copy-start(pred[256,256]{1,0:T(8,128)(4,1)} %get-tuple-element.40) | copy-start | bytes 196612
  174.5 32.1 %copy-start.12 = (pred[256,256]{1,0:T(8,128)(4,1)S(1)}, pred[256,256]{1,0:T(8,128)(4,1)}, u32[]{:S(2)}) copy-start(pred[256,256]{1,0:T(8,128)(4,1)} %get-tuple-element.41) | copy-start | bytes 196612
  174.5 32.1 %copy-start.13 = (f32[4,4,256]{2,1,0:T(4,128)S(1)}, f32[4,4,256]{2,1,0:T(4,128)}, u32[]{:S(2)}) copy-start(f32[4,4,256]{2,1,0:T(4,128)} %copy.156) | copy-start | bytes 49156
  174.5 32.1 %copy-start.14 = (f32[4,4,256]{2,1,0:T(4,128)S(1)}, f32[4,4,256]{2,1,0:T(4,128)}, u32[]{:S(2)}) copy-start(f32[4,4,256]{2,1,0:T(4,128)} %copy.155) | copy-start | bytes 49156
  174.5 32.1 %copy-start.15 = (f32[4,4,256]{2,1,0:T(4,128)S(1)}, f32[4,4,256]{2,1,0:T(4,128)}, u32[]{:S(2)}) copy-start(f32[4,4,256]{2,1,0:T(4,128)} %copy.154) | copy-start | bytes 49156
  174.5 32.1 %copy-start.16 = (f32[4,4,256]{2,1,0:T(4,128)S(1)}, f32[4,4,256]{2,1,0:T(4,128)}, u32[]{:S(2)}) copy-start(f32[4,4,256]{2,1,0:T(4,128)} %copy.153) | copy-start | bytes 49156
  174.5 32.1 %copy-start.17 = (f32[4,4,256]{2,1,0:T(4,128)S(1)}, f32[4,4,256]{2,1,0:T(4,128)}, u32[]{:S(2)}) copy-start(f32[4,4,256]{2,1,0:T(4,128)} %copy.152) | copy-start | bytes 49156
  174.5 32.1 %copy-start.18 = (f32[4,4,256]{2,1,0:T(4,128)S(1)}, f32[4,4,256]{2,1,0:T(4,128)}, u32[]{:S(2)}) copy-start(f32[4,4,256]{2,1,0:T(4,128)} %copy.151) | copy-start | bytes 49156
  174.6 32.1 %copy-start.19 = (f32[4,4,256]{2,1,0:T(4,128)S(1)}, f32[4,4,256]{2,1,0:T(4,128)}, u32[]{:S(2)}) copy-start(f32[4,4,256]{2,1,0:T(4,128)} %copy.150) | copy-start | bytes 49156
  174.6 32.1 %copy-start.20 = (f32[4,4,256]{2,1,0:T(4,128)S(1)}, f32[4,4,256]{2,1,0:T(4,128)}, u32[]{:S(2)}) copy-start(f32[4,4,256]{2,1,0:T(4,128)} %copy.149) | copy-start | bytes 49156
  174.6 32.1 %copy-start.21 = (f32[4,4,256]{2,1,0:T(4,128)S(1)}, f32[4,4,256]{2,1,0:T(4,128)}, u32[]{:S(2)}) copy-start(f32[4,4,256]{2,1,0:T(4,128)} %copy.148) | copy-start | bytes 49156
  174.6 32.1 %copy-start.25 = (f32[4]{0:T(128)S(1)}, f32[4]{0:T(128)}, u32[]{:S(2)}) copy-start(f32[4]{0:T(128)} %param.11) | copy-start | bytes 52
  174.6 30.9 %collective-permute-start.8 = (f32[4,4,128,64]{2,3,1,0:T(8,128)S(1)}, f32[4,4,128,64]{2,3,1,0:T(8,128)S(1)}, u32[]{:S(2)}, u32[]{:S(2)}) collective-permute-start(f32[4,4,128,64]{2,3,1,0:T(8,128)S(1)} %add_select_fusion), channel_id=1, source_target_pairs={{0,256},{16,272},{32,288},{48,304},{64,320},{80,336},{96,352},{112... | collective-permute-start | bytes 1572872 | tf_op jit(solution)/shard_map/ppermute | solution.py:14
where the time goes:
time: 241 us; the launch traced here: 240 us
  starting transfers between devices  68.5 us (28%)
  local copies, waits for them, and re-layouts  58.2 us (24%)
  waiting for transfers between devices  52.7 us (22%)
  blocking collectives  25.2 us (10%)
  other arithmetic  24.5 us (10%)
  matrix products  9.57 us (4%)
    ppermute x9, waiting for transfers between devices, from_partner(): return lax.ppermute(value, axis, pairs)  43.9 us
    unnamed x67, local copies, waits for them, and re-layouts  38.3 us
    ppermute x9, starting transfers between devices, from_partner(): return lax.ppermute(value, axis, pairs)  34.5 us
    all_to_all x1, blocking collectives, per_device(): lax.all_to_all(mixed_out, 'tp', split_axis=1, concat_axis=2, tiled=True)  25.2 us
    all_to_all x1, starting transfers between devices, per_device(): lax.all_to_all(log_decay, 'tp', split_axis=2, concat_axis=1, tiled=True)  10.2 us
    select_n x4, other arithmetic, per_device(): jnp.where(upper_half, jnp.exp(block_log)[:, :, None, None] * partner + ag...  7.51 us
    all_to_all x1, starting transfers between devices, per_device(): lax.all_to_all(x_heads, 'tp', split_axis=2, concat_axis=1, tiled=True)  7.24 us
    all_to_all x1, starting transfers between devices, per_device(): lax.all_to_all(c_queries, 'tp', split_axis=2, concat_axis=1, tiled=True)  7.17 us
  transfers between devices with their start and end apart: 14, of which 6 were waited for; matrix products, arithmetic and copies ran while one was open for 34% of the time, Pallas kernels for 0%

commit v1 on v0

v1 whole, which is shorter than its diff:
```python
import functools

import jax
import jax.numpy as jnp
from jax import lax
from jax.experimental import pallas as pl
from jax.experimental.pallas import tpu as pltpu
from jax.sharding import Mesh
from jax.sharding import PartitionSpec as P

SEQS = 4
HEADS = 64
HEAD_DIM = 64
STATE = 128
GROUPS = 16
PER_GROUP = 4
LEVELS = 14
NEAR_LEVELS = 9
CHUNK = 1024
BLOCK = 256
SUB = 64
ROWS = 72
WIDTH = PER_GROUP * HEAD_DIM
GATES = PER_GROUP * LEVELS
F32 = jnp.float32
BF16 = jnp.bfloat16
VMEM_LIMIT = 48 * 1024 * 1024


def dot(a, b):
    return jnp.dot(a, b, preferred_element_type=F32)


def dot_t(a, b):
    return lax.dot_general(a, b, (((0,), (0,)), ((), ())), preferred_element_type=F32)


def dot_nt(a, b):
    return lax.dot_general(a, b, (((1,), (1,)), ((), ())), preferred_element_type=F32)


def params():
    return pltpu.CompilerParams(vmem_limit_bytes=VMEM_LIMIT)


def pack_kernel(x_ref, b_ref, c_ref, decay_ref, level_ref, out_ref):
    gates = jnp.exp(level_ref[0])
    decay = decay_ref[0]
    high = decay.astype(BF16).astype(F32)
    low = decay - high
    for g in range(GROUPS):
        out_ref[g, 0:16, :] = x_ref[0, :, g * WIDTH : g * WIDTH + 128]
        out_ref[g, 16:32, :] = x_ref[0, :, g * WIDTH + 128 : (g + 1) * WIDTH]
        out_ref[g, 32:48, :] = b_ref[0, :, g * STATE : (g + 1) * STATE]
        out_ref[g, 48:64, :] = c_ref[0, :, g * STATE : (g + 1) * STATE]
        heads = slice(g * PER_GROUP, (g + 1) * PER_GROUP)
        piece = jnp.concatenate(
            [gates[:, g * GATES : (g + 1) * GATES], high[:, heads], low[:, heads]], axis=1
        )
        out_ref[g, 64:72, :] = jnp.concatenate([piece[0:8], piece[8:16]], axis=1).astype(BF16)


def pack(x, b, c, decay, level):
    def spec(arr):
        return pl.BlockSpec((1,) + arr.shape[1:], lambda q: (q, 0, 0))

    return pl.pallas_call(
        pack_kernel,
        grid=(SEQS,),
        in_specs=[spec(a) for a in (x, b, c, decay, level)],
        out_specs=pl.BlockSpec((GROUPS, ROWS, 128), lambda q: (q, 0, 0)),
        out_shape=jax.ShapeDtypeStruct((SEQS * GROUPS, ROWS, 128), BF16),
        compiler_params=params(),
        name="pack_messages",
    )(x, b, c, decay, level)


def load_rows(ref, first, count, start, stop):
    part = ref[pl.ds(first // 16, count // 16), start:stop, :]
    return part.reshape(count, 128)


def load_x(ref, first, count):
    return jnp.concatenate(
        [load_rows(ref, first, count, 0, 16), load_rows(ref, first, count, 16, 32)], axis=1
    )


def load_b(ref, first, count):
    return load_rows(ref, first, count, 32, 48)


def load_c(ref, first, count):
    return load_rows(ref, first, count, 48, 64)


def unpack_gates(ref, gate_ref):
    both = ref[:, 64:72, :].astype(F32)
    gate_ref[:, 0:8, :] = both[:, :, 0:64]
    gate_ref[:, 8:16, :] = both[:, :, 64:128]


def load_gates(gate_ref, first, count):
    return gate_ref[pl.ds(first // 16, count // 16)].reshape(count, 64).astype(BF16)


def spread(offset, stride):
    row = lax.broadcasted_iota(jnp.int32, (64, WIDTH), 0)
    head = lax.broadcasted_iota(jnp.int32, (64, WIDTH), 1) // HEAD_DIM
    return jnp.where(row == offset + stride * head, 1.0, 0.0).astype(BF16)


def chunk_cumsum(gate_ref, cum_ref):
    row = lax.broadcasted_iota(jnp.int32, (BLOCK, BLOCK), 0)
    col = lax.broadcasted_iota(jnp.int32, (BLOCK, BLOCK), 1)
    lower = jnp.where(row >= col, 1.0, 0.0).astype(BF16)
    to_high = spread(GATES, 1)
    to_low = spread(GATES + PER_GROUP, 1)
    offset = jnp.zeros((1, WIDTH), F32)
    for k in range(CHUNK // BLOCK):
        gates = load_gates(gate_ref, k * BLOCK, BLOCK)
        high = dot(gates, to_high).astype(BF16)
        low = dot(gates, to_low).astype(BF16)
        cum = dot(lower, high) + dot(lower, low) + offset
        cum_ref[k * BLOCK : (k + 1) * BLOCK, :] = cum
        offset = cum[BLOCK - 1 :, :]
    return offset


def split_rows(total):
    high = total.astype(BF16).astype(F32)
    middle = (total - high).astype(BF16).astype(F32)
    low = total - high - middle
    row = lax.broadcasted_iota(jnp.int32, (16, WIDTH), 0)
    rows = jnp.where(row == 0, high, jnp.where(row == 1, middle, jnp.where(row == 2, low, 0.0)))
    return rows.astype(BF16)


def message_state(ref):
    return ref[0:STATE, :].astype(F32)


def message_total(ref):
    rows = ref[STATE : STATE + 16, :].astype(F32)
    return rows[0:1] + rows[1:2] + rows[2:3]


def state_kernel(ref, out_ref, gate_ref, cum_ref):
    unpack_gates(ref, gate_ref)
    total = chunk_cumsum(gate_ref, cum_ref)
    state = jnp.zeros((STATE, WIDTH), F32)
    for k in range(CHUNK // BLOCK):
        x = load_x(ref, k * BLOCK, BLOCK).astype(F32)
        tail = jnp.exp(total - cum_ref[k * BLOCK : (k + 1) * BLOCK, :])
        state += dot_t(load_b(ref, k * BLOCK, BLOCK), (x * tail).astype(BF16))
    out_ref[0:STATE, :] = state.astype(BF16)
    out_ref[STATE : STATE + 16, :] = split_rows(total)


def chunk_state(received):
    return pl.pallas_call(
        state_kernel,
        out_shape=jax.ShapeDtypeStruct((STATE + 16, WIDTH), BF16),
        scratch_shapes=[pltpu.VMEM((64, 16, 64), F32), pltpu.VMEM((CHUNK, WIDTH), F32)],
        compiler_params=params(),
        name="chunk_state",
    )(received)


def join_kernel(bits_ref, own_ref, partner_ref, out_ref, *, bit):
    upper = bits_ref[bit] == 1
    own, own_total = message_state(own_ref), message_total(own_ref)
    partner, partner_total = message_state(partner_ref), message_total(partner_ref)
    late_total = jnp.where(upper, own_total, partner_total)
    early = jnp.where(upper, partner, own)
    late = jnp.where(upper, own, partner)
    out_ref[0:STATE, :] = (jnp.exp(late_total) * early + late).astype(BF16)
    out_ref[STATE : STATE + 16, :] = split_rows(own_total + partner_total)


def join(bits, own, partner, bit):
    return pl.pallas_call(
        functools.partial(join_kernel, bit=bit),
        in_specs=[
            pl.BlockSpec(memory_space=pltpu.SMEM),
            pl.BlockSpec(memory_space=pltpu.VMEM),
            pl.BlockSpec(memory_space=pltpu.VMEM),
        ],
        out_shape=jax.ShapeDtypeStruct(own.shape, BF16),
        compiler_params=params(),
        name="join_states",
    )(bits, own, partner)


def inner_kernel(ref, gain_ref, out_ref, grow_ref, gate_ref, cum_ref, state_ref, first_ref):
    unpack_gates(ref, gate_ref)
    chunk_cumsum(gate_ref, cum_ref)
    subs = CHUNK // SUB
    gain = gain_ref[...]

    row = lax.broadcasted_iota(jnp.int32, (SUB, WIDTH), 0)
    col = lax.broadcasted_iota(jnp.int32, (SUB, WIDTH), 1) % SUB
    differ = jnp.bitwise_xor(row, col)
    causal = row >= col
    diagonal = row == col
    head_row = lax.broadcasted_iota(jnp.int32, (PER_GROUP * SUB, WIDTH), 0) // SUB
    head_col = lax.broadcasted_iota(jnp.int32, (PER_GROUP * SUB, WIDTH), 1) // HEAD_DIM
    same_head = head_row == head_col
    spreads = [spread(level, LEVELS) for level in range(7)]

    def one_sub(i, before):
        first = i * SUB
        cum = cum_ref[pl.ds(first, SUB), :]
        last = cum[SUB - 1 :, :]
        x = load_x(ref, first, SUB)
        b = load_b(ref, first, SUB)
        c = load_c(ref, first, SUB)
        gates = load_gates(gate_ref, first, SUB)
        wide_x = x.astype(F32)
        state_ref[i] = dot_t(b, (wide_x * jnp.exp(last - cum)).astype(BF16))
        grow_ref[pl.ds(first, SUB), :] = jnp.exp(cum - before)
        first_ref[pl.ds(i, 1), :] = before
        raw = dot_nt(c, jnp.concatenate([b] * PER_GROUP, axis=0))
        cum_row = jnp.sum(jnp.where(diagonal, cum, 0.0), axis=0, keepdims=True)
        picked = dot(gates, spreads[6])
        for level in range(5, 0, -1):
            picked = jnp.where(differ < (1 << level), dot(gates, spreads[level]), picked)
        picked = jnp.where(diagonal, dot(gates, spreads[0]), picked)
        decay = jnp.exp(jnp.minimum(cum - cum_row, 0.0))
        scores = jnp.where(causal, raw * decay * picked, 0.0).astype(BF16)
        tall_x = jnp.concatenate([x] * PER_GROUP, axis=0)
        block_x = jnp.where(same_head, tall_x, jnp.zeros_like(tall_x))
        out_ref[pl.ds(first, SUB), :] = dot(scores, block_x) + gain * wide_x
        return last

    final = lax.fori_loop(0, subs, one_sub, jnp.zeros((1, WIDTH), F32))

    starts = [first_ref[i : i + 1, :] for i in range(subs)] + [final]
    states = [state_ref[i] for i in range(subs)]
    size = 1
    for bit in range(4):
        to_lanes = spread(7 + bit, LEVELS)
        for group in range(1, subs // size, 2):
            lower = states[group - 1].astype(BF16)
            for part in range(size):
                i = group * size + part
                rows = slice(i * SUB, (i + 1) * SUB)
                weight = dot(load_gates(gate_ref, i * SUB, SUB), to_lanes) * grow_ref[rows, :]
                if part:
                    weight = weight * jnp.exp(starts[i] - starts[group * size])
                out_ref[rows, :] += weight * dot(load_c(ref, i * SUB, SUB), lower)
        states = [
            states[g] * jnp.exp(starts[(g + 2) * size] - starts[(g + 1) * size]) + states[g + 1]
            for g in range(0, subs // size, 2)
        ]
        size *= 2
    for i in range(1, subs):
        rows = slice(i * SUB, (i + 1) * SUB)
        grow_ref[rows, :] = grow_ref[rows, :] * jnp.exp(starts[i])


def inner_part(received, gain):
    wide = jax.ShapeDtypeStruct((CHUNK, WIDTH), F32)
    return pl.pallas_call(
        inner_kernel,
        out_shape=(wide, wide),
        scratch_shapes=[
            pltpu.VMEM((64, 16, 64), F32),
            pltpu.VMEM((CHUNK, WIDTH), F32),
            pltpu.VMEM((CHUNK // SUB, STATE, WIDTH), F32),
            pltpu.VMEM((CHUNK // SUB, WIDTH), F32),
        ],
        compiler_params=params(),
        cost_estimate=pl.CostEstimate(
            flops=2 * CHUNK * WIDTH * 2048, bytes_accessed=4 * 1024 * 1024, transcendentals=10**6
        ),
        name="inner_part",
    )(received, gain)


def outer_kernel(bits_ref, ref, inner_ref, grow_ref, m0_ref, m1_ref, m2_ref, out_ref):
    both = ref[:, 64:72, :].astype(F32)
    gates = jnp.concatenate([both[:, :, 0:64], both[:, :, 64:128]], axis=1)
    gates = gates.reshape(BLOCK, 64).astype(BF16)
    c = load_rows(ref, 0, BLOCK, 48, 64)
    prefix = jnp.zeros((1, WIDTH), F32)
    total = jnp.zeros((BLOCK, WIDTH), F32)
    for bit, message in enumerate((m0_ref, m1_ref, m2_ref)):
        upper = bits_ref[bit] == 1
        level_state = jnp.where(upper, jnp.exp(prefix) * message_state(message), 0.0).astype(BF16)
        prefix = prefix + jnp.where(upper, message_total(message), 0.0)
        total += dot(gates, spread(11 + bit, LEVELS)) * dot(c, level_state)
    mixed = inner_ref[...] + grow_ref[...] * total
    out_ref[...] = mixed.astype(BF16).reshape(BLOCK // 16, 16, WIDTH)


def outer_part(bits, received, inner, grow, messages):
    steps = CHUNK // BLOCK
    wide = pl.BlockSpec((BLOCK, WIDTH), lambda k: (k, 0))
    state = pl.BlockSpec((STATE + 16, WIDTH), lambda k: (0, 0))
    return pl.pallas_call(
        outer_kernel,
        grid=(steps,),
        in_specs=[
            pl.BlockSpec(memory_space=pltpu.SMEM),
            pl.BlockSpec((64 // steps, ROWS, 128), lambda k: (k, 0, 0)),
            wide,
            wide,
            state,
            state,
            state,
        ],
        out_specs=pl.BlockSpec((64 // steps, 16, WIDTH), lambda k: (k, 0, 0)),
        out_shape=jax.ShapeDtypeStruct((64, 16, WIDTH), BF16),
        compiler_params=params(),
        name="outer_part",
    )(bits, received, inner, grow, *messages)


def unpack_kernel(ref, out_ref):
    for g in range(GROUPS):
        out_ref[0, :, g * WIDTH : (g + 1) * WIDTH] = ref[g]


def unpack(received):
    return pl.pallas_call(
        unpack_kernel,
        grid=(SEQS,),
        in_specs=[pl.BlockSpec((GROUPS, 16, WIDTH), lambda q: (q, 0, 0))],
        out_specs=pl.BlockSpec((1, 16, HEADS * HEAD_DIM), lambda q: (q, 0, 0)),
        out_shape=jax.ShapeDtypeStruct((SEQS, 16, HEADS * HEAD_DIM), BF16),
        compiler_params=params(),
        name="unpack_outputs",
    )(received)


def per_device(x_heads, b_keys, c_queries, log_decay, level_log, skip_gain):
    near_axes = ("block", "tp")
    packed = pack(x_heads, b_keys, c_queries, log_decay, level_log)
    received = lax.all_to_all(packed, near_axes, 0, 0, tiled=True)
    gain = jnp.repeat(skip_gain, HEAD_DIM)[None, :]
    chunk = lax.axis_index("chunk")
    bits = jnp.stack([(chunk >> bit) & 1 for bit in range(3)]).astype(jnp.int32)
    own = chunk_state(received)
    inner, grow = inner_part(received, gain)
    messages = []
    for bit in range(3):
        pairs = [(source, source ^ (1 << bit)) for source in range(8)]
        partner = lax.ppermute(own, "chunk", pairs)
        messages.append(partner)
        if bit < 2:
            own = join(bits, own, partner, bit)
    mixed = outer_part(bits, received, inner, grow, messages)
    return unpack(lax.all_to_all(mixed, near_axes, 0, 0, tiled=True))


def solution(mesh):
    cut = Mesh(mesh.devices.reshape(8, 4, 16), ("chunk", "block", "tp"))
    split = P(None, ("chunk", "block", "tp"), None)
    return jax.shard_map(
        per_device,
        mesh=cut,
        in_specs=(split, split, split, split, split, P("tp")),
        out_specs=split,
        check_vma=False,
    )
```

time: 241 us -> 114 us (0.47)
  local copies, waits for them, and re-layouts: 58.2 us -> 4.8 us
  starting transfers between devices: 68.5 us -> 29.3 us
  other arithmetic: 24.5 us -> 0.08 us
  waiting for transfers between devices: 52.7 us -> 35.8 us
  Pallas kernels: 0 us -> 16.8 us
  matrix products: 9.57 us -> 0 us
    ppermute x9 -> x3, waiting for transfers between devices: 43.9 us -> 4.45 us  [per_device(): partner = lax.ppermute(own, 'chunk', pairs)]
    unnamed x67 -> x12, local copies, waits for them, and re-layouts: 38.3 us -> 4.64 us
    all_to_all x5 -> x1, waiting for transfers between devices: 8.8 us -> 31.3 us  [per_device(): received = lax.all_to_all(packed, near_axes, 0, 0, tiled=True)]
    all_to_all x5 -> x1, starting transfers between devices: 34.1 us -> 11.6 us  [per_device(): received = lax.all_to_all(packed, near_axes, 0, 0, tiled=True)]
    pallas_call x0 -> x7, Pallas kernels: none -> 16.8 us  [the longest x1 8.45 us: inner_part(): pl.pallas_call(inner_kernel, out_shape=(wide, wide), scratch_shapes=[pltp...]
    ppermute x9 -> x3, starting transfers between devices: 34.5 us -> 17.7 us  [per_device(): partner = lax.ppermute(own, 'chunk', pairs)]
    all_to_all x9 -> x0, local copies, waits for them, and re-layouts: 10.4 us -> none  [the longest x1 5.48 us: per_device(): lax.all_to_all(x_heads, 'tp', split_axis=2, concat_axis=1, tiled=True)]
    dot_general x4 -> x0, matrix products: 9.57 us -> none  [the longest x1 6.38 us: local_terms(): jnp.einsum('shtu,suhp->sthp', scores, x_vals, preferred_element_type=jnp....]
  transfers between devices with their start and end apart: 14 -> 4, of which waited for: 6 -> 3; matrix products, arithmetic and copies ran while one was open for 34% -> 0% of each run, Pallas kernels for 0% -> 7%
where the time goes in v1:
time: 114 us
  waiting for transfers between devices  35.8 us (31%)
  starting transfers between devices  29.3 us (26%)
  blocking collectives  26.6 us (23%)
  Pallas kernels  16.8 us (15%)
  local copies, waits for them, and re-layouts  4.8 us (4%)
    all_to_all x1, waiting for transfers between devices, per_device(): received = lax.all_to_all(packed, near_axes, 0, 0, tiled=True)  31.3 us
    all_to_all x1, blocking collectives, per_device(): return unpack(lax.all_to_all(mixed, near_axes, 0, 0, tiled=True))  26.6 us
    ppermute x3, starting transfers between devices, per_device(): partner = lax.ppermute(own, 'chunk', pairs)  17.7 us
    all_to_all x1, starting transfers between devices, per_device(): received = lax.all_to_all(packed, near_axes, 0, 0, tiled=True)  11.6 us
    pallas_call x1, Pallas kernels, inner_part(): pl.pallas_call(inner_kernel, out_shape=(wide, wide), scratch_shapes=[pltp...  8.45 us
    unnamed x12, local copies, waits for them, and re-layouts  4.64 us
    ppermute x3, waiting for transfers between devices, per_device(): partner = lax.ppermute(own, 'chunk', pairs)  4.45 us
    pallas_call x1, Pallas kernels, outer_part(): pl.pallas_call(outer_kernel, grid=(steps,), in_specs=[pl.BlockSpec(memory...  2.29 us
  transfers between devices with their start and end apart: 4, of which 3 were waited for; matrix products, arithmetic and copies ran while one was open for 0% of the time, Pallas kernels for 7%

profile of v1, /device:TPU:1, one launch (start us, length us, event | category | flops | bytes accessed | tf_op | source)
XLA Modules:
  0.0 113.5 jit_solution(5594830088518161566)
XLA Ops:
  0.0 0.0 copy-start
  0.0 1.0 copy-done
  1.0 0.0 copy-start.1
  1.0 0.9 copy-done.1
  2.0 0.0 copy-start.2
  2.0 0.9 copy-done.2
  2.9 0.0 copy-start.3
  2.9 0.9 copy-done.3
  3.9 0.0 copy-start.4
  3.9 0.8 copy-done.4
  4.6 2.2 %pack_messages.1 = bf16[64,72,128]{2,1,0:T(8,128)(2,1)} custom-call(bf16[4,16,4096]{2,1,0:T(8,128)(2,1)S(1)} %copy-done, bf16[4,16,2048]{2,1,0:T(8,128)(2,1)S(1)} %copy-done.1, bf16[4,16,2048]{2,1,0:T(8,128)(2,1)S(1)} %copy-done.2, f32[4,16,64]{2,1,0:T(8,128)S(1)} %copy-done.4, f32[4,16,896]{2,1,0:T(8,128)S(1)} %copy-done.3), custom_call_target="tpu_custom_call" | custom-call | tf_op jit(solution)/shard_map/pack_messages/pallas_call | solution.py:67
  6.8 11.6 %all-to-all-start = ((bf16[64,72,128]{2,1,0:T(8,128)(2,1)}), bf16[64,72,128]{2,1,0:T(8,128)(2,1)S(1)}, u32[]{:S(2)}, u32[]{:S(2)}) async-start(bf16[64,72,128]{2,1,0:T(8,128)(2,1)} %pack_messages.1), calls=%async_computation | async-start | bytes 2359296 | tf_op jit(solution)/shard_map/all_to_all | solution.py:340
  18.4 0.0 copy-start.5
  18.5 31.3 %all-to-all-done.ref = bf16[64,72,128]{2,1,0:T(8,128)(2,1)S(1)} async-done(((bf16[64,72,128]{2,1,0:T(8,128)(2,1)}), bf16[64,72,128]{2,1,0:T(8,128)(2,1)S(1)}, u32[]{:S(2)}, u32[]{:S(2)}) %all-to-all-start) | async-done | bytes 1179680 | tf_op jit(solution)/shard_map/all_to_all | solution.py:340
  49.8 1.4 %chunk_state.1.own_ref = bf16[144,256]{1,0:T(8,128)(2,1)S(1)} custom-call(bf16[64,72,128]{2,1,0:T(8,128)(2,1)S(1)} %all-to-all-done.ref), custom_call_target="tpu_custom_call" | custom-call | tf_op jit(solution)/shard_map/chunk_state/pallas_call | solution.py:161
  51.2 4.0 %collective-permute-start = (bf16[144,256]{1,0:T(8,128)(2,1)S(1)}, bf16[144,256]{1,0:T(8,128)(2,1)S(1)}, u32[]{:S(2)}, u32[]{:S(2)}) collective-permute-start(bf16[144,256]{1,0:T(8,128)(2,1)S(1)} %chunk_state.1.own_ref), channel_id=1, source_target_pairs={{0,64},{64,0},{128,192},{192,128},{256,320},{320,256},{384,448},{4... | collective-permute-start | bytes 221192 | tf_op jit(solution)/shard_map/ppermute | solution.py:349
  55.2 0.1 pad_add_fusion.bits_ref
  55.3 2.5 %collective-permute-done.partner_ref.m0_ref = bf16[144,256]{1,0:T(8,128)(2,1)S(1)} collective-permute-done((bf16[144,256]{1,0:T(8,128)(2,1)S(1)}, bf16[144,256]{1,0:T(8,128)(2,1)S(1)}, u32[]{:S(2)}, u32[]{:S(2)}) %collective-permute-start) | collective-permute-done | bytes 73760 | tf_op jit(solution)/shard_map/ppermute | solution.py:349
  57.8 0.6 join_states.2.own_ref
  58.4 5.8 %collective-permute-start.1 = (bf16[144,256]{1,0:T(8,128)(2,1)S(1)}, bf16[144,256]{1,0:T(8,128)(2,1)S(1)}, u32[]{:S(2)}, u32[]{:S(2)}) collective-permute-start(bf16[144,256]{1,0:T(8,128)(2,1)S(1)} %join_states.2.own_ref), channel_id=1, source_target_pairs={{0,128},{64,192},{128,0},{192,64},{256,384},{320,448},{384,256},{4... | collective-permute-start | bytes 221192 | tf_op jit(solution)/shard_map/ppermute | solution.py:349
  64.2 0.0 copy-done.5
  64.3 0.1 broadcast_in_dim.3
  64.3 0.1 broadcast_in_dim_reshape.3.gain_ref
  64.4 1.9 %collective-permute-done.1.partner_ref.m1_ref = bf16[144,256]{1,0:T(8,128)(2,1)S(1)} collective-permute-done((bf16[144,256]{1,0:T(8,128)(2,1)S(1)}, bf16[144,256]{1,0:T(8,128)(2,1)S(1)}, u32[]{:S(2)}, u32[]{:S(2)}) %collective-permute-start.1) | collective-permute-done | bytes 73760 | tf_op jit(solution)/shard_map/ppermute | solution.py:349
  66.3 0.6 join_states.3
  66.9 7.9 %collective-permute-start.2 = (bf16[144,256]{1,0:T(8,128)(2,1)S(1)}, bf16[144,256]{1,0:T(8,128)(2,1)S(1)}, u32[]{:S(2)}, u32[]{:S(2)}) collective-permute-start(bf16[144,256]{1,0:T(8,128)(2,1)S(1)} %join_states.3), channel_id=1, source_target_pairs={{0,256},{64,320},{128,384},{192,448},{256,0},{320,64},{384,128},{4... | collective-permute-start | bytes 221192 | tf_op jit(solution)/shard_map/ppermute | solution.py:349
  74.8 8.5 %inner_part.1 = (f32[1024,256]{1,0:T(8,128)S(1)}, f32[1024,256]{1,0:T(8,128)S(1)}) custom-call(bf16[64,72,128]{2,1,0:T(8,128)(2,1)S(1)} %all-to-all-done.ref, f32[1,256]{1,0:T(1,128)S(1)} %broadcast_in_dim_reshape.3.gain_ref), custom_call_target="tpu_custom_call" | custom-call | flops 1073741824 | bytes 4194304 | tf_op jit(solution)/shard_map/inner_part/pallas_call | solution.py:264
  83.3 0.0 collective-permute-done.2.m2_ref
  83.3 2.3 %outer_part.1 = bf16[64,16,256]{2,1,0:T(8,128)(2,1)S(1)} custom-call(s32[3]{0:T(128)S(1)} %pad_add_fusion.bits_ref, bf16[64,72,128]{2,1,0:T(8,128)(2,1)S(1)} %all-to-all-done.ref, f32[1024,256]{1,0:T(8,128)S(1)} %get-tuple-element.7.inner_ref, f32[1024,256]{1,0:T(8,128)S(1)} %get-tuple-element.8.grow_ref, ...), custom_call_target="tpu_custom_call" | custom-call | tf_op jit(solution)/shard_map/outer_part/pallas_call | solution.py:301
  85.6 26.6 %all_to_all.10.ref = bf16[64,16,256]{2,1,0:T(8,128)(2,1)S(1)} all-to-all(bf16[64,16,256]{2,1,0:T(8,128)(2,1)S(1)} %outer_part.1), channel_id=1, replica_groups=mesh['chunk'=8,'block'=4,'tp'=16] {'block','tp'}, dimensions={0} | all-to-all | bytes 1048576 | tf_op jit(solution)/shard_map/all_to_all | solution.py:354
  112.1 1.4 %unpack_outputs.1 = bf16[4,16,4096]{2,1,0:T(8,128)(2,1)} custom-call(bf16[64,16,256]{2,1,0:T(8,128)(2,1)S(1)} %all_to_all.10.ref), custom_call_target="tpu_custom_call" | custom-call | tf_op jit(solution)/shard_map/unpack_outputs/pallas_call | solution.py:326
Async XLA Ops:
  0.0 1.0 copy-start
  1.0 0.9 copy-start.1
  2.0 0.9 copy-start.2
  2.9 0.9 copy-start.3
  3.9 0.8 copy-start.4
  6.8 43.0 %all-to-all-start = ((bf16[64,72,128]{2,1,0:T(8,128)(2,1)}), bf16[64,72,128]{2,1,0:T(8,128)(2,1)S(1)}, u32[]{:S(2)}, u32[]{:S(2)}) async-start(bf16[64,72,128]{2,1,0:T(8,128)(2,1)} %pack_messages.1), calls=%async_computation | async-start | bytes 2359296 | tf_op jit(solution)/shard_map/all_to_all | solution.py:340
  18.4 45.8 %copy-start.5 = (f32[4]{0:T(128)S(1)}, f32[4]{0:T(128)}, u32[]{:S(2)}) copy-start(f32[4]{0:T(128)} %param.11) | copy-start | bytes 52
  51.2 6.6 %collective-permute-start = (bf16[144,256]{1,0:T(8,128)(2,1)S(1)}, bf16[144,256]{1,0:T(8,128)(2,1)S(1)}, u32[]{:S(2)}, u32[]{:S(2)}) collective-permute-start(bf16[144,256]{1,0:T(8,128)(2,1)S(1)} %chunk_state.1.own_ref), channel_id=1, source_target_pairs={{0,64},{64,0},{128,192},{192,128},{256,320},{320,256},{384,448},{4... | collective-permute-start | bytes 221192 | tf_op jit(solution)/shard_map/ppermute | solution.py:349
  58.4 7.9 %collective-permute-start.1 = (bf16[144,256]{1,0:T(8,128)(2,1)S(1)}, bf16[144,256]{1,0:T(8,128)(2,1)S(1)}, u32[]{:S(2)}, u32[]{:S(2)}) collective-permute-start(bf16[144,256]{1,0:T(8,128)(2,1)S(1)} %join_states.2.own_ref), channel_id=1, source_target_pairs={{0,128},{64,192},{128,0},{192,64},{256,384},{320,448},{384,256},{4... | collective-permute-start | bytes 221192 | tf_op jit(solution)/shard_map/ppermute | solution.py:349
  66.9 16.4 %collective-permute-start.2 = (bf16[144,256]{1,0:T(8,128)(2,1)S(1)}, bf16[144,256]{1,0:T(8,128)(2,1)S(1)}, u32[]{:S(2)}, u32[]{:S(2)}) collective-permute-start(bf16[144,256]{1,0:T(8,128)(2,1)S(1)} %join_states.3), channel_id=1, source_target_pairs={{0,256},{64,320},{128,384},{192,448},{256,0},{320,64},{384,128},{4... | collective-permute-start | bytes 221192 | tf_op jit(solution)/shard_map/ppermute | solution.py:349

commit v2 on v1

--- a/solution.py
+++ b/solution.py
@@ -1,5 +1,3 @@
-import functools
-
 import jax
 import jax.numpy as jnp
 from jax import lax
@@ -70,7 +68,6 @@
         in_specs=[spec(a) for a in (x, b, c, decay, level)],
         out_specs=pl.BlockSpec((GROUPS, ROWS, 128), lambda q: (q, 0, 0)),
         out_shape=jax.ShapeDtypeStruct((SEQS * GROUPS, ROWS, 128), BF16),
-        compiler_params=params(),
         name="pack_messages",
     )(x, b, c, decay, level)
 
@@ -167,8 +164,8 @@
     )(received)
 
 
-def join_kernel(bits_ref, own_ref, partner_ref, out_ref, *, bit):
-    upper = bits_ref[bit] == 1
+def join_kernel(place_ref, own_ref, partner_ref, near_ref, out_ref):
+    upper = place_ref[0] % 2 == 1
     own, own_total = message_state(own_ref), message_total(own_ref)
     partner, partner_total = message_state(partner_ref), message_total(partner_ref)
     late_total = jnp.where(upper, own_total, partner_total)
@@ -178,26 +175,25 @@
     out_ref[STATE : STATE + 16, :] = split_rows(own_total + partner_total)
 
 
-def join(bits, own, partner, bit):
-    return pl.pallas_call(
-        functools.partial(join_kernel, bit=bit),
+def join(place, own, partner, near):
+    return pl.pallas_call(
+        join_kernel,
         in_specs=[
             pl.BlockSpec(memory_space=pltpu.SMEM),
             pl.BlockSpec(memory_space=pltpu.VMEM),
             pl.BlockSpec(memory_space=pltpu.VMEM),
+            pl.BlockSpec(memory_space=pl.ANY),
         ],
         out_shape=jax.ShapeDtypeStruct(own.shape, BF16),
         compiler_params=params(),
         name="join_states",
-    )(bits, own, partner)
-
-
-def inner_kernel(ref, gain_ref, out_ref, grow_ref, gate_ref, cum_ref, state_ref, first_ref):
+    )(place, own, partner, near)
+
+
+def near_kernel(ref, gain_ref, own_ref, out_ref, gate_ref, cum_ref):
     unpack_gates(ref, gate_ref)
     chunk_cumsum(gate_ref, cum_ref)
-    subs = CHUNK // SUB
     gain = gain_ref[...]
-
     row = lax.broadcasted_iota(jnp.int32, (SUB, WIDTH), 0)
     col = lax.broadcasted_iota(jnp.int32, (SUB, WIDTH), 1) % SUB
     differ = jnp.bitwise_xor(row, col)
@@ -208,18 +204,14 @@
     same_head = head_row == head_col
     spreads = [spread(level, LEVELS) for level in range(7)]
 
-    def one_sub(i, before):
+    @pl.loop(0, CHUNK // SUB)
+    def _(i):
         first = i * SUB
         cum = cum_ref[pl.ds(first, SUB), :]
-        last = cum[SUB - 1 :, :]
         x = load_x(ref, first, SUB)
         b = load_b(ref, first, SUB)
         c = load_c(ref, first, SUB)
         gates = load_gates(gate_ref, first, SUB)
-        wide_x = x.astype(F32)
-        state_ref[i] = dot_t(b, (wide_x * jnp.exp(last - cum)).astype(BF16))
-        grow_ref[pl.ds(first, SUB), :] = jnp.exp(cum - before)
-        first_ref[pl.ds(i, 1), :] = before
         raw = dot_nt(c, jnp.concatenate([b] * PER_GROUP, axis=0))
         cum_row = jnp.sum(jnp.where(diagonal, cum, 0.0), axis=0, keepdims=True)
         picked = dot(gates, spreads[6])
@@ -230,12 +222,42 @@
         scores = jnp.where(causal, raw * decay * picked, 0.0).astype(BF16)
         tall_x = jnp.concatenate([x] * PER_GROUP, axis=0)
         block_x = jnp.where(same_head, tall_x, jnp.zeros_like(tall_x))
-        out_ref[pl.ds(first, SUB), :] = dot(scores, block_x) + gain * wide_x
-        return last
-
-    final = lax.fori_loop(0, subs, one_sub, jnp.zeros((1, WIDTH), F32))
-
-    starts = [first_ref[i : i + 1, :] for i in range(subs)] + [final]
+        out_ref[pl.ds(first, SUB), :] = dot(scores, block_x) + gain * x.astype(F32)
+
+
+def near_part(received, gain, own):
+    return pl.pallas_call(
+        near_kernel,
+        in_specs=[
+            pl.BlockSpec(memory_space=pltpu.VMEM),
+            pl.BlockSpec(memory_space=pltpu.VMEM),
+            pl.BlockSpec(memory_space=pl.ANY),
+        ],
+        out_shape=jax.ShapeDtypeStruct((CHUNK, WIDTH), F32),
+        scratch_shapes=[pltpu.VMEM((64, 16, 64), F32), pltpu.VMEM((CHUNK, WIDTH), F32)],
+        compiler_params=params(),
+        cost_estimate=pl.CostEstimate(
+            flops=4 * 10**9, bytes_accessed=4 * 1024 * 1024, transcendentals=10**6
+        ),
+        name="near_part",
+    )(received, gain, own)
+
+
+def levels_kernel(ref, near_ref, own_ref, out_ref, grow_ref, gate_ref, cum_ref, state_ref):
+    unpack_gates(ref, gate_ref)
+    final = chunk_cumsum(gate_ref, cum_ref)
+    subs = CHUNK // SUB
+    starts = [jnp.zeros((1, WIDTH), F32)]
+    starts += [cum_ref[i * SUB - 1 : i * SUB, :] for i in range(1, subs)] + [final]
+    for i in range(subs):
+        rows = slice(i * SUB, (i + 1) * SUB)
+        x = load_x(ref, i * SUB, SUB).astype(F32)
+        cum = cum_ref[rows, :]
+        tail = jnp.exp(starts[i + 1] - cum)
+        state_ref[i] = dot_t(load_b(ref, i * SUB, SUB), (x * tail).astype(BF16))
+        grow_ref[rows, :] = jnp.exp(cum - starts[i])
+        out_ref[rows, :] = near_ref[rows, :]
+
     states = [state_ref[i] for i in range(subs)]
     size = 1
     for bit in range(4):
@@ -259,42 +281,59 @@
         grow_ref[rows, :] = grow_ref[rows, :] * jnp.exp(starts[i])
 
 
-def inner_part(received, gain):
+def levels_part(received, near, own):
     wide = jax.ShapeDtypeStruct((CHUNK, WIDTH), F32)
     return pl.pallas_call(
-        inner_kernel,
+        levels_kernel,
+        in_specs=[
+            pl.BlockSpec(memory_space=pltpu.VMEM),
+            pl.BlockSpec(memory_space=pltpu.VMEM),
+            pl.BlockSpec(memory_space=pl.ANY),
+        ],
         out_shape=(wide, wide),
         scratch_shapes=[
             pltpu.VMEM((64, 16, 64), F32),
             pltpu.VMEM((CHUNK, WIDTH), F32),
             pltpu.VMEM((CHUNK // SUB, STATE, WIDTH), F32),
-            pltpu.VMEM((CHUNK // SUB, WIDTH), F32),
         ],
         compiler_params=params(),
         cost_estimate=pl.CostEstimate(
-            flops=2 * CHUNK * WIDTH * 2048, bytes_accessed=4 * 1024 * 1024, transcendentals=10**6
+            flops=4 * 10**9, bytes_accessed=4 * 1024 * 1024, transcendentals=10**6
         ),
-        name="inner_part",
-    )(received, gain)
-
-
-def outer_kernel(bits_ref, ref, inner_ref, grow_ref, m0_ref, m1_ref, m2_ref, out_ref):
+        name="levels_part",
+    )(received, near, own)
+
+
+def outer_kernel(
+    place_ref, ref, inner_ref, grow_ref, pair_ref, one_ref, two_ref, three_ref, out_ref, level_ref
+):
+    @pl.when(pl.program_id(0) == 0)
+    def _():
+        place = place_ref[0]
+        in_half, odd, high = place % 2 == 1, place // 2 % 2 == 1, place // 4 == 1
+        level_ref[0] = jnp.where(in_half, pair_ref[0:STATE, :].astype(F32), 0.0).astype(BF16)
+        prefix = jnp.where(in_half, message_total(pair_ref), 0.0)
+        near_state, near_total = message_state(one_ref), message_total(one_ref)
+        level_ref[1] = jnp.where(odd, jnp.exp(prefix) * near_state, 0.0).astype(BF16)
+        prefix = prefix + jnp.where(odd, near_total, 0.0)
+        late = jnp.where(odd, message_state(two_ref), near_state)
+        late_total = jnp.where(odd, message_total(two_ref), near_total)
+        early = jnp.where(odd, message_state(three_ref), message_state(two_ref))
+        joined = jnp.exp(late_total) * early + late
+        level_ref[2] = jnp.where(high, jnp.exp(prefix) * joined, 0.0).astype(BF16)
+
     both = ref[:, 64:72, :].astype(F32)
     gates = jnp.concatenate([both[:, :, 0:64], both[:, :, 64:128]], axis=1)
     gates = gates.reshape(BLOCK, 64).astype(BF16)
     c = load_rows(ref, 0, BLOCK, 48, 64)
-    prefix = jnp.zeros((1, WIDTH), F32)
     total = jnp.zeros((BLOCK, WIDTH), F32)
-    for bit, message in enumerate((m0_ref, m1_ref, m2_ref)):
-        upper = bits_ref[bit] == 1
-        level_state = jnp.where(upper, jnp.exp(prefix) * message_state(message), 0.0).astype(BF16)
-        prefix = prefix + jnp.where(upper, message_total(message), 0.0)
-        total += dot(gates, spread(11 + bit, LEVELS)) * dot(c, level_state)
+    for bit in range(3):
+        total += dot(gates, spread(11 + bit, LEVELS)) * dot(c, level_ref[bit])
     mixed = inner_ref[...] + grow_ref[...] * total
     out_ref[...] = mixed.astype(BF16).reshape(BLOCK // 16, 16, WIDTH)
 
 
-def outer_part(bits, received, inner, grow, messages):
+def outer_part(place, received, inner, grow, messages):
     steps = CHUNK // BLOCK
     wide = pl.BlockSpec((BLOCK, WIDTH), lambda k: (k, 0))
     state = pl.BlockSpec((STATE + 16, WIDTH), lambda k: (0, 0))
@@ -309,12 +348,14 @@
             state,
             state,
             state,
+            state,
         ],
         out_specs=pl.BlockSpec((64 // steps, 16, WIDTH), lambda k: (k, 0, 0)),
         out_shape=jax.ShapeDtypeStruct((64, 16, WIDTH), BF16),
+        scratch_shapes=[pltpu.VMEM((3, STATE, WIDTH), BF16)],
         compiler_params=params(),
         name="outer_part",
-    )(bits, received, inner, grow, *messages)
+    )(place, received, inner, grow, *messages)
 
 
 def unpack_kernel(ref, out_ref):
@@ -339,18 +380,17 @@
     packed = pack(x_heads, b_keys, c_queries, log_decay, level_log)
     received = lax.all_to_all(packed, near_axes, 0, 0, tiled=True)
     gain = jnp.repeat(skip_gain, HEAD_DIM)[None, :]
-    chunk = lax.axis_index("chunk")
-    bits = jnp.stack([(chunk >> bit) & 1 for bit in range(3)]).astype(jnp.int32)
+    place = lax.axis_index("chunk").astype(jnp.int32)[None]
     own = chunk_state(received)
-    inner, grow = inner_part(received, gain)
-    messages = []
-    for bit in range(3):
-        pairs = [(source, source ^ (1 << bit)) for source in range(8)]
-        partner = lax.ppermute(own, "chunk", pairs)
-        messages.append(partner)
-        if bit < 2:
-            own = join(bits, own, partner, bit)
-    mixed = outer_part(bits, received, inner, grow, messages)
+    pair = lax.ppermute(own, "chunk", [(source, source ^ 1) for source in range(8)])
+    near = near_part(received, gain, own)
+    own = join(place, own, pair, near)
+    shifted = [
+        lax.ppermute(own, "chunk", [(source, source + 2 * z) for source in range(8 - 2 * z)])
+        for z in (1, 2, 3)
+    ]
+    inner, grow = levels_part(received, near, own)
+    mixed = outer_part(place, received, inner, grow, [pair] + shifted)
     return unpack(lax.all_to_all(mixed, near_axes, 0, 0, tiled=True))
 
 

time: 114 us -> 106 us (0.930)
  local copies, waits for them, and re-layouts: 4.8 us -> 0.16 us
  blocking collectives: 26.6 us -> 23.4 us
  waiting for transfers between devices: 35.8 us -> 33.6 us
  starting transfers between devices: 29.3 us -> 30.8 us
    unnamed x12 -> x2, local copies, waits for them, and re-layouts: 4.64 us -> 0.01 us
    all_to_all x1, blocking collectives: 26.6 us -> 23.4 us  [per_device(): return unpack(lax.all_to_all(mixed, near_axes, 0, 0, tiled=True))]
    ppermute x3 -> x4, waiting for transfers between devices: 4.45 us -> 2.37 us  [the longest x3 2.37 us: per_device(): lax.ppermute(own, 'chunk', [(source, source + 2 * z) for source in range(...]
    pallas_call x1, Pallas kernels: 2.16 us -> 3.87 us  [pack(): pl.pallas_call(pack_kernel, grid=(SEQS,), in_specs=[spec(a) for a in (x,...]
    ppermute x3 -> x4, starting transfers between devices: 17.7 us -> 19 us  [the longest x3 15 us: per_device(): lax.ppermute(own, 'chunk', [(source, source + 2 * z) for source in range(...]
  transfers between devices with their start and end apart: 4 -> 5, of which waited for: 3 -> 2; matrix products, arithmetic and copies ran while one was open for 0% -> 0% of each run, Pallas kernels for 7% -> 8%
where the time goes in v2:
time: 106 us; the launch traced here: 105 us
  waiting for transfers between devices  33.6 us (32%)
  starting transfers between devices  30.8 us (29%)
  blocking collectives  23.4 us (22%)
  Pallas kernels  17.2 us (16%)
    all_to_all x1, waiting for transfers between devices, per_device(): received = lax.all_to_all(packed, near_axes, 0, 0, tiled=True)  31.2 us
    all_to_all x1, blocking collectives, per_device(): return unpack(lax.all_to_all(mixed, near_axes, 0, 0, tiled=True))  23.4 us
    ppermute x3, starting transfers between devices, per_device(): lax.ppermute(own, 'chunk', [(source, source + 2 * z) for source in range(...  15 us
    all_to_all x1, starting transfers between devices, per_device(): received = lax.all_to_all(packed, near_axes, 0, 0, tiled=True)  11.8 us
    pallas_call x1, Pallas kernels, near_part(): pl.pallas_call(near_kernel, in_specs=[pl.BlockSpec(memory_space=pltpu.VME...  6.77 us
    ppermute x1, starting transfers between devices, per_device(): lax.ppermute(own, 'chunk', [(source, source ^ 1) for source in range(8)])  4 us
    pallas_call x1, Pallas kernels, pack(): pl.pallas_call(pack_kernel, grid=(SEQS,), in_specs=[spec(a) for a in (x,...  3.87 us
    ppermute x3, waiting for transfers between devices, per_device(): lax.ppermute(own, 'chunk', [(source, source + 2 * z) for source in range(...  2.37 us
  transfers between devices with their start and end apart: 5, of which 2 were waited for; matrix products, arithmetic and copies ran while one was open for 0% of the time, Pallas kernels for 8%

profile of v2, /device:TPU:1, one launch (start us, length us, event | category | flops | bytes accessed | tf_op | source)
XLA Modules:
  0.0 105.2 jit_solution(5755669112447147542)
XLA Ops:
  0.0 3.9 %pack_messages.1 = bf16[64,72,128]{2,1,0:T(8,128)(2,1)} custom-call(bf16[4,16,4096]{2,1,0:T(8,128)(2,1)} %x_ref.1, bf16[4,16,2048]{2,1,0:T(8,128)(2,1)} %b_ref.1, bf16[4,16,2048]{2,1,0:T(8,128)(2,1)} %c_ref.1, f32[4,16,64]{2,1,0:T(8,128)} %decay_ref.1, f32[4,16,896]{2,1,0:T(8,128)} %level_ref.1), custom_call_target="tpu_custom_call" | custom-call | tf_op jit(solution)/shard_map/pack_messages/pallas_call | solution.py:65
  3.9 0.0 copy-start
  3.9 11.8 %all-to-all-start = ((bf16[64,72,128]{2,1,0:T(8,128)(2,1)}), bf16[64,72,128]{2,1,0:T(8,128)(2,1)S(1)}, u32[]{:S(2)}, u32[]{:S(2)}) async-start(bf16[64,72,128]{2,1,0:T(8,128)(2,1)} %pack_messages.1), calls=%async_computation | async-start | bytes 2359296 | tf_op jit(solution)/shard_map/all_to_all | solution.py:381
  15.6 0.0 copy-done
  15.7 0.1 broadcast_in_dim.7
  15.7 0.1 broadcast_in_dim_reshape.3.gain_ref
  15.8 31.2 %all-to-all-done.ref = bf16[64,72,128]{2,1,0:T(8,128)(2,1)S(1)} async-done(((bf16[64,72,128]{2,1,0:T(8,128)(2,1)}), bf16[64,72,128]{2,1,0:T(8,128)(2,1)S(1)}, u32[]{:S(2)}, u32[]{:S(2)}) %all-to-all-start) | async-done | bytes 1179680 | tf_op jit(solution)/shard_map/all_to_all | solution.py:381
  47.0 1.4 %chunk_state.1.own_ref = bf16[144,256]{1,0:T(8,128)(2,1)S(1)} custom-call(bf16[64,72,128]{2,1,0:T(8,128)(2,1)S(1)} %all-to-all-done.ref), custom_call_target="tpu_custom_call" | custom-call | tf_op jit(solution)/shard_map/chunk_state/pallas_call | solution.py:158
  48.4 4.0 %collective-permute-start = (bf16[144,256]{1,0:T(8,128)(2,1)S(1)}, bf16[144,256]{1,0:T(8,128)(2,1)S(1)}, u32[]{:S(2)}, u32[]{:S(2)}) collective-permute-start(bf16[144,256]{1,0:T(8,128)(2,1)S(1)} %chunk_state.1.own_ref), channel_id=1, source_target_pairs={{0,64},{64,0},{128,192},{192,128},{256,320},{320,256},{384,448},{4... | collective-permute-start | bytes 221192 | tf_op jit(solution)/shard_map/ppermute | solution.py:385
  52.4 6.8 %near_part.1.near_ref = f32[1024,256]{1,0:T(8,128)S(1)} custom-call(bf16[64,72,128]{2,1,0:T(8,128)(2,1)S(1)} %all-to-all-done.ref, f32[1,256]{1,0:T(1,128)S(1)} %broadcast_in_dim_reshape.3.gain_ref, bf16[144,256]{1,0:T(8,128)(2,1)S(1)} %chunk_state.1.own_ref), custom_call_target="tpu_custom_call" | custom-call | flops 4000000000 | bytes 4194304 | tf_op jit(solution)/shard_map/near_part/pallas_call | solution.py:229
  59.2 0.0 collective-permute-done.partner_ref.pair_ref
  59.3 5.8 %collective-permute-start.1 = (bf16[144,256]{1,0:T(8,128)(2,1)S(1)}, bf16[144,256]{1,0:T(8,128)(2,1)S(1)}, u32[]{:S(2)}, u32[]{:S(2)}) collective-permute-start(bf16[144,256]{1,0:T(8,128)(2,1)S(1)} %join_states.1.own_ref), channel_id=1, source_target_pairs={{0,128},{64,192},{128,256},{192,320},{256,384},{320,448},{1,129},{... | collective-permute-start | bytes 221192 | tf_op jit(solution)/shard_map/ppermute | solution.py:389
  65.1 7.9 %collective-permute-start.2 = (bf16[144,256]{1,0:T(8,128)(2,1)S(1)}, bf16[144,256]{1,0:T(8,128)(2,1)S(1)}, u32[]{:S(2)}, u32[]{:S(2)}) collective-permute-start(bf16[144,256]{1,0:T(8,128)(2,1)S(1)} %join_states.1.own_ref), channel_id=1, source_target_pairs={{0,256},{64,320},{128,384},{192,448},{1,257},{65,321},{129,385},{1... | collective-permute-start | bytes 221192 | tf_op jit(solution)/shard_map/ppermute | solution.py:389
  73.0 1.3 %collective-permute-start.3 = (bf16[144,256]{1,0:T(8,128)(2,1)S(1)}, bf16[144,256]{1,0:T(8,128)(2,1)S(1)}, u32[]{:S(2)}, u32[]{:S(2)}) collective-permute-start(bf16[144,256]{1,0:T(8,128)(2,1)S(1)} %join_states.1.own_ref), channel_id=1, source_target_pairs={{0,384},{64,448},{1,385},{65,449},{2,386},{66,450},{3,387},{67,451... | collective-permute-start | bytes 221192 | tf_op jit(solution)/shard_map/ppermute | solution.py:389
  74.3 2.0 %levels_part.1 = (f32[1024,256]{1,0:T(8,128)S(1)}, f32[1024,256]{1,0:T(8,128)S(1)}) custom-call(bf16[64,72,128]{2,1,0:T(8,128)(2,1)S(1)} %all-to-all-done.ref, f32[1024,256]{1,0:T(8,128)S(1)} %near_part.1.near_ref, bf16[144,256]{1,0:T(8,128)(2,1)S(1)} %join_states.1.own_ref), custom_call_target="tpu_custom_call" | custom-call | flops 4000000000 | bytes 4194304 | tf_op jit(solution)/shard_map/levels_part/pallas_call | solution.py:286
  76.3 0.0 collective-permute-done.1.one_ref
  76.3 0.0 collective-permute-done.2.two_ref
  76.3 2.4 %collective-permute-done.3.three_ref = bf16[144,256]{1,0:T(8,128)(2,1)S(1)} collective-permute-done((bf16[144,256]{1,0:T(8,128)(2,1)S(1)}, bf16[144,256]{1,0:T(8,128)(2,1)S(1)}, u32[]{:S(2)}, u32[]{:S(2)}) %collective-permute-start.3) | collective-permute-done | bytes 73760 | tf_op jit(solution)/shard_map/ppermute | solution.py:389
  78.7 1.8 %outer_part.1 = bf16[64,16,256]{2,1,0:T(8,128)(2,1)S(1)} custom-call(s32[1]{0:T(128)} %bitcast.place_ref, bf16[64,72,128]{2,1,0:T(8,128)(2,1)S(1)} %all-to-all-done.ref, f32[1024,256]{1,0:T(8,128)S(1)} %get-tuple-element.7.inner_ref, f32[1024,256]{1,0:T(8,128)S(1)} %get-tuple-element.8.grow_ref, ...), custom_call_target="tpu_custom_call" | custom-call | tf_op jit(solution)/shard_map/outer_part/pallas_call | solution.py:340
  80.5 23.4 %all_to_all.10.ref = bf16[64,16,256]{2,1,0:T(8,128)(2,1)S(1)} all-to-all(bf16[64,16,256]{2,1,0:T(8,128)(2,1)S(1)} %outer_part.1), channel_id=1, replica_groups=mesh['chunk'=8,'block'=4,'tp'=16] {'block','tp'}, dimensions={0} | all-to-all | bytes 1048576 | tf_op jit(solution)/shard_map/all_to_all | solution.py:394
  103.9 1.4 %unpack_outputs.1 = bf16[4,16,4096]{2,1,0:T(8,128)(2,1)} custom-call(bf16[64,16,256]{2,1,0:T(8,128)(2,1)S(1)} %all_to_all.10.ref), custom_call_target="tpu_custom_call" | custom-call | tf_op jit(solution)/shard_map/unpack_outputs/pallas_call | solution.py:367
  (1 shorter events, 0.0 us)
Async XLA Ops:
  3.9 11.8 %copy-start = (f32[4]{0:T(128)S(1)}, f32[4]{0:T(128)}, u32[]{:S(2)}) copy-start(f32[4]{0:T(128)} %param.11) | copy-start | bytes 52
  3.9 43.1 %all-to-all-start = ((bf16[64,72,128]{2,1,0:T(8,128)(2,1)}), bf16[64,72,128]{2,1,0:T(8,128)(2,1)S(1)}, u32[]{:S(2)}, u32[]{:S(2)}) async-start(bf16[64,72,128]{2,1,0:T(8,128)(2,1)} %pack_messages.1), calls=%async_computation | async-start | bytes 2359296 | tf_op jit(solution)/shard_map/all_to_all | solution.py:381
  48.4 10.8 %collective-permute-start = (bf16[144,256]{1,0:T(8,128)(2,1)S(1)}, bf16[144,256]{1,0:T(8,128)(2,1)S(1)}, u32[]{:S(2)}, u32[]{:S(2)}) collective-permute-start(bf16[144,256]{1,0:T(8,128)(2,1)S(1)} %chunk_state.1.own_ref), channel_id=1, source_target_pairs={{0,64},{64,0},{128,192},{192,128},{256,320},{320,256},{384,448},{4... | collective-permute-start | bytes 221192 | tf_op jit(solution)/shard_map/ppermute | solution.py:385
  59.3 17.0 %collective-permute-start.1 = (bf16[144,256]{1,0:T(8,128)(2,1)S(1)}, bf16[144,256]{1,0:T(8,128)(2,1)S(1)}, u32[]{:S(2)}, u32[]{:S(2)}) collective-permute-start(bf16[144,256]{1,0:T(8,128)(2,1)S(1)} %join_states.1.own_ref), channel_id=1, source_target_pairs={{0,128},{64,192},{128,256},{192,320},{256,384},{320,448},{1,129},{... | collective-permute-start | bytes 221192 | tf_op jit(solution)/shard_map/ppermute | solution.py:389
  65.1 11.2 %collective-permute-start.2 = (bf16[144,256]{1,0:T(8,128)(2,1)S(1)}, bf16[144,256]{1,0:T(8,128)(2,1)S(1)}, u32[]{:S(2)}, u32[]{:S(2)}) collective-permute-start(bf16[144,256]{1,0:T(8,128)(2,1)S(1)} %join_states.1.own_ref), channel_id=1, source_target_pairs={{0,256},{64,320},{128,384},{192,448},{1,257},{65,321},{129,385},{1... | collective-permute-start | bytes 221192 | tf_op jit(solution)/shard_map/ppermute | solution.py:389
  73.0 5.7 %collective-permute-start.3 = (bf16[144,256]{1,0:T(8,128)(2,1)S(1)}, bf16[144,256]{1,0:T(8,128)(2,1)S(1)}, u32[]{:S(2)}, u32[]{:S(2)}) collective-permute-start(bf16[144,256]{1,0:T(8,128)(2,1)S(1)} %join_states.1.own_ref), channel_id=1, source_target_pairs={{0,384},{64,448},{1,385},{65,449},{2,386},{66,450},{3,387},{67,451... | collective-permute-start | bytes 221192 | tf_op jit(solution)/shard_map/ppermute | solution.py:389

commit v3 on v2

v3 whole, which is shorter than its diff:
```python
import jax
import jax.numpy as jnp
from jax import lax
from jax.experimental import pallas as pl
from jax.experimental.pallas import tpu as pltpu
from jax.sharding import Mesh
from jax.sharding import PartitionSpec as P

SEQS = 4
HEADS = 64
HEAD_DIM = 64
STATE = 128
GROUPS = 16
PER_GROUP = 4
LEVELS = 14
NEAR_LEVELS = 9
CHUNK = 1024
BLOCK = 256
SUB = 64
ROWS = 72
WIDTH = PER_GROUP * HEAD_DIM
GATES = PER_GROUP * LEVELS
CODE = 64.0
F32 = jnp.float32
BF16 = jnp.bfloat16
VMEM_LIMIT = 48 * 1024 * 1024


def dot(a, b):
    return jnp.dot(a, b, preferred_element_type=F32)


def dot_t(a, b):
    return lax.dot_general(a, b, (((0,), (0,)), ((), ())), preferred_element_type=F32)


def dot_nt(a, b):
    return lax.dot_general(a, b, (((1,), (1,)), ((), ())), preferred_element_type=F32)


def params():
    return pltpu.CompilerParams(vmem_limit_bytes=VMEM_LIMIT)


def sequence_at(block, place):
    return jnp.bitwise_xor(block, 2 * (place % 2))


def pack_kernel(place_ref, *refs):
    sources, out_ref = refs[:5], refs[5]
    x_ref, b_ref, c_ref, decay_ref, level_ref = held = refs[6:11]
    packed_ref, sems, out_sems = refs[11:]
    copies = [
        [
            pltpu.make_async_copy(
                source.at[sequence_at(k, place_ref[0])], slot.at[k], sems.at[i, k]
            )
            for i, (source, slot) in enumerate(zip(sources, held))
        ]
        for k in range(SEQS)
    ]
    for group in copies:
        for copy in group:
            copy.start()
    sends = []
    for k, group in enumerate(copies):
        for copy in group:
            copy.wait()
        gates = jnp.exp(CODE * level_ref[k])
        decay = decay_ref[k]
        high = decay.astype(BF16).astype(F32)
        low = decay - high
        for g in range(GROUPS):
            at = k * GROUPS + g
            packed_ref[at, 0:16, :] = x_ref[k, :, g * WIDTH : g * WIDTH + 128]
            packed_ref[at, 16:32, :] = x_ref[k, :, g * WIDTH + 128 : (g + 1) * WIDTH]
            packed_ref[at, 32:48, :] = b_ref[k, :, g * STATE : (g + 1) * STATE]
            packed_ref[at, 48:64, :] = c_ref[k, :, g * STATE : (g + 1) * STATE]
            heads = slice(g * PER_GROUP, (g + 1) * PER_GROUP)
            piece = jnp.concatenate(
                [gates[:, g * GATES : (g + 1) * GATES], high[:, heads], low[:, heads]], axis=1
            )
            packed_ref[at, 64:72, :] = jnp.concatenate([piece[0:8], piece[8:16]], axis=1).astype(BF16)
        part = pl.ds(k * GROUPS, GROUPS)
        sends.append(
            pltpu.make_async_copy(packed_ref.at[part], out_ref.at[part], out_sems.at[k])
        )
        sends[-1].start()
    for copy in sends:
        copy.wait()


def pack(place, *arrays):
    shape = (SEQS * GROUPS, ROWS, 128)
    return pl.pallas_call(
        pack_kernel,
        in_specs=[pl.BlockSpec(memory_space=pltpu.SMEM)]
        + [pl.BlockSpec(memory_space=pltpu.HBM)] * len(arrays),
        out_specs=pl.BlockSpec(memory_space=pltpu.HBM),
        out_shape=jax.ShapeDtypeStruct(shape, BF16),
        scratch_shapes=[pltpu.VMEM(a.shape, a.dtype) for a in arrays]
        + [
            pltpu.VMEM(shape, BF16),
            pltpu.SemaphoreType.DMA((len(arrays), SEQS)),
            pltpu.SemaphoreType.DMA((SEQS,)),
        ],
        name="pack_messages",
    )(place, *arrays)


def load_rows(ref, first, count, start, stop):
    part = ref[pl.ds(first // 16, count // 16), start:stop, :]
    return part.reshape(count, 128)


def load_x(ref, first, count):
    return jnp.concatenate(
        [load_rows(ref, first, count, 0, 16), load_rows(ref, first, count, 16, 32)], axis=1
    )


def load_b(ref, first, count):
    return load_rows(ref, first, count, 32, 48)


def load_c(ref, first, count):
    return load_rows(ref, first, count, 48, 64)


def halves_wide(value):
    high = value.astype(BF16)
    return high, value - high.astype(F32)


def halves(value):
    high = value.astype(BF16)
    return high, (value - high.astype(F32)).astype(BF16)


def spread(rows, offset, stride):
    row = lax.broadcasted_iota(jnp.int32, (rows, WIDTH), 0) % 64
    head = lax.broadcasted_iota(jnp.int32, (rows, WIDTH), 1) // HEAD_DIM
    return jnp.where(row == offset + stride * head, 1.0, 0.0).astype(BF16)


def chunk_cumsum(ref, wide_ref, cum_ref):
    both = ref[:, 64:72, :].astype(F32)
    wide_ref[:, 0:8, :] = both[:, :, 0:64]
    wide_ref[:, 8:16, :] = both[:, :, 64:128]
    row = lax.broadcasted_iota(jnp.int32, (BLOCK, BLOCK), 0)
    col = lax.broadcasted_iota(jnp.int32, (BLOCK, BLOCK), 1)
    lower = jnp.where(row >= col, 1.0, 0.0).astype(BF16)
    lane = lax.broadcasted_iota(jnp.int32, (64, WIDTH), 0)
    head = lax.broadcasted_iota(jnp.int32, (64, WIDTH), 1) // HEAD_DIM
    wanted = (lane >= GATES) & (lane % PER_GROUP == head)
    widen = jnp.where(wanted, 1.0, 0.0).astype(BF16)
    widen = jnp.concatenate([widen] * 3, axis=0)
    offset = jnp.zeros((1, WIDTH), F32)
    for k in range(CHUNK // BLOCK):
        values = wide_ref[k * 16 : (k + 1) * 16].reshape(BLOCK, 64).astype(BF16)
        sums = dot(lower, values)
        high, rest = halves_wide(sums)
        middle, rest = halves_wide(rest)
        parts = jnp.concatenate([high, middle, rest.astype(BF16)], axis=1)
        cum = dot(parts, widen) + offset
        cum_ref[k * BLOCK : (k + 1) * BLOCK, :] = cum
        offset = cum[BLOCK - 1 :, :]
    return offset


def decode_gates(ref, wide_ref, gate_ref):
    both = ref[:, 64:72, :].astype(F32)
    lane = lax.broadcasted_iota(jnp.int32, both.shape, 2) % 64
    gates = jnp.exp(jnp.log(jnp.where(lane < GATES, both, 1.0)) * (1.0 / CODE))
    wide_ref[:, 0:8, :] = gates[:, :, 0:64]
    wide_ref[:, 8:16, :] = gates[:, :, 64:128]
    high, low = halves(wide_ref[...].reshape(CHUNK, 64))
    gate_ref[...] = jnp.concatenate([high, low], axis=1)


def split_rows(total):
    high = total.astype(BF16).astype(F32)
    middle = (total - high).astype(BF16).astype(F32)
    low = total - high - middle
    row = lax.broadcasted_iota(jnp.int32, (16, WIDTH), 0)
    rows = jnp.where(row == 0, high, jnp.where(row == 1, middle, jnp.where(row == 2, low, 0.0)))
    return rows.astype(BF16)


def message_state(ref):
    return ref[0:STATE, :].astype(F32)


def message_total(ref):
    rows = ref[STATE : STATE + 16, :].astype(F32)
    return rows[0:1] + rows[1:2] + rows[2:3]


def state_kernel(ref, out_ref, cum_ref, wide_ref):
    total = chunk_cumsum(ref, wide_ref, cum_ref)
    state = jnp.zeros((STATE, WIDTH), F32)
    for k in range(CHUNK // BLOCK):
        tail = jnp.exp(total - cum_ref[k * BLOCK : (k + 1) * BLOCK, :])
        high, low = halves(load_x(ref, k * BLOCK, BLOCK).astype(F32) * tail)
        b = load_b(ref, k * BLOCK, BLOCK)
        both = dot_t(b, jnp.concatenate([high, low], axis=1))
        state += both[:, :WIDTH] + both[:, WIDTH:]
    out_ref[0:STATE, :] = state.astype(BF16)
    out_ref[STATE : STATE + 16, :] = split_rows(total)


def chunk_state(received):
    return pl.pallas_call(
        state_kernel,
        out_shape=(
            jax.ShapeDtypeStruct((STATE + 16, WIDTH), BF16),
            jax.ShapeDtypeStruct((CHUNK, WIDTH), F32),
        ),
        scratch_shapes=[pltpu.VMEM((64, 16, 64), F32)],
        compiler_params=params(),
        name="chunk_state",
    )(received)


def join_kernel(place_ref, own_ref, partner_ref, near_ref, out_ref):
    upper = place_ref[0] % 2 == 1
    own, own_total = message_state(own_ref), message_total(own_ref)
    partner, partner_total = message_state(partner_ref), message_total(partner_ref)
    late_total = jnp.where(upper, own_total, partner_total)
    early = jnp.where(upper, partner, own)
    late = jnp.where(upper, own, partner)
    out_ref[0:STATE, :] = (jnp.exp(late_total) * early + late).astype(BF16)
    out_ref[STATE : STATE + 16, :] = split_rows(own_total + partner_total)


def join(place, own, partner, near):
    return pl.pallas_call(
        join_kernel,
        in_specs=[
            pl.BlockSpec(memory_space=pltpu.SMEM),
            pl.BlockSpec(memory_space=pltpu.VMEM),
            pl.BlockSpec(memory_space=pltpu.VMEM),
            pl.BlockSpec(memory_space=pl.ANY),
        ],
        out_shape=jax.ShapeDtypeStruct(own.shape, BF16),
        compiler_params=params(),
        name="join_states",
    )(place, own, partner, near)


def near_kernel(ref, cum_ref, gain_ref, out_ref, gate_ref, wide_ref):
    decode_gates(ref, wide_ref, gate_ref)
    gain = gain_ref[...]
    row = lax.broadcasted_iota(jnp.int32, (SUB, WIDTH), 0)
    col = lax.broadcasted_iota(jnp.int32, (SUB, WIDTH), 1) % SUB
    diagonal = row == col
    row = lax.broadcasted_iota(jnp.int32, (BLOCK, WIDTH), 0) % SUB
    col = lax.broadcasted_iota(jnp.int32, (BLOCK, WIDTH), 1) % SUB
    differ = jnp.bitwise_xor(row, col)
    causal = row >= col
    head_row = lax.broadcasted_iota(jnp.int32, (PER_GROUP * SUB, WIDTH), 0) // SUB
    head_col = lax.broadcasted_iota(jnp.int32, (PER_GROUP * SUB, WIDTH), 1) // HEAD_DIM
    same_head = head_row == head_col
    spreads = [spread(128, level, LEVELS) for level in range(7)]
    subs = BLOCK // SUB

    @pl.loop(0, CHUNK // BLOCK)
    def _(k):
        first = k * BLOCK
        cum = cum_ref[pl.ds(first, BLOCK), :]
        x = load_x(ref, first, BLOCK)
        gates = gate_ref[pl.ds(first, BLOCK), :]
        dots = dot_nt(load_c(ref, first, BLOCK), load_b(ref, first, BLOCK))
        picked = dot(gates, spreads[6])
        for level in range(5, -1, -1):
            picked = jnp.where(differ < (1 << level), dot(gates, spreads[level]), picked)
        raw, gap = [], []
        for i in range(subs):
            rows = slice(i * SUB, (i + 1) * SUB)
            raw.append(jnp.concatenate([dots[rows, rows]] * PER_GROUP, axis=1))
            cum_row = jnp.sum(jnp.where(diagonal, cum[rows], 0.0), axis=0, keepdims=True)
            gap.append(cum[rows] - cum_row)
        decay = jnp.exp(jnp.minimum(jnp.concatenate(gap, axis=0), 0.0))
        raw = jnp.concatenate(raw, axis=0)
        scores = jnp.where(causal, raw * decay * picked, 0.0).astype(BF16)
        skip = gain * x.astype(F32)
        for i in range(subs):
            rows = slice(i * SUB, (i + 1) * SUB)
            tall_x = jnp.concatenate([x[rows]] * PER_GROUP, axis=0)
            block_x = jnp.where(same_head, tall_x, jnp.zeros_like(tall_x))
            out_ref[pl.ds(first + i * SUB, SUB), :] = dot(scores[rows], block_x) + skip[rows]


def near_part(received, cum, gain):
    return pl.pallas_call(
        near_kernel,
        out_shape=(
            jax.ShapeDtypeStruct((CHUNK, WIDTH), F32),
            jax.ShapeDtypeStruct((CHUNK, 128), BF16),
        ),
        scratch_shapes=[pltpu.VMEM((64, 16, 64), F32)],
        compiler_params=params(),
        cost_estimate=pl.CostEstimate(
            flops=4 * 10**9, bytes_accessed=4 * 1024 * 1024, transcendentals=10**6
        ),
        name="near_part",
    )(received, cum, gain)


def levels_kernel(ref, cum_ref, gate_ref, near_ref, own_ref, out_ref, grow_ref):
    subs = CHUNK // SUB
    starts = [jnp.zeros((1, WIDTH), F32)]
    starts += [cum_ref[i * SUB - 1 : i * SUB, :] for i in range(1, subs + 1)]
    states = []
    for i in range(subs):
        rows = slice(i * SUB, (i + 1) * SUB)
        cum = cum_ref[rows, :]
        tail = jnp.exp(starts[i + 1] - cum)
        high, low = halves(load_x(ref, i * SUB, SUB).astype(F32) * tail)
        b = load_b(ref, i * SUB, SUB)
        tall = jnp.concatenate([b, b], axis=0)
        states.append(dot_t(tall, jnp.concatenate([high, low], axis=0)))
        grow_ref[rows, :] = jnp.exp(cum - starts[i])
        out_ref[rows, :] = near_ref[rows, :]

    size = 1
    for bit in range(4):
        to_lanes = spread(128, 7 + bit, LEVELS)
        for group in range(1, subs // size, 2):
            rows = slice(group * size * SUB, (group + 1) * size * SUB)
            c = load_c(ref, rows.start, size * SUB)
            lower = jnp.concatenate(halves(states[group - 1]), axis=0)
            reached = dot(jnp.concatenate([c, c], axis=1), lower)
            gates = dot(gate_ref[rows, :], to_lanes)
            for part in range(size):
                i = group * size + part
                here = slice(i * SUB, (i + 1) * SUB)
                there = slice(part * SUB, (part + 1) * SUB)
                weight = gates[there] * grow_ref[here, :]
                if part:
                    weight = weight * jnp.exp(starts[i] - starts[group * size])
                out_ref[here, :] += weight * reached[there]
        states = [
            states[g] * jnp.exp(starts[(g + 2) * size] - starts[(g + 1) * size]) + states[g + 1]
            for g in range(0, subs // size, 2)
        ]
        size *= 2
    for i in range(1, subs):
        rows = slice(i * SUB, (i + 1) * SUB)
        grow_ref[rows, :] = grow_ref[rows, :] * jnp.exp(starts[i])


def levels_part(received, cum, gates, near, own):
    wide = jax.ShapeDtypeStruct((CHUNK, WIDTH), F32)
    vmem = pl.BlockSpec(memory_space=pltpu.VMEM)
    return pl.pallas_call(
        levels_kernel,
        in_specs=[vmem, vmem, vmem, vmem, pl.BlockSpec(memory_space=pl.ANY)],
        out_shape=(wide, wide),
        compiler_params=params(),
        cost_estimate=pl.CostEstimate(
            flops=4 * 10**9, bytes_accessed=4 * 1024 * 1024, transcendentals=10**6
        ),
        name="levels_part",
    )(received, cum, gates, near, own)


def outer_kernel(
    place_ref,
    ref,
    inner_ref,
    grow_ref,
    gate_ref,
    pair_ref,
    one_ref,
    two_ref,
    three_ref,
    out_ref,
):
    place = place_ref[0]
    in_half, odd, high = place % 2 == 1, place // 2 % 2 == 1, place // 4 == 1
    near_state, near_total = message_state(one_ref), message_total(one_ref)
    prefix = jnp.where(in_half, message_total(pair_ref), 0.0)
    far_prefix = prefix + jnp.where(odd, near_total, 0.0)
    late = jnp.where(odd, message_state(two_ref), near_state)
    late_total = jnp.where(odd, message_total(two_ref), near_total)
    early = jnp.where(odd, message_state(three_ref), message_state(two_ref))
    joined = jnp.exp(late_total) * early + late
    levels = (
        jnp.where(in_half, message_state(pair_ref), 0.0),
        jnp.where(odd, jnp.exp(prefix) * near_state, 0.0),
        jnp.where(high, jnp.exp(far_prefix) * joined, 0.0),
    )
    levels = [jnp.concatenate(halves(value), axis=0) for value in levels]
    spreads = [spread(128, 11 + bit, LEVELS) for bit in range(3)]
    for k in range(CHUNK // BLOCK):
        rows = slice(k * BLOCK, (k + 1) * BLOCK)
        c = load_c(ref, k * BLOCK, BLOCK)
        c = jnp.concatenate([c, c], axis=1)
        gates = gate_ref[rows, :]
        total = jnp.zeros((BLOCK, WIDTH), F32)
        for bit in range(3):
            total += dot(gates, spreads[bit]) * dot(c, levels[bit])
        mixed = inner_ref[rows, :] + grow_ref[rows, :] * total
        out_ref[k * 16 : (k + 1) * 16] = mixed.astype(BF16).reshape(BLOCK // 16, 16, WIDTH)


def outer_part(place, received, inner, grow, gates, messages):
    vmem = pl.BlockSpec(memory_space=pltpu.VMEM)
    return pl.pallas_call(
        outer_kernel,
        in_specs=[pl.BlockSpec(memory_space=pltpu.SMEM)] + [vmem] * 8,
        out_specs=vmem,
        out_shape=jax.ShapeDtypeStruct((64, 16, WIDTH), BF16),
        compiler_params=params(),
        name="outer_part",
    )(place, received, inner, grow, gates, *messages)


def unpack_kernel(place_ref, ref, out_ref, held_ref, sems):
    copies = []
    for k in range(SEQS):
        for g in range(GROUPS):
            held_ref[k, :, g * WIDTH : (g + 1) * WIDTH] = ref[k * GROUPS + g]
        copy = pltpu.make_async_copy(
            held_ref.at[k], out_ref.at[sequence_at(k, place_ref[0])], sems.at[k]
        )
        copy.start()
        copies.append(copy)
    for copy in copies:
        copy.wait()


def unpack(place, received):
    shape = (SEQS, 16, HEADS * HEAD_DIM)
    return pl.pallas_call(
        unpack_kernel,
        in_specs=[pl.BlockSpec(memory_space=pltpu.SMEM), pl.BlockSpec(memory_space=pltpu.VMEM)],
        out_specs=pl.BlockSpec(memory_space=pltpu.HBM),
        out_shape=jax.ShapeDtypeStruct(shape, BF16),
        scratch_shapes=[pltpu.VMEM(shape, BF16), pltpu.SemaphoreType.DMA((SEQS,))],
        compiler_params=params(),
        name="unpack_outputs",
    )(place, received)


def per_device(x_heads, b_keys, c_queries, log_decay, level_log, skip_gain):
    near_axes = ("block", "tp")
    place = lax.axis_index("chunk").astype(jnp.int32)[None]
    packed = pack(place, x_heads, b_keys, c_queries, log_decay, level_log)
    received = lax.all_to_all(packed, near_axes, 0, 0, tiled=True)
    gain = jnp.repeat(skip_gain, HEAD_DIM)[None, :]
    own, cum = chunk_state(received)
    pair = lax.ppermute(own, ("chunk", "block"), [(source, source ^ 6) for source in range(32)])
    near, gates = near_part(received, cum, gain)
    own = join(place, own, pair, near)
    shifted = [
        lax.ppermute(own, "chunk", [(source, source + 2 * z) for source in range(8 - 2 * z)])
        for z in (1, 2, 3)
    ]
    inner, grow = levels_part(received, cum, gates, near, own)
    mixed = outer_part(place, received, inner, grow, gates, [pair] + shifted)
    return unpack(place, lax.all_to_all(mixed, near_axes, 0, 0, tiled=True))


def solution(mesh):
    cut = Mesh(mesh.devices.reshape(8, 4, 16), ("chunk", "block", "tp"))
    split = P(None, ("chunk", "block", "tp"), None)
    return jax.shard_map(
        per_device,
        mesh=cut,
        in_specs=(split, split, split, split, split, P("tp")),
        out_specs=split,
        check_vma=False,
    )
```

time: 106 us -> 100 us (0.943)
  Pallas kernels: 17.2 us -> 10.5 us
  starting transfers between devices: 30.8 us -> 33.2 us
  waiting for transfers between devices: 33.6 us -> 31.2 us
    pallas_call x6, Pallas kernels: 17.2 us -> 10.5 us  [the longest x1 2.89 us: pack(): pl.pallas_call(pack_kernel, in_specs=[pl.BlockSpec(memory_space=pltpu.SME...]
    ppermute x1, starting transfers between devices: 4 us -> 6.56 us  [per_device(): lax.ppermute(own, ('chunk', 'block'), [(source, source ^ 6) for source in...]
    ppermute x3, waiting for transfers between devices: 2.37 us -> 0.01 us  [per_device(): lax.ppermute(own, 'chunk', [(source, source + 2 * z) for source in range(...]
  transfers between devices with their start and end apart: 5 -> 5, of which waited for: 2 -> 1; matrix products, arithmetic and copies ran while one was open for 0% -> 0% of each run, Pallas kernels for 8% -> 4%
where the time goes in v3:
time: 100 us; the launch traced here: 99.7 us
  starting transfers between devices  33.2 us (33%)
  waiting for transfers between devices  31.2 us (31%)
  blocking collectives  24.4 us (24%)
  Pallas kernels  10.5 us (10%)
    all_to_all x1, waiting for transfers between devices, per_device(): received = lax.all_to_all(packed, near_axes, 0, 0, tiled=True)  31.2 us
    all_to_all x1, blocking collectives, per_device(): return unpack(place, lax.all_to_all(mixed, near_axes, 0, 0, tiled=True))  24.4 us
    ppermute x3, starting transfers between devices, per_device(): lax.ppermute(own, 'chunk', [(source, source + 2 * z) for source in range(...  15 us
    all_to_all x1, starting transfers between devices, per_device(): received = lax.all_to_all(packed, near_axes, 0, 0, tiled=True)  11.6 us
    ppermute x1, starting transfers between devices, per_device(): lax.ppermute(own, ('chunk', 'block'), [(source, source ^ 6) for source in...  6.56 us
    pallas_call x1, Pallas kernels, pack(): pl.pallas_call(pack_kernel, in_specs=[pl.BlockSpec(memory_space=pltpu.SME...  2.89 us
    pallas_call x1, Pallas kernels, near_part(): pl.pallas_call(near_kernel, out_shape=(jax.ShapeDtypeStruct((CHUNK, WIDTH...  2.84 us
  transfers between devices with their start and end apart: 5, of which 1 were waited for; matrix products, arithmetic and copies ran while one was open for 0% of the time, Pallas kernels for 4%

profile of v3, /device:TPU:1, one launch (start us, length us, event | category | flops | bytes accessed | tf_op | source)
XLA Modules:
  0.0 99.7 jit_solution(12832446660377626357)
XLA Ops:
  0.0 2.9 %pack_messages.1 = bf16[64,72,128]{2,1,0:T(8,128)(2,1)} custom-call(s32[1]{0:T(128)} %bitcast.place_ref, bf16[4,16,4096]{2,1,0:T(8,128)(2,1)} %refs_0_.1, bf16[4,16,2048]{2,1,0:T(8,128)(2,1)} %refs_1_.1, bf16[4,16,2048]{2,1,0:T(8,128)(2,1)} %refs_2_.1, f32[4,16,64]{2,1,0:T(8,128)} %refs_3_.1, f32[4,16,896]{2,1,0:T(8,128)} %refs_4_.1), custom_call_target="tpu_custom_call" | custom-call | tf_op jit(solution)/shard_map/pack_messages/pallas_call | solution.py:95
  2.9 0.0 copy-start
  2.9 11.6 %all-to-all-start = ((bf16[64,72,128]{2,1,0:T(8,128)(2,1)}), bf16[64,72,128]{2,1,0:T(8,128)(2,1)S(1)}, u32[]{:S(2)}, u32[]{:S(2)}) async-start(bf16[64,72,128]{2,1,0:T(8,128)(2,1)} %pack_messages.1), calls=%async_computation | async-start | bytes 2359296 | tf_op jit(solution)/shard_map/all_to_all | solution.py:451
  14.5 0.0 copy-done
  14.6 0.1 broadcast_in_dim.7
  14.6 0.1 broadcast_in_dim_reshape.3.gain_ref
  14.7 31.2 %all-to-all-done.ref = bf16[64,72,128]{2,1,0:T(8,128)(2,1)S(1)} async-done(((bf16[64,72,128]{2,1,0:T(8,128)(2,1)}), bf16[64,72,128]{2,1,0:T(8,128)(2,1)S(1)}, u32[]{:S(2)}, u32[]{:S(2)}) %all-to-all-start) | async-done | bytes 1179680 | tf_op jit(solution)/shard_map/all_to_all | solution.py:451
  45.9 1.4 %chunk_state.1 = (bf16[144,256]{1,0:T(8,128)(2,1)S(1)}, f32[1024,256]{1,0:T(8,128)S(1)}) custom-call(bf16[64,72,128]{2,1,0:T(8,128)(2,1)S(1)} %all-to-all-done.ref), custom_call_target="tpu_custom_call" | custom-call | tf_op jit(solution)/shard_map/chunk_state/pallas_call | solution.py:213
  47.3 6.6 %collective-permute-start = (bf16[144,256]{1,0:T(8,128)(2,1)S(1)}, bf16[144,256]{1,0:T(8,128)(2,1)S(1)}, u32[]{:S(2)}, u32[]{:S(2)}) collective-permute-start(bf16[144,256]{1,0:T(8,128)(2,1)S(1)} %get-tuple-element.14.own_ref), channel_id=1, source_target_pairs={{0,96},{16,112},{32,64},{48,80},{64,32},{80,48},{96,0},{112,16},{1... | collective-permute-start | bytes 221192 | tf_op jit(solution)/shard_map/ppermute | solution.py:454
  53.8 2.8 %near_part.1 = (f32[1024,256]{1,0:T(8,128)S(1)}, bf16[1024,128]{1,0:T(8,128)(2,1)S(1)}) custom-call(bf16[64,72,128]{2,1,0:T(8,128)(2,1)S(1)} %all-to-all-done.ref, f32[1024,256]{1,0:T(8,128)S(1)} %get-tuple-element.11.cum_ref, f32[1,256]{1,0:T(1,128)S(1)} %broadcast_in_dim_reshape.3.gain_ref), custom_call_target="tpu_custom_call" | custom-call | flops 4000000000 | bytes 4194304 | tf_op jit(solution)/shard_map/near_part/pallas_call | solution.py:295
  56.7 0.0 collective-permute-done.partner_ref.pair_ref
  56.8 9.8 %collective-permute-start.3 = (bf16[144,256]{1,0:T(8,128)(2,1)S(1)}, bf16[144,256]{1,0:T(8,128)(2,1)S(1)}, u32[]{:S(2)}, u32[]{:S(2)}) collective-permute-start(bf16[144,256]{1,0:T(8,128)(2,1)S(1)} %join_states.1.own_ref), channel_id=1, source_target_pairs={{0,384},{64,448},{1,385},{65,449},{2,386},{66,450},{3,387},{67,451... | collective-permute-start | bytes 221192 | tf_op jit(solution)/shard_map/ppermute | solution.py:458
  66.5 1.3 %collective-permute-start.2 = (bf16[144,256]{1,0:T(8,128)(2,1)S(1)}, bf16[144,256]{1,0:T(8,128)(2,1)S(1)}, u32[]{:S(2)}, u32[]{:S(2)}) collective-permute-start(bf16[144,256]{1,0:T(8,128)(2,1)S(1)} %join_states.1.own_ref), channel_id=1, source_target_pairs={{0,256},{64,320},{128,384},{192,448},{1,257},{65,321},{129,385},{1... | collective-permute-start | bytes 221192 | tf_op jit(solution)/shard_map/ppermute | solution.py:458
  67.8 4.0 %collective-permute-start.1 = (bf16[144,256]{1,0:T(8,128)(2,1)S(1)}, bf16[144,256]{1,0:T(8,128)(2,1)S(1)}, u32[]{:S(2)}, u32[]{:S(2)}) collective-permute-start(bf16[144,256]{1,0:T(8,128)(2,1)S(1)} %join_states.1.own_ref), channel_id=1, source_target_pairs={{0,128},{64,192},{128,256},{192,320},{256,384},{320,448},{1,129},{... | collective-permute-start | bytes 221192 | tf_op jit(solution)/shard_map/ppermute | solution.py:458
  71.8 1.5 %levels_part.1 = (f32[1024,256]{1,0:T(8,128)S(1)}, f32[1024,256]{1,0:T(8,128)S(1)}) custom-call(bf16[64,72,128]{2,1,0:T(8,128)(2,1)S(1)} %all-to-all-done.ref, f32[1024,256]{1,0:T(8,128)S(1)} %get-tuple-element.11.cum_ref, bf16[1024,128]{1,0:T(8,128)(2,1)S(1)} %get-tuple-element.12.gate_ref, f32[1024,256]{1,0:T(8,128)S(1)} %get-tuple-element.13.near_ref, ...), custom_call_target="tpu_custom_call" | custom-call | flops 4000000000 | bytes 4194304 | tf_op jit(solution)/shard_map/levels_part/pallas_call | solution.py:356
  73.3 0.0 collective-permute-done.3.three_ref
  73.3 0.0 collective-permute-done.2.two_ref
  73.4 0.0 collective-permute-done.1.one_ref
  73.4 1.1 %outer_part.1 = bf16[64,16,256]{2,1,0:T(8,128)(2,1)S(1)} custom-call(s32[1]{0:T(128)} %bitcast.place_ref, bf16[64,72,128]{2,1,0:T(8,128)(2,1)S(1)} %all-to-all-done.ref, f32[1024,256]{1,0:T(8,128)S(1)} %get-tuple-element.15.inner_ref, f32[1024,256]{1,0:T(8,128)S(1)} %get-tuple-element.16.grow_ref, bf16[1024,128]{1,0:T(8,128)(2,1)S(1)} %get-tuple-element.12.gate_ref, ...), custom_call_target="tpu_custom_call" | custom-call | tf_op jit(solution)/shard_map/outer_part/pallas_call | solution.py:410
  74.4 24.4 %all_to_all.10.ref = bf16[64,16,256]{2,1,0:T(8,128)(2,1)S(1)} all-to-all(bf16[64,16,256]{2,1,0:T(8,128)(2,1)S(1)} %outer_part.1), channel_id=1, replica_groups=mesh['chunk'=8,'block'=4,'tp'=16] {'block','tp'}, dimensions={0} | all-to-all | bytes 1048576 | tf_op jit(solution)/shard_map/all_to_all | solution.py:463
  98.8 0.8 unpack_outputs.1
  (1 shorter events, 0.0 us)
Async XLA Ops:
  2.9 11.7 %copy-start = (f32[4]{0:T(128)S(1)}, f32[4]{0:T(128)}, u32[]{:S(2)}) copy-start(f32[4]{0:T(128)} %param.11) | copy-start | bytes 52
  2.9 43.0 %all-to-all-start = ((bf16[64,72,128]{2,1,0:T(8,128)(2,1)}), bf16[64,72,128]{2,1,0:T(8,128)(2,1)S(1)}, u32[]{:S(2)}, u32[]{:S(2)}) async-start(bf16[64,72,128]{2,1,0:T(8,128)(2,1)} %pack_messages.1), calls=%async_computation | async-start | bytes 2359296 | tf_op jit(solution)/shard_map/all_to_all | solution.py:451
  47.3 9.4 %collective-permute-start = (bf16[144,256]{1,0:T(8,128)(2,1)S(1)}, bf16[144,256]{1,0:T(8,128)(2,1)S(1)}, u32[]{:S(2)}, u32[]{:S(2)}) collective-permute-start(bf16[144,256]{1,0:T(8,128)(2,1)S(1)} %get-tuple-element.14.own_ref), channel_id=1, source_target_pairs={{0,96},{16,112},{32,64},{48,80},{64,32},{80,48},{96,0},{112,16},{1... | collective-permute-start | bytes 221192 | tf_op jit(solution)/shard_map/ppermute | solution.py:454
  56.8 16.6 %collective-permute-start.3 = (bf16[144,256]{1,0:T(8,128)(2,1)S(1)}, bf16[144,256]{1,0:T(8,128)(2,1)S(1)}, u32[]{:S(2)}, u32[]{:S(2)}) collective-permute-start(bf16[144,256]{1,0:T(8,128)(2,1)S(1)} %join_states.1.own_ref), channel_id=1, source_target_pairs={{0,384},{64,448},{1,385},{65,449},{2,386},{66,450},{3,387},{67,451... | collective-permute-start | bytes 221192 | tf_op jit(solution)/shard_map/ppermute | solution.py:458
  66.5 6.8 %collective-permute-start.2 = (bf16[144,256]{1,0:T(8,128)(2,1)S(1)}, bf16[144,256]{1,0:T(8,128)(2,1)S(1)}, u32[]{:S(2)}, u32[]{:S(2)}) collective-permute-start(bf16[144,256]{1,0:T(8,128)(2,1)S(1)} %join_states.1.own_ref), channel_id=1, source_target_pairs={{0,256},{64,320},{128,384},{192,448},{1,257},{65,321},{129,385},{1... | collective-permute-start | bytes 221192 | tf_op jit(solution)/shard_map/ppermute | solution.py:458
  67.8 5.5 %collective-permute-start.1 = (bf16[144,256]{1,0:T(8,128)(2,1)S(1)}, bf16[144,256]{1,0:T(8,128)(2,1)S(1)}, u32[]{:S(2)}, u32[]{:S(2)}) collective-permute-start(bf16[144,256]{1,0:T(8,128)(2,1)S(1)} %join_states.1.own_ref), channel_id=1, source_target_pairs={{0,128},{64,192},{128,256},{192,320},{256,384},{320,448},{1,129},{... | collective-permute-start | bytes 221192 | tf_op jit(solution)/shard_map/ppermute | solution.py:458

commit v4 on v3

--- a/solution.py
+++ b/solution.py
@@ -42,19 +42,13 @@
     return pltpu.CompilerParams(vmem_limit_bytes=VMEM_LIMIT)
 
 
-def sequence_at(block, place):
-    return jnp.bitwise_xor(block, 2 * (place % 2))
-
-
-def pack_kernel(place_ref, *refs):
+def pack_kernel(*refs):
     sources, out_ref = refs[:5], refs[5]
     x_ref, b_ref, c_ref, decay_ref, level_ref = held = refs[6:11]
     packed_ref, sems, out_sems = refs[11:]
     copies = [
         [
-            pltpu.make_async_copy(
-                source.at[sequence_at(k, place_ref[0])], slot.at[k], sems.at[i, k]
-            )
+            pltpu.make_async_copy(source.at[k], slot.at[k], sems.at[i, k])
             for i, (source, slot) in enumerate(zip(sources, held))
         ]
         for k in range(SEQS)
@@ -90,12 +84,11 @@
         copy.wait()
 
 
-def pack(place, *arrays):
+def pack(*arrays):
     shape = (SEQS * GROUPS, ROWS, 128)
     return pl.pallas_call(
         pack_kernel,
-        in_specs=[pl.BlockSpec(memory_space=pltpu.SMEM)]
-        + [pl.BlockSpec(memory_space=pltpu.HBM)] * len(arrays),
+        in_specs=[pl.BlockSpec(memory_space=pltpu.HBM)] * len(arrays),
         out_specs=pl.BlockSpec(memory_space=pltpu.HBM),
         out_shape=jax.ShapeDtypeStruct(shape, BF16),
         scratch_shapes=[pltpu.VMEM(a.shape, a.dtype) for a in arrays]
@@ -105,7 +98,7 @@
             pltpu.SemaphoreType.DMA((SEQS,)),
         ],
         name="pack_messages",
-    )(place, *arrays)
+    )(*arrays)
 
 
 def load_rows(ref, first, count, start, stop):
@@ -372,24 +365,23 @@
     grow_ref,
     gate_ref,
     pair_ref,
-    one_ref,
-    two_ref,
-    three_ref,
+    top_ref,
+    skip_ref,
+    cross_ref,
+    low_ref,
     out_ref,
 ):
     place = place_ref[0]
-    in_half, odd, high = place % 2 == 1, place // 2 % 2 == 1, place // 4 == 1
-    near_state, near_total = message_state(one_ref), message_total(one_ref)
+    in_half, odd = place % 2 == 1, place // 2 % 2 == 1
     prefix = jnp.where(in_half, message_total(pair_ref), 0.0)
-    far_prefix = prefix + jnp.where(odd, near_total, 0.0)
-    late = jnp.where(odd, message_state(two_ref), near_state)
-    late_total = jnp.where(odd, message_total(two_ref), near_total)
-    early = jnp.where(odd, message_state(three_ref), message_state(two_ref))
-    joined = jnp.exp(late_total) * early + late
+    far_prefix = prefix + message_total(low_ref) + message_total(top_ref)
+    cross, skip = message_state(cross_ref), message_state(skip_ref)
+    late_total = jnp.where(odd, message_total(skip_ref), message_total(cross_ref))
+    joined = jnp.exp(late_total) * jnp.where(odd, cross, skip) + jnp.where(odd, skip, cross)
     levels = (
         jnp.where(in_half, message_state(pair_ref), 0.0),
-        jnp.where(odd, jnp.exp(prefix) * near_state, 0.0),
-        jnp.where(high, jnp.exp(far_prefix) * joined, 0.0),
+        jnp.exp(prefix) * (message_state(low_ref) + message_state(top_ref)),
+        jnp.exp(far_prefix) * joined,
     )
     levels = [jnp.concatenate(halves(value), axis=0) for value in levels]
     spreads = [spread(128, 11 + bit, LEVELS) for bit in range(3)]
@@ -409,7 +401,7 @@
     vmem = pl.BlockSpec(memory_space=pltpu.VMEM)
     return pl.pallas_call(
         outer_kernel,
-        in_specs=[pl.BlockSpec(memory_space=pltpu.SMEM)] + [vmem] * 8,
+        in_specs=[pl.BlockSpec(memory_space=pltpu.SMEM)] + [vmem] * 9,
         out_specs=vmem,
         out_shape=jax.ShapeDtypeStruct((64, 16, WIDTH), BF16),
         compiler_params=params(),
@@ -417,50 +409,49 @@
     )(place, received, inner, grow, gates, *messages)
 
 
-def unpack_kernel(place_ref, ref, out_ref, held_ref, sems):
+def unpack_kernel(ref, out_ref, held_ref, sems):
     copies = []
     for k in range(SEQS):
         for g in range(GROUPS):
             held_ref[k, :, g * WIDTH : (g + 1) * WIDTH] = ref[k * GROUPS + g]
-        copy = pltpu.make_async_copy(
-            held_ref.at[k], out_ref.at[sequence_at(k, place_ref[0])], sems.at[k]
-        )
+        copy = pltpu.make_async_copy(held_ref.at[k], out_ref.at[k], sems.at[k])
         copy.start()
         copies.append(copy)
     for copy in copies:
         copy.wait()
 
 
-def unpack(place, received):
+def unpack(received):
     shape = (SEQS, 16, HEADS * HEAD_DIM)
     return pl.pallas_call(
         unpack_kernel,
-        in_specs=[pl.BlockSpec(memory_space=pltpu.SMEM), pl.BlockSpec(memory_space=pltpu.VMEM)],
+        in_specs=[pl.BlockSpec(memory_space=pltpu.VMEM)],
         out_specs=pl.BlockSpec(memory_space=pltpu.HBM),
         out_shape=jax.ShapeDtypeStruct(shape, BF16),
         scratch_shapes=[pltpu.VMEM(shape, BF16), pltpu.SemaphoreType.DMA((SEQS,))],
         compiler_params=params(),
         name="unpack_outputs",
-    )(place, received)
+    )(received)
 
 
 def per_device(x_heads, b_keys, c_queries, log_decay, level_log, skip_gain):
     near_axes = ("block", "tp")
     place = lax.axis_index("chunk").astype(jnp.int32)[None]
-    packed = pack(place, x_heads, b_keys, c_queries, log_decay, level_log)
+    packed = pack(x_heads, b_keys, c_queries, log_decay, level_log)
     received = lax.all_to_all(packed, near_axes, 0, 0, tiled=True)
     gain = jnp.repeat(skip_gain, HEAD_DIM)[None, :]
     own, cum = chunk_state(received)
-    pair = lax.ppermute(own, ("chunk", "block"), [(source, source ^ 6) for source in range(32)])
+    pair = lax.ppermute(own, "chunk", [(source, source ^ 1) for source in range(8)])
     near, gates = near_part(received, cum, gain)
     own = join(place, own, pair, near)
-    shifted = [
-        lax.ppermute(own, "chunk", [(source, source + 2 * z) for source in range(8 - 2 * z)])
-        for z in (1, 2, 3)
+    steps = [[(2, 3)], [(0, 2), (1, 3)], [(0, 3), (1, 2)], [(0, 1)]]
+    shared = [
+        lax.ppermute(own, "chunk", [(2 * a + half, 2 * b + 1 - half) for a, b in step for half in (0, 1)])
+        for step in steps
     ]
     inner, grow = levels_part(received, cum, gates, near, own)
-    mixed = outer_part(place, received, inner, grow, gates, [pair] + shifted)
-    return unpack(place, lax.all_to_all(mixed, near_axes, 0, 0, tiled=True))
+    mixed = outer_part(place, received, inner, grow, gates, [pair] + shared)
+    return unpack(lax.all_to_all(mixed, near_axes, 0, 0, tiled=True))
 
 
 def solution(mesh):

time: 100 us -> 97 us (0.970)
  starting transfers between devices: 33.2 us -> 27.8 us
  waiting for transfers between devices: 31.2 us -> 34 us
    ppermute x4 -> x5, starting transfers between devices: 21.6 us -> 16.2 us  [the longest x4 12.2 us: per_device(): lax.ppermute(own, 'chunk', [(2 * a + half, 2 * b + 1 - half) for a, b in...]
    ppermute x4 -> x5, waiting for transfers between devices: 0.01 us -> 2.83 us  [the longest x4 2.83 us: per_device(): lax.ppermute(own, 'chunk', [(2 * a + half, 2 * b + 1 - half) for a, b in...]
  transfers between devices with their start and end apart: 5 -> 6, of which waited for: 1 -> 2; matrix products, arithmetic and copies ran while one was open for 0% -> 0% of each run, Pallas kernels for 4% -> 4%
where the time goes in v4:
time: 97 us; the launch traced here: 96.7 us
  waiting for transfers between devices  34 us (35%)
  starting transfers between devices  27.8 us (29%)
  blocking collectives  24.1 us (25%)
  Pallas kernels  10.4 us (11%)
    all_to_all x1, waiting for transfers between devices, per_device(): received = lax.all_to_all(packed, near_axes, 0, 0, tiled=True)  31.2 us
    all_to_all x1, blocking collectives, per_device(): return unpack(lax.all_to_all(mixed, near_axes, 0, 0, tiled=True))  24.1 us
    ppermute x4, starting transfers between devices, per_device(): lax.ppermute(own, 'chunk', [(2 * a + half, 2 * b + 1 - half) for a, b in...  12.2 us
    all_to_all x1, starting transfers between devices, per_device(): received = lax.all_to_all(packed, near_axes, 0, 0, tiled=True)  11.6 us
    ppermute x1, starting transfers between devices, per_device(): lax.ppermute(own, 'chunk', [(source, source ^ 1) for source in range(8)])  4 us
    pallas_call x1, Pallas kernels, pack(): pl.pallas_call(pack_kernel, in_specs=[pl.BlockSpec(memory_space=pltpu.HBM...  2.87 us
    pallas_call x1, Pallas kernels, near_part(): pl.pallas_call(near_kernel, out_shape=(jax.ShapeDtypeStruct((CHUNK, WIDTH...  2.83 us
    ppermute x4, waiting for transfers between devices, per_device(): lax.ppermute(own, 'chunk', [(2 * a + half, 2 * b + 1 - half) for a, b in...  2.83 us
  transfers between devices with their start and end apart: 6, of which 2 were waited for; matrix products, arithmetic and copies ran while one was open for 0% of the time, Pallas kernels for 4%

profile of v4, /device:TPU:1, one launch (start us, length us, event | category | flops | bytes accessed | tf_op | source)
XLA Modules:
  0.0 96.7 jit_solution(299313393747150077)
XLA Ops:
  0.0 2.9 %pack_messages.1 = bf16[64,72,128]{2,1,0:T(8,128)(2,1)} custom-call(bf16[4,16,4096]{2,1,0:T(8,128)(2,1)} %refs_0_.1, bf16[4,16,2048]{2,1,0:T(8,128)(2,1)} %refs_1_.1, bf16[4,16,2048]{2,1,0:T(8,128)(2,1)} %refs_2_.1, f32[4,16,64]{2,1,0:T(8,128)} %refs_3_.1, f32[4,16,896]{2,1,0:T(8,128)} %refs_4_.1), custom_call_target="tpu_custom_call" | custom-call | tf_op jit(solution)/shard_map/pack_messages/pallas_call | solution.py:89
  2.9 0.0 copy-start
  2.9 11.6 %all-to-all-start = ((bf16[64,72,128]{2,1,0:T(8,128)(2,1)}), bf16[64,72,128]{2,1,0:T(8,128)(2,1)S(1)}, u32[]{:S(2)}, u32[]{:S(2)}) async-start(bf16[64,72,128]{2,1,0:T(8,128)(2,1)} %pack_messages.1), calls=%async_computation | async-start | bytes 2359296 | tf_op jit(solution)/shard_map/all_to_all | solution.py:441
  14.5 0.0 copy-done
  14.5 0.1 broadcast_in_dim.7
  14.6 0.1 broadcast_in_dim_reshape.3.gain_ref
  14.7 31.2 %all-to-all-done.ref = bf16[64,72,128]{2,1,0:T(8,128)(2,1)S(1)} async-done(((bf16[64,72,128]{2,1,0:T(8,128)(2,1)}), bf16[64,72,128]{2,1,0:T(8,128)(2,1)S(1)}, u32[]{:S(2)}, u32[]{:S(2)}) %all-to-all-start) | async-done | bytes 1179680 | tf_op jit(solution)/shard_map/all_to_all | solution.py:441
  45.9 1.4 %chunk_state.1 = (bf16[144,256]{1,0:T(8,128)(2,1)S(1)}, f32[1024,256]{1,0:T(8,128)S(1)}) custom-call(bf16[64,72,128]{2,1,0:T(8,128)(2,1)S(1)} %all-to-all-done.ref), custom_call_target="tpu_custom_call" | custom-call | tf_op jit(solution)/shard_map/chunk_state/pallas_call | solution.py:206
  47.3 4.0 %collective-permute-start = (bf16[144,256]{1,0:T(8,128)(2,1)S(1)}, bf16[144,256]{1,0:T(8,128)(2,1)S(1)}, u32[]{:S(2)}, u32[]{:S(2)}) collective-permute-start(bf16[144,256]{1,0:T(8,128)(2,1)S(1)} %get-tuple-element.14.own_ref), channel_id=1, source_target_pairs={{0,64},{64,0},{128,192},{192,128},{256,320},{320,256},{384,448},{4... | collective-permute-start | bytes 221192 | tf_op jit(solution)/shard_map/ppermute | solution.py:444
  51.3 2.8 %near_part.1 = (f32[1024,256]{1,0:T(8,128)S(1)}, bf16[1024,128]{1,0:T(8,128)(2,1)S(1)}) custom-call(bf16[64,72,128]{2,1,0:T(8,128)(2,1)S(1)} %all-to-all-done.ref, f32[1024,256]{1,0:T(8,128)S(1)} %get-tuple-element.11.cum_ref, f32[1,256]{1,0:T(1,128)S(1)} %broadcast_in_dim_reshape.3.gain_ref), custom_call_target="tpu_custom_call" | custom-call | flops 4000000000 | bytes 4194304 | tf_op jit(solution)/shard_map/near_part/pallas_call | solution.py:288
  54.1 0.0 collective-permute-done.partner_ref.pair_ref
  54.1 0.1 join_states.1.own_ref
  54.2 6.5 %collective-permute-start.4 = (bf16[144,256]{1,0:T(8,128)(2,1)S(1)}, bf16[144,256]{1,0:T(8,128)(2,1)S(1)}, u32[]{:S(2)}, u32[]{:S(2)}) collective-permute-start(bf16[144,256]{1,0:T(8,128)(2,1)S(1)} %join_states.1.own_ref), channel_id=1, source_target_pairs={{0,192},{64,128},{1,193},{65,129},{2,194},{66,130},{3,195},{67,131... | collective-permute-start | bytes 221192 | tf_op jit(solution)/shard_map/ppermute | solution.py:449
  60.7 3.7 %collective-permute-start.3 = (bf16[144,256]{1,0:T(8,128)(2,1)S(1)}, bf16[144,256]{1,0:T(8,128)(2,1)S(1)}, u32[]{:S(2)}, u32[]{:S(2)}) collective-permute-start(bf16[144,256]{1,0:T(8,128)(2,1)S(1)} %join_states.1.own_ref), channel_id=1, source_target_pairs={{0,448},{64,384},{128,320},{192,256},{1,449},{65,385},{129,321},{1... | collective-permute-start | bytes 221192 | tf_op jit(solution)/shard_map/ppermute | solution.py:449
  64.4 1.3 %collective-permute-start.2 = (bf16[144,256]{1,0:T(8,128)(2,1)S(1)}, bf16[144,256]{1,0:T(8,128)(2,1)S(1)}, u32[]{:S(2)}, u32[]{:S(2)}) collective-permute-start(bf16[144,256]{1,0:T(8,128)(2,1)S(1)} %join_states.1.own_ref), channel_id=1, source_target_pairs={{0,320},{64,256},{128,448},{192,384},{1,321},{65,257},{129,449},{1... | collective-permute-start | bytes 221192 | tf_op jit(solution)/shard_map/ppermute | solution.py:449
  65.7 0.7 collective-permute-start.1
  66.4 1.5 %levels_part.1 = (f32[1024,256]{1,0:T(8,128)S(1)}, f32[1024,256]{1,0:T(8,128)S(1)}) custom-call(bf16[64,72,128]{2,1,0:T(8,128)(2,1)S(1)} %all-to-all-done.ref, f32[1024,256]{1,0:T(8,128)S(1)} %get-tuple-element.11.cum_ref, bf16[1024,128]{1,0:T(8,128)(2,1)S(1)} %get-tuple-element.12.gate_ref, f32[1024,256]{1,0:T(8,128)S(1)} %get-tuple-element.13.near_ref, ...), custom_call_target="tpu_custom_call" | custom-call | flops 4000000000 | bytes 4194304 | tf_op jit(solution)/shard_map/levels_part/pallas_call | solution.py:349
  67.9 0.0 collective-permute-done.4.low_ref
  67.9 0.0 collective-permute-done.3.cross_ref
  67.9 2.8 %collective-permute-done.2.skip_ref = bf16[144,256]{1,0:T(8,128)(2,1)S(1)} collective-permute-done((bf16[144,256]{1,0:T(8,128)(2,1)S(1)}, bf16[144,256]{1,0:T(8,128)(2,1)S(1)}, u32[]{:S(2)}, u32[]{:S(2)}) %collective-permute-start.2) | collective-permute-done | bytes 73760 | tf_op jit(solution)/shard_map/ppermute | solution.py:449
  70.8 0.0 collective-permute-done.1.top_ref
  70.8 1.0 %outer_part.1 = bf16[64,16,256]{2,1,0:T(8,128)(2,1)S(1)} custom-call(s32[1]{0:T(128)} %bitcast.place_ref, bf16[64,72,128]{2,1,0:T(8,128)(2,1)S(1)} %all-to-all-done.ref, f32[1024,256]{1,0:T(8,128)S(1)} %get-tuple-element.15.inner_ref, f32[1024,256]{1,0:T(8,128)S(1)} %get-tuple-element.16.grow_ref, bf16[1024,128]{1,0:T(8,128)(2,1)S(1)} %get-tuple-element.12.gate_ref, ...), custom_call_target="tpu_custom_call" | custom-call | tf_op jit(solution)/shard_map/outer_part/pallas_call | solution.py:402
  71.8 24.1 %all_to_all.10.ref = bf16[64,16,256]{2,1,0:T(8,128)(2,1)S(1)} all-to-all(bf16[64,16,256]{2,1,0:T(8,128)(2,1)S(1)} %outer_part.1), channel_id=1, replica_groups=mesh['chunk'=8,'block'=4,'tp'=16] {'block','tp'}, dimensions={0} | all-to-all | bytes 1048576 | tf_op jit(solution)/shard_map/all_to_all | solution.py:454
  95.9 0.8 unpack_outputs.1
Async XLA Ops:
  2.9 11.7 %copy-start = (f32[4]{0:T(128)S(1)}, f32[4]{0:T(128)}, u32[]{:S(2)}) copy-start(f32[4]{0:T(128)} %param.11) | copy-start | bytes 52
  2.9 43.0 %all-to-all-start = ((bf16[64,72,128]{2,1,0:T(8,128)(2,1)}), bf16[64,72,128]{2,1,0:T(8,128)(2,1)S(1)}, u32[]{:S(2)}, u32[]{:S(2)}) async-start(bf16[64,72,128]{2,1,0:T(8,128)(2,1)} %pack_messages.1), calls=%async_computation | async-start | bytes 2359296 | tf_op jit(solution)/shard_map/all_to_all | solution.py:441
  47.3 6.9 %collective-permute-start = (bf16[144,256]{1,0:T(8,128)(2,1)S(1)}, bf16[144,256]{1,0:T(8,128)(2,1)S(1)}, u32[]{:S(2)}, u32[]{:S(2)}) collective-permute-start(bf16[144,256]{1,0:T(8,128)(2,1)S(1)} %get-tuple-element.14.own_ref), channel_id=1, source_target_pairs={{0,64},{64,0},{128,192},{192,128},{256,320},{320,256},{384,448},{4... | collective-permute-start | bytes 221192 | tf_op jit(solution)/shard_map/ppermute | solution.py:444
  54.2 13.7 %collective-permute-start.4 = (bf16[144,256]{1,0:T(8,128)(2,1)S(1)}, bf16[144,256]{1,0:T(8,128)(2,1)S(1)}, u32[]{:S(2)}, u32[]{:S(2)}) collective-permute-start(bf16[144,256]{1,0:T(8,128)(2,1)S(1)} %join_states.1.own_ref), channel_id=1, source_target_pairs={{0,192},{64,128},{1,193},{65,129},{2,194},{66,130},{3,195},{67,131... | collective-permute-start | bytes 221192 | tf_op jit(solution)/shard_map/ppermute | solution.py:449
  60.7 7.2 %collective-permute-start.3 = (bf16[144,256]{1,0:T(8,128)(2,1)S(1)}, bf16[144,256]{1,0:T(8,128)(2,1)S(1)}, u32[]{:S(2)}, u32[]{:S(2)}) collective-permute-start(bf16[144,256]{1,0:T(8,128)(2,1)S(1)} %join_states.1.own_ref), channel_id=1, source_target_pairs={{0,448},{64,384},{128,320},{192,256},{1,449},{65,385},{129,321},{1... | collective-permute-start | bytes 221192 | tf_op jit(solution)/shard_map/ppermute | solution.py:449
  64.4 6.3 %collective-permute-start.2 = (bf16[144,256]{1,0:T(8,128)(2,1)S(1)}, bf16[144,256]{1,0:T(8,128)(2,1)S(1)}, u32[]{:S(2)}, u32[]{:S(2)}) collective-permute-start(bf16[144,256]{1,0:T(8,128)(2,1)S(1)} %join_states.1.own_ref), channel_id=1, source_target_pairs={{0,320},{64,256},{128,448},{192,384},{1,321},{65,257},{129,449},{1... | collective-permute-start | bytes 221192 | tf_op jit(solution)/shard_map/ppermute | solution.py:449
  65.7 5.0 %collective-permute-start.1 = (bf16[144,256]{1,0:T(8,128)(2,1)S(1)}, bf16[144,256]{1,0:T(8,128)(2,1)S(1)}, u32[]{:S(2)}, u32[]{:S(2)}) collective-permute-start(bf16[144,256]{1,0:T(8,128)(2,1)S(1)} %join_states.1.own_ref), channel_id=1, source_target_pairs={{256,448},{320,384},{257,449},{321,385},{258,450},{322,386},{259,4... | collective-permute-start | bytes 221192 | tf_op jit(solution)/shard_map/ppermute | solution.py:449

commit v5 on v4

--- a/solution.py
+++ b/solution.py
@@ -241,6 +241,24 @@
     )(place, own, partner, near)
 
 
+def relay_kernel(before_ref, first_ref, inner_ref, out_ref):
+    total = message_total(before_ref)
+    state = jnp.exp(total) * message_state(first_ref) + message_state(before_ref)
+    out_ref[0:STATE, :] = state.astype(BF16)
+    out_ref[STATE : STATE + 16, :] = split_rows(total + message_total(first_ref))
+
+
+def relay(before, first, inner):
+    vmem = pl.BlockSpec(memory_space=pltpu.VMEM)
+    return pl.pallas_call(
+        relay_kernel,
+        in_specs=[vmem, vmem, pl.BlockSpec(memory_space=pl.ANY)],
+        out_shape=jax.ShapeDtypeStruct(before.shape, BF16),
+        compiler_params=params(),
+        name="relay_states",
+    )(before, first, inner)
+
+
 def near_kernel(ref, cum_ref, gain_ref, out_ref, gate_ref, wide_ref):
     decode_gates(ref, wide_ref, gate_ref)
     gain = gain_ref[...]
@@ -300,7 +318,8 @@
     )(received, cum, gain)
 
 
-def levels_kernel(ref, cum_ref, gate_ref, near_ref, own_ref, out_ref, grow_ref):
+def levels_kernel(ref, cum_ref, gate_ref, near_ref, own_ref, out_ref, grow_ref, copy_ref):
+    copy_ref[...] = own_ref[...]
     subs = CHUNK // SUB
     starts = [jnp.zeros((1, WIDTH), F32)]
     starts += [cum_ref[i * SUB - 1 : i * SUB, :] for i in range(1, subs + 1)]
@@ -348,8 +367,8 @@
     vmem = pl.BlockSpec(memory_space=pltpu.VMEM)
     return pl.pallas_call(
         levels_kernel,
-        in_specs=[vmem, vmem, vmem, vmem, pl.BlockSpec(memory_space=pl.ANY)],
-        out_shape=(wide, wide),
+        in_specs=[vmem] * 5,
+        out_shape=(wide, wide, jax.ShapeDtypeStruct(own.shape, BF16)),
         compiler_params=params(),
         cost_estimate=pl.CostEstimate(
             flops=4 * 10**9, bytes_accessed=4 * 1024 * 1024, transcendentals=10**6
@@ -365,23 +384,20 @@
     grow_ref,
     gate_ref,
     pair_ref,
-    top_ref,
-    skip_ref,
-    cross_ref,
-    low_ref,
+    before_ref,
+    last_ref,
+    own_far_ref,
+    far_ref,
     out_ref,
 ):
     place = place_ref[0]
-    in_half, odd = place % 2 == 1, place // 2 % 2 == 1
+    in_half, one, two = place % 2 == 1, place // 2 == 1, place // 2 == 2
     prefix = jnp.where(in_half, message_total(pair_ref), 0.0)
-    far_prefix = prefix + message_total(low_ref) + message_total(top_ref)
-    cross, skip = message_state(cross_ref), message_state(skip_ref)
-    late_total = jnp.where(odd, message_total(skip_ref), message_total(cross_ref))
-    joined = jnp.exp(late_total) * jnp.where(odd, cross, skip) + jnp.where(odd, skip, cross)
+    far_prefix = prefix + message_total(last_ref)
     levels = (
         jnp.where(in_half, message_state(pair_ref), 0.0),
-        jnp.exp(prefix) * (message_state(low_ref) + message_state(top_ref)),
-        jnp.exp(far_prefix) * joined,
+        jnp.exp(prefix) * jnp.where(one, message_state(before_ref), message_state(last_ref)),
+        jnp.exp(far_prefix) * jnp.where(two, message_state(own_far_ref), message_state(far_ref)),
     )
     levels = [jnp.concatenate(halves(value), axis=0) for value in levels]
     spreads = [spread(128, 11 + bit, LEVELS) for bit in range(3)]
@@ -444,12 +460,18 @@
     pair = lax.ppermute(own, "chunk", [(source, source ^ 1) for source in range(8)])
     near, gates = near_part(received, cum, gain)
     own = join(place, own, pair, near)
-    steps = [[(2, 3)], [(0, 2), (1, 3)], [(0, 3), (1, 2)], [(0, 1)]]
-    shared = [
-        lax.ppermute(own, "chunk", [(2 * a + half, 2 * b + 1 - half) for a, b in step for half in (0, 1)])
-        for step in steps
-    ]
-    inner, grow = levels_part(received, cum, gates, near, own)
+
+    def up(value, step):
+        pairs = [(2 * a + half, 2 * b + 1 - half) for a, b in step for half in (0, 1)]
+        return lax.ppermute(value, "chunk", pairs)
+
+    first = up(own, [(0, 2)])
+    before = up(own, [(0, 1), (1, 2)])
+    inner, grow, later = levels_part(received, cum, gates, near, own)
+    last = up(later, [(2, 3)])
+    own_far = relay(before, first, inner)
+    far = up(own_far, [(2, 3)])
+    shared = [before, last, own_far, far]
     mixed = outer_part(place, received, inner, grow, gates, [pair] + shared)
     return unpack(lax.all_to_all(mixed, near_axes, 0, 0, tiled=True))
 

time: 97 us -> 94.8 us (0.977)
  waiting for transfers between devices: 34 us -> 31.2 us
    ppermute x4, waiting for transfers between devices: 2.83 us -> 0.01 us  [up(): return lax.ppermute(value, 'chunk', pairs)]
  transfers between devices with their start and end apart: 6 -> 6, of which waited for: 2 -> 1; matrix products, arithmetic and copies ran while one was open for 0% -> 0% of each run, Pallas kernels for 4% -> 5%
where the time goes in v5:
time: 94.8 us; the launch traced here: 93.8 us
  waiting for transfers between devices  31.2 us (33%)
  starting transfers between devices  27.9 us (29%)
  blocking collectives  24 us (25%)
  Pallas kernels  10.4 us (11%)
    all_to_all x1, waiting for transfers between devices, per_device(): received = lax.all_to_all(packed, near_axes, 0, 0, tiled=True)  31.2 us
    all_to_all x1, blocking collectives, per_device(): return unpack(lax.all_to_all(mixed, near_axes, 0, 0, tiled=True))  24 us
    ppermute x4, starting transfers between devices, up(): return lax.ppermute(value, 'chunk', pairs)  12.3 us
    all_to_all x1, starting transfers between devices, per_device(): received = lax.all_to_all(packed, near_axes, 0, 0, tiled=True)  11.6 us
    ppermute x1, starting transfers between devices, per_device(): lax.ppermute(own, 'chunk', [(source, source ^ 1) for source in range(8)])  4 us
    pallas_call x1, Pallas kernels, pack(): pl.pallas_call(pack_kernel, in_specs=[pl.BlockSpec(memory_space=pltpu.HBM...  2.87 us
    pallas_call x1, Pallas kernels, near_part(): pl.pallas_call(near_kernel, out_shape=(jax.ShapeDtypeStruct((CHUNK, WIDTH...  2.77 us
  transfers between devices with their start and end apart: 6, of which 1 were waited for; matrix products, arithmetic and copies ran while one was open for 0% of the time, Pallas kernels for 5%

profile of v5, /device:TPU:1, one launch (start us, length us, event | category | flops | bytes accessed | tf_op | source)
XLA Modules:
  0.0 93.8 jit_solution(15558902394913033830)
XLA Ops:
  0.0 2.9 %pack_messages.1 = bf16[64,72,128]{2,1,0:T(8,128)(2,1)} custom-call(bf16[4,16,4096]{2,1,0:T(8,128)(2,1)} %refs_0_.1, bf16[4,16,2048]{2,1,0:T(8,128)(2,1)} %refs_1_.1, bf16[4,16,2048]{2,1,0:T(8,128)(2,1)} %refs_2_.1, f32[4,16,64]{2,1,0:T(8,128)} %refs_3_.1, f32[4,16,896]{2,1,0:T(8,128)} %refs_4_.1), custom_call_target="tpu_custom_call" | custom-call | tf_op jit(solution)/shard_map/pack_messages/pallas_call | solution.py:89
  2.9 0.0 copy-start
  2.9 11.6 %all-to-all-start = ((bf16[64,72,128]{2,1,0:T(8,128)(2,1)}), bf16[64,72,128]{2,1,0:T(8,128)(2,1)S(1)}, u32[]{:S(2)}, u32[]{:S(2)}) async-start(bf16[64,72,128]{2,1,0:T(8,128)(2,1)} %pack_messages.1), calls=%async_computation | async-start | bytes 2359296 | tf_op jit(solution)/shard_map/all_to_all | solution.py:457
  14.5 0.0 copy-done
  14.5 0.1 broadcast_in_dim.7
  14.6 0.1 broadcast_in_dim_reshape.3.gain_ref
  14.7 31.2 %all-to-all-done.ref = bf16[64,72,128]{2,1,0:T(8,128)(2,1)S(1)} async-done(((bf16[64,72,128]{2,1,0:T(8,128)(2,1)}), bf16[64,72,128]{2,1,0:T(8,128)(2,1)S(1)}, u32[]{:S(2)}, u32[]{:S(2)}) %all-to-all-start) | async-done | bytes 1179680 | tf_op jit(solution)/shard_map/all_to_all | solution.py:457
  45.9 1.3 %chunk_state.1 = (bf16[144,256]{1,0:T(8,128)(2,1)S(1)}, f32[1024,256]{1,0:T(8,128)S(1)}) custom-call(bf16[64,72,128]{2,1,0:T(8,128)(2,1)S(1)} %all-to-all-done.ref), custom_call_target="tpu_custom_call" | custom-call | tf_op jit(solution)/shard_map/chunk_state/pallas_call | solution.py:206
  47.2 4.0 %collective-permute-start = (bf16[144,256]{1,0:T(8,128)(2,1)S(1)}, bf16[144,256]{1,0:T(8,128)(2,1)S(1)}, u32[]{:S(2)}, u32[]{:S(2)}) collective-permute-start(bf16[144,256]{1,0:T(8,128)(2,1)S(1)} %get-tuple-element.15.own_ref), channel_id=1, source_target_pairs={{0,64},{64,0},{128,192},{192,128},{256,320},{320,256},{384,448},{4... | collective-permute-start | bytes 221192 | tf_op jit(solution)/shard_map/ppermute | solution.py:460
  51.3 2.8 %near_part.1 = (f32[1024,256]{1,0:T(8,128)S(1)}, bf16[1024,128]{1,0:T(8,128)(2,1)S(1)}) custom-call(bf16[64,72,128]{2,1,0:T(8,128)(2,1)S(1)} %all-to-all-done.ref, f32[1024,256]{1,0:T(8,128)S(1)} %get-tuple-element.12.cum_ref, f32[1,256]{1,0:T(1,128)S(1)} %broadcast_in_dim_reshape.3.gain_ref), custom_call_target="tpu_custom_call" | custom-call | flops 4000000000 | bytes 4194304 | tf_op jit(solution)/shard_map/near_part/pallas_call | solution.py:306
  54.0 0.0 collective-permute-done.partner_ref.pair_ref
  54.0 0.1 join_states.1.own_ref
  54.1 9.6 %collective-permute-start.3 = (bf16[144,256]{1,0:T(8,128)(2,1)S(1)}, bf16[144,256]{1,0:T(8,128)(2,1)S(1)}, u32[]{:S(2)}, u32[]{:S(2)}) collective-permute-start(bf16[144,256]{1,0:T(8,128)(2,1)S(1)} %join_states.1.own_ref), channel_id=1, source_target_pairs={{0,320},{64,256},{1,321},{65,257},{2,322},{66,258},{3,323},{67,259... | collective-permute-start | bytes 221192 | tf_op jit(solution)/shard_map/ppermute | solution.py:466
  63.7 1.3 %collective-permute-start.1 = (bf16[144,256]{1,0:T(8,128)(2,1)S(1)}, bf16[144,256]{1,0:T(8,128)(2,1)S(1)}, u32[]{:S(2)}, u32[]{:S(2)}) collective-permute-start(bf16[144,256]{1,0:T(8,128)(2,1)S(1)} %join_states.1.own_ref), channel_id=1, source_target_pairs={{0,192},{64,128},{128,320},{192,256},{1,193},{65,129},{129,321},{1... | collective-permute-start | bytes 221192 | tf_op jit(solution)/shard_map/ppermute | solution.py:466
  65.0 1.5 %levels_part.1 = (f32[1024,256]{1,0:T(8,128)S(1)}, f32[1024,256]{1,0:T(8,128)S(1)}, bf16[144,256]{1,0:T(8,128)(2,1)S(1)}) custom-call(bf16[64,72,128]{2,1,0:T(8,128)(2,1)S(1)} %all-to-all-done.ref, f32[1024,256]{1,0:T(8,128)S(1)} %get-tuple-element.12.cum_ref, bf16[1024,128]{1,0:T(8,128)(2,1)S(1)} %get-tuple-element.13.gate_ref, ...), custom_call_target="tpu_custom_call" | custom-call | flops 4000000000 | bytes 4194304 | tf_op jit(solution)/shard_map/levels_part/pallas_call | solution.py:368
  66.5 0.7 collective-permute-start.2
  67.2 0.0 collective-permute-done.3.first_ref
  67.2 0.0 collective-permute-done.1.before_ref
  67.2 0.7 collective-permute-start.4
  67.9 0.0 collective-permute-done.2.last_ref
  67.9 0.0 collective-permute-done.4.far_ref
  67.9 1.0 %outer_part.1 = bf16[64,16,256]{2,1,0:T(8,128)(2,1)S(1)} custom-call(s32[1]{0:T(128)} %bitcast.place_ref, bf16[64,72,128]{2,1,0:T(8,128)(2,1)S(1)} %all-to-all-done.ref, f32[1024,256]{1,0:T(8,128)S(1)} %get-tuple-element.16.inner_ref, f32[1024,256]{1,0:T(8,128)S(1)} %get-tuple-element.17.grow_ref, bf16[1024,128]{1,0:T(8,128)(2,1)S(1)} %get-tuple-element.13.gate_ref, ...), custom_call_target="tpu_custom_call" | custom-call | tf_op jit(solution)/shard_map/outer_part/pallas_call | solution.py:418
  68.9 24.0 %all_to_all.10.ref = bf16[64,16,256]{2,1,0:T(8,128)(2,1)S(1)} all-to-all(bf16[64,16,256]{2,1,0:T(8,128)(2,1)S(1)} %outer_part.1), channel_id=1, replica_groups=mesh['chunk'=8,'block'=4,'tp'=16] {'block','tp'}, dimensions={0} | all-to-all | bytes 1048576 | tf_op jit(solution)/shard_map/all_to_all | solution.py:476
  93.0 0.8 unpack_outputs.1
  (1 shorter events, 0.0 us)
Async XLA Ops:
  2.9 11.7 %copy-start = (f32[4]{0:T(128)S(1)}, f32[4]{0:T(128)}, u32[]{:S(2)}) copy-start(f32[4]{0:T(128)} %param.11) | copy-start | bytes 52
  2.9 43.0 %all-to-all-start = ((bf16[64,72,128]{2,1,0:T(8,128)(2,1)}), bf16[64,72,128]{2,1,0:T(8,128)(2,1)S(1)}, u32[]{:S(2)}, u32[]{:S(2)}) async-start(bf16[64,72,128]{2,1,0:T(8,128)(2,1)} %pack_messages.1), calls=%async_computation | async-start | bytes 2359296 | tf_op jit(solution)/shard_map/all_to_all | solution.py:457
  47.2 6.8 %collective-permute-start = (bf16[144,256]{1,0:T(8,128)(2,1)S(1)}, bf16[144,256]{1,0:T(8,128)(2,1)S(1)}, u32[]{:S(2)}, u32[]{:S(2)}) collective-permute-start(bf16[144,256]{1,0:T(8,128)(2,1)S(1)} %get-tuple-element.15.own_ref), channel_id=1, source_target_pairs={{0,64},{64,0},{128,192},{192,128},{256,320},{320,256},{384,448},{4... | collective-permute-start | bytes 221192 | tf_op jit(solution)/shard_map/ppermute | solution.py:460
  54.1 13.1 %collective-permute-start.3 = (bf16[144,256]{1,0:T(8,128)(2,1)S(1)}, bf16[144,256]{1,0:T(8,128)(2,1)S(1)}, u32[]{:S(2)}, u32[]{:S(2)}) collective-permute-start(bf16[144,256]{1,0:T(8,128)(2,1)S(1)} %join_states.1.own_ref), channel_id=1, source_target_pairs={{0,320},{64,256},{1,321},{65,257},{2,322},{66,258},{3,323},{67,259... | collective-permute-start | bytes 221192 | tf_op jit(solution)/shard_map/ppermute | solution.py:466
  63.7 3.5 %collective-permute-start.1 = (bf16[144,256]{1,0:T(8,128)(2,1)S(1)}, bf16[144,256]{1,0:T(8,128)(2,1)S(1)}, u32[]{:S(2)}, u32[]{:S(2)}) collective-permute-start(bf16[144,256]{1,0:T(8,128)(2,1)S(1)} %join_states.1.own_ref), channel_id=1, source_target_pairs={{0,192},{64,128},{128,320},{192,256},{1,193},{65,129},{129,321},{1... | collective-permute-start | bytes 221192 | tf_op jit(solution)/shard_map/ppermute | solution.py:466
  66.5 1.4 %collective-permute-start.2 = (bf16[144,256]{1,0:T(8,128)(2,1)S(1)}, bf16[144,256]{1,0:T(8,128)(2,1)S(1)}, u32[]{:S(2)}, u32[]{:S(2)}) collective-permute-start(bf16[144,256]{1,0:T(8,128)(2,1)S(1)} %get-tuple-element.18), channel_id=1, source_target_pairs={{256,448},{320,384},{257,449},{321,385},{258,450},{322,386},{259,4... | collective-permute-start | bytes 221192 | tf_op jit(solution)/shard_map/ppermute | solution.py:466
  67.2 0.7 collective-permute-start.4

commit v6 on v4

--- a/solution.py
+++ b/solution.py
@@ -241,6 +241,31 @@
     )(place, own, partner, near)
 
 
+def relay_kernel(place_ref, own_ref, before_ref, inner_ref, out_ref, shift_ref):
+    total = message_total(own_ref)
+    state = jnp.exp(total) * message_state(before_ref) + message_state(own_ref)
+    out_ref[0:STATE, :] = state.astype(BF16)
+    out_ref[STATE : STATE + 16, :] = split_rows(total + message_total(before_ref))
+    shift_ref[...] = jnp.where(place_ref[0] // 2 == 2, own_ref[...], out_ref[...])
+
+
+def relay(place, own, before, inner):
+    vmem = pl.BlockSpec(memory_space=pltpu.VMEM)
+    message = jax.ShapeDtypeStruct(own.shape, BF16)
+    return pl.pallas_call(
+        relay_kernel,
+        in_specs=[
+            pl.BlockSpec(memory_space=pltpu.SMEM),
+            vmem,
+            vmem,
+            pl.BlockSpec(memory_space=pl.ANY),
+        ],
+        out_shape=(message, message),
+        compiler_params=params(),
+        name="relay_states",
+    )(place, own, before, inner)
+
+
 def near_kernel(ref, cum_ref, gain_ref, out_ref, gate_ref, wide_ref):
     decode_gates(ref, wide_ref, gate_ref)
     gain = gain_ref[...]
@@ -348,7 +373,7 @@
     vmem = pl.BlockSpec(memory_space=pltpu.VMEM)
     return pl.pallas_call(
         levels_kernel,
-        in_specs=[vmem, vmem, vmem, vmem, pl.BlockSpec(memory_space=pl.ANY)],
+        in_specs=[vmem] * 4 + [pl.BlockSpec(memory_space=pl.ANY)],
         out_shape=(wide, wide),
         compiler_params=params(),
         cost_estimate=pl.CostEstimate(
@@ -365,23 +390,20 @@
     grow_ref,
     gate_ref,
     pair_ref,
-    top_ref,
+    one_ref,
+    shift_ref,
     skip_ref,
-    cross_ref,
-    low_ref,
     out_ref,
 ):
     place = place_ref[0]
-    in_half, odd = place % 2 == 1, place // 2 % 2 == 1
+    in_half, two, three = place % 2 == 1, place // 2 == 2, place // 2 == 3
     prefix = jnp.where(in_half, message_total(pair_ref), 0.0)
-    far_prefix = prefix + message_total(low_ref) + message_total(top_ref)
-    cross, skip = message_state(cross_ref), message_state(skip_ref)
-    late_total = jnp.where(odd, message_total(skip_ref), message_total(cross_ref))
-    joined = jnp.exp(late_total) * jnp.where(odd, cross, skip) + jnp.where(odd, skip, cross)
+    far_prefix = prefix + jnp.where(three, message_total(shift_ref), 0.0)
+    shifted = message_state(shift_ref)
     levels = (
         jnp.where(in_half, message_state(pair_ref), 0.0),
-        jnp.exp(prefix) * (message_state(low_ref) + message_state(top_ref)),
-        jnp.exp(far_prefix) * joined,
+        jnp.exp(prefix) * (message_state(one_ref) + jnp.where(three, shifted, 0.0)),
+        jnp.exp(far_prefix) * (jnp.where(two, shifted, 0.0) + message_state(skip_ref)),
     )
     levels = [jnp.concatenate(halves(value), axis=0) for value in levels]
     spreads = [spread(128, 11 + bit, LEVELS) for bit in range(3)]
@@ -401,7 +423,7 @@
     vmem = pl.BlockSpec(memory_space=pltpu.VMEM)
     return pl.pallas_call(
         outer_kernel,
-        in_specs=[pl.BlockSpec(memory_space=pltpu.SMEM)] + [vmem] * 9,
+        in_specs=[pl.BlockSpec(memory_space=pltpu.SMEM)] + [vmem] * 8,
         out_specs=vmem,
         out_shape=jax.ShapeDtypeStruct((64, 16, WIDTH), BF16),
         compiler_params=params(),
@@ -444,13 +466,17 @@
     pair = lax.ppermute(own, "chunk", [(source, source ^ 1) for source in range(8)])
     near, gates = near_part(received, cum, gain)
     own = join(place, own, pair, near)
-    steps = [[(2, 3)], [(0, 2), (1, 3)], [(0, 3), (1, 2)], [(0, 1)]]
-    shared = [
-        lax.ppermute(own, "chunk", [(2 * a + half, 2 * b + 1 - half) for a, b in step for half in (0, 1)])
-        for step in steps
-    ]
+
+    def up(value, *steps):
+        pairs = [(2 * a + half, 2 * b + 1 - half) for a, b in steps for half in (0, 1)]
+        return lax.ppermute(value, "chunk", pairs)
+
+    one = up(own, (0, 1))
     inner, grow = levels_part(received, cum, gates, near, own)
-    mixed = outer_part(place, received, inner, grow, gates, [pair] + shared)
+    joined, shifting = relay(place, own, one, inner)
+    shift = up(shifting, (1, 2), (2, 3))
+    skip = up(joined, (1, 3))
+    mixed = outer_part(place, received, inner, grow, gates, [pair, one, shift, skip])
     return unpack(lax.all_to_all(mixed, near_axes, 0, 0, tiled=True))
 
 

time: 97 us -> 92.9 us (0.958)
  the two profiles are of different devices: /device:TPU:1 before, /device:TPU:135 now
where the time goes in v6:
time: 92.9 us; the launch traced here: 92.6 us
  waiting for transfers between devices  35.5 us (38%)
  blocking collectives  24.6 us (26%)
  starting transfers between devices  21.9 us (24%)
  Pallas kernels  10.3 us (11%)
    all_to_all x1, waiting for transfers between devices, per_device(): received = lax.all_to_all(packed, near_axes, 0, 0, tiled=True)  31 us
    all_to_all x1, blocking collectives, per_device(): return unpack(lax.all_to_all(mixed, near_axes, 0, 0, tiled=True))  24.6 us
    all_to_all x1, starting transfers between devices, per_device(): received = lax.all_to_all(packed, near_axes, 0, 0, tiled=True)  11.1 us
    ppermute x3, starting transfers between devices, up(): return lax.ppermute(value, 'chunk', pairs)  6.74 us
    ppermute x3, waiting for transfers between devices, up(): return lax.ppermute(value, 'chunk', pairs)  4.44 us
    ppermute x1, starting transfers between devices, per_device(): lax.ppermute(own, 'chunk', [(source, source ^ 1) for source in range(8)])  4 us
    pallas_call x1, Pallas kernels, pack(): pl.pallas_call(pack_kernel, in_specs=[pl.BlockSpec(memory_space=pltpu.HBM...  2.87 us
    pallas_call x1, Pallas kernels, near_part(): pl.pallas_call(near_kernel, out_shape=(jax.ShapeDtypeStruct((CHUNK, WIDTH...  2.77 us
  transfers between devices with their start and end apart: 5, of which 3 were waited for; matrix products, arithmetic and copies ran while one was open for 0% of the time, Pallas kernels for 5%

profile of v6, /device:TPU:135, one launch (start us, length us, event | category | flops | bytes accessed | tf_op | source)
XLA Modules:
  0.0 92.6 jit_solution(10917018384238076887)
XLA Ops:
  0.0 2.9 %pack_messages.1 = bf16[64,72,128]{2,1,0:T(8,128)(2,1)} custom-call(bf16[4,16,4096]{2,1,0:T(8,128)(2,1)} %refs_0_.1, bf16[4,16,2048]{2,1,0:T(8,128)(2,1)} %refs_1_.1, bf16[4,16,2048]{2,1,0:T(8,128)(2,1)} %refs_2_.1, f32[4,16,64]{2,1,0:T(8,128)} %refs_3_.1, f32[4,16,896]{2,1,0:T(8,128)} %refs_4_.1), custom_call_target="tpu_custom_call" | custom-call | tf_op jit(solution)/shard_map/pack_messages/pallas_call | solution.py:89
  2.9 0.0 copy-start
  2.9 11.1 %all-to-all-start = ((bf16[64,72,128]{2,1,0:T(8,128)(2,1)}), bf16[64,72,128]{2,1,0:T(8,128)(2,1)S(1)}, u32[]{:S(2)}, u32[]{:S(2)}) async-start(bf16[64,72,128]{2,1,0:T(8,128)(2,1)} %pack_messages.1), calls=%async_computation | async-start | bytes 2359296 | tf_op jit(solution)/shard_map/all_to_all | solution.py:463
  14.0 0.0 copy-done
  14.0 0.1 broadcast_in_dim.7
  14.1 0.1 broadcast_in_dim_reshape.3.gain_ref
  14.2 31.0 %all-to-all-done.ref = bf16[64,72,128]{2,1,0:T(8,128)(2,1)S(1)} async-done(((bf16[64,72,128]{2,1,0:T(8,128)(2,1)}), bf16[64,72,128]{2,1,0:T(8,128)(2,1)S(1)}, u32[]{:S(2)}, u32[]{:S(2)}) %all-to-all-start) | async-done | bytes 1179680 | tf_op jit(solution)/shard_map/all_to_all | solution.py:463
  45.2 1.3 %chunk_state.1 = (bf16[144,256]{1,0:T(8,128)(2,1)S(1)}, f32[1024,256]{1,0:T(8,128)S(1)}) custom-call(bf16[64,72,128]{2,1,0:T(8,128)(2,1)S(1)} %all-to-all-done.ref), custom_call_target="tpu_custom_call" | custom-call | tf_op jit(solution)/shard_map/chunk_state/pallas_call | solution.py:206
  46.6 4.0 %collective-permute-start = (bf16[144,256]{1,0:T(8,128)(2,1)S(1)}, bf16[144,256]{1,0:T(8,128)(2,1)S(1)}, u32[]{:S(2)}, u32[]{:S(2)}) collective-permute-start(bf16[144,256]{1,0:T(8,128)(2,1)S(1)} %get-tuple-element.16.own_ref), channel_id=1, source_target_pairs={{0,64},{64,0},{128,192},{192,128},{256,320},{320,256},{384,448},{4... | collective-permute-start | bytes 221192 | tf_op jit(solution)/shard_map/ppermute | solution.py:466
  50.6 2.8 %near_part.1 = (f32[1024,256]{1,0:T(8,128)S(1)}, bf16[1024,128]{1,0:T(8,128)(2,1)S(1)}) custom-call(bf16[64,72,128]{2,1,0:T(8,128)(2,1)S(1)} %all-to-all-done.ref, f32[1024,256]{1,0:T(8,128)S(1)} %get-tuple-element.13.cum_ref, f32[1,256]{1,0:T(1,128)S(1)} %broadcast_in_dim_reshape.3.gain_ref), custom_call_target="tpu_custom_call" | custom-call | flops 4000000000 | bytes 4194304 | tf_op jit(solution)/shard_map/near_part/pallas_call | solution.py:313
  53.4 0.0 collective-permute-done.partner_ref.pair_ref
  53.4 1.3 %collective-permute-start.1 = (bf16[144,256]{1,0:T(8,128)(2,1)S(1)}, bf16[144,256]{1,0:T(8,128)(2,1)S(1)}, u32[]{:S(2)}, u32[]{:S(2)}) collective-permute-start(bf16[144,256]{1,0:T(8,128)(2,1)S(1)} %join_states.1.own_ref), channel_id=1, source_target_pairs={{0,192},{64,128},{1,193},{65,129},{2,194},{66,130},{3,195},{67,131... | collective-permute-start | bytes 221192 | tf_op jit(solution)/shard_map/ppermute | solution.py:472
  54.7 1.4 %levels_part.1 = (f32[1024,256]{1,0:T(8,128)S(1)}, f32[1024,256]{1,0:T(8,128)S(1)}) custom-call(bf16[64,72,128]{2,1,0:T(8,128)(2,1)S(1)} %all-to-all-done.ref, f32[1024,256]{1,0:T(8,128)S(1)} %get-tuple-element.13.cum_ref, bf16[1024,128]{1,0:T(8,128)(2,1)S(1)} %get-tuple-element.14.gate_ref, f32[1024,256]{1,0:T(8,128)S(1)} %get-tuple-element.15.near_ref, ...), custom_call_target="tpu_custom_call" | custom-call | flops 4000000000 | bytes 4194304 | tf_op jit(solution)/shard_map/levels_part/pallas_call | solution.py:374
  56.2 2.4 %collective-permute-done.1.before_ref.one_ref = bf16[144,256]{1,0:T(8,128)(2,1)S(1)} collective-permute-done((bf16[144,256]{1,0:T(8,128)(2,1)S(1)}, bf16[144,256]{1,0:T(8,128)(2,1)S(1)}, u32[]{:S(2)}, u32[]{:S(2)}) %collective-permute-start.1) | collective-permute-done | bytes 73760 | tf_op jit(solution)/shard_map/ppermute | solution.py:472
  58.6 3.2 %collective-permute-start.2 = (bf16[144,256]{1,0:T(8,128)(2,1)S(1)}, bf16[144,256]{1,0:T(8,128)(2,1)S(1)}, u32[]{:S(2)}, u32[]{:S(2)}) collective-permute-start(bf16[144,256]{1,0:T(8,128)(2,1)S(1)} %get-tuple-element.19), channel_id=1, source_target_pairs={{128,320},{192,256},{256,448},{320,384},{129,321},{193,257},{257,4... | collective-permute-start | bytes 221192 | tf_op jit(solution)/shard_map/ppermute | solution.py:472
  61.8 2.2 %collective-permute-start.3 = (bf16[144,256]{1,0:T(8,128)(2,1)S(1)}, bf16[144,256]{1,0:T(8,128)(2,1)S(1)}, u32[]{:S(2)}, u32[]{:S(2)}) collective-permute-start(bf16[144,256]{1,0:T(8,128)(2,1)S(1)} %get-tuple-element.20), channel_id=1, source_target_pairs={{128,448},{192,384},{129,449},{193,385},{130,450},{194,386},{131,4... | collective-permute-start | bytes 221192 | tf_op jit(solution)/shard_map/ppermute | solution.py:472
  64.1 0.0 collective-permute-done.2.shift_ref
  64.1 2.1 %collective-permute-done.3.skip_ref = bf16[144,256]{1,0:T(8,128)(2,1)S(1)} collective-permute-done((bf16[144,256]{1,0:T(8,128)(2,1)S(1)}, bf16[144,256]{1,0:T(8,128)(2,1)S(1)}, u32[]{:S(2)}, u32[]{:S(2)}) %collective-permute-start.3) | collective-permute-done | bytes 73760 | tf_op jit(solution)/shard_map/ppermute | solution.py:472
  66.1 1.0 %outer_part.1 = bf16[64,16,256]{2,1,0:T(8,128)(2,1)S(1)} custom-call(s32[1]{0:T(128)} %bitcast.place_ref, bf16[64,72,128]{2,1,0:T(8,128)(2,1)S(1)} %all-to-all-done.ref, f32[1024,256]{1,0:T(8,128)S(1)} %get-tuple-element.17.inner_ref, f32[1024,256]{1,0:T(8,128)S(1)} %get-tuple-element.18.grow_ref, bf16[1024,128]{1,0:T(8,128)(2,1)S(1)} %get-tuple-element.14.gate_ref, ...), custom_call_target="tpu_custom_call" | custom-call | tf_op jit(solution)/shard_map/outer_part/pallas_call | solution.py:424
  67.1 24.6 %all_to_all.10.ref = bf16[64,16,256]{2,1,0:T(8,128)(2,1)S(1)} all-to-all(bf16[64,16,256]{2,1,0:T(8,128)(2,1)S(1)} %outer_part.1), channel_id=1, replica_groups=mesh['chunk'=8,'block'=4,'tp'=16] {'block','tp'}, dimensions={0} | all-to-all | bytes 1048576 | tf_op jit(solution)/shard_map/all_to_all | solution.py:480
  91.7 0.8 unpack_outputs.1
  (2 shorter events, 0.1 us)
Async XLA Ops:
  2.9 11.2 %copy-start = (f32[4]{0:T(128)S(1)}, f32[4]{0:T(128)}, u32[]{:S(2)}) copy-start(f32[4]{0:T(128)} %param.11) | copy-start | bytes 52
  2.9 42.4 %all-to-all-start = ((bf16[64,72,128]{2,1,0:T(8,128)(2,1)}), bf16[64,72,128]{2,1,0:T(8,128)(2,1)S(1)}, u32[]{:S(2)}, u32[]{:S(2)}) async-start(bf16[64,72,128]{2,1,0:T(8,128)(2,1)} %pack_messages.1), calls=%async_computation | async-start | bytes 2359296 | tf_op jit(solution)/shard_map/all_to_all | solution.py:463
  46.6 6.8 %collective-permute-start = (bf16[144,256]{1,0:T(8,128)(2,1)S(1)}, bf16[144,256]{1,0:T(8,128)(2,1)S(1)}, u32[]{:S(2)}, u32[]{:S(2)}) collective-permute-start(bf16[144,256]{1,0:T(8,128)(2,1)S(1)} %get-tuple-element.16.own_ref), channel_id=1, source_target_pairs={{0,64},{64,0},{128,192},{192,128},{256,320},{320,256},{384,448},{4... | collective-permute-start | bytes 221192 | tf_op jit(solution)/shard_map/ppermute | solution.py:466
  53.4 5.1 %collective-permute-start.1 = (bf16[144,256]{1,0:T(8,128)(2,1)S(1)}, bf16[144,256]{1,0:T(8,128)(2,1)S(1)}, u32[]{:S(2)}, u32[]{:S(2)}) collective-permute-start(bf16[144,256]{1,0:T(8,128)(2,1)S(1)} %join_states.1.own_ref), channel_id=1, source_target_pairs={{0,192},{64,128},{1,193},{65,129},{2,194},{66,130},{3,195},{67,131... | collective-permute-start | bytes 221192 | tf_op jit(solution)/shard_map/ppermute | solution.py:472
  58.6 5.5 %collective-permute-start.2 = (bf16[144,256]{1,0:T(8,128)(2,1)S(1)}, bf16[144,256]{1,0:T(8,128)(2,1)S(1)}, u32[]{:S(2)}, u32[]{:S(2)}) collective-permute-start(bf16[144,256]{1,0:T(8,128)(2,1)S(1)} %get-tuple-element.19), channel_id=1, source_target_pairs={{128,320},{192,256},{256,448},{320,384},{129,321},{193,257},{257,4... | collective-permute-start | bytes 221192 | tf_op jit(solution)/shard_map/ppermute | solution.py:472
  61.8 4.3 %collective-permute-start.3 = (bf16[144,256]{1,0:T(8,128)(2,1)S(1)}, bf16[144,256]{1,0:T(8,128)(2,1)S(1)}, u32[]{:S(2)}, u32[]{:S(2)}) collective-permute-start(bf16[144,256]{1,0:T(8,128)(2,1)S(1)} %get-tuple-element.20), channel_id=1, source_target_pairs={{128,448},{192,384},{129,449},{193,385},{130,450},{194,386},{131,4... | collective-permute-start | bytes 221192 | tf_op jit(solution)/shard_map/ppermute | solution.py:472

commit v7 on v6

--- a/solution.py
+++ b/solution.py
@@ -325,7 +325,9 @@
     )(received, cum, gain)
 
 
-def levels_kernel(ref, cum_ref, gate_ref, near_ref, own_ref, out_ref, grow_ref):
+def levels_kernel(
+    place_ref, ref, cum_ref, gate_ref, near_ref, pair_ref, own_ref, out_ref, grow_ref
+):
     subs = CHUNK // SUB
     starts = [jnp.zeros((1, WIDTH), F32)]
     starts += [cum_ref[i * SUB - 1 : i * SUB, :] for i in range(1, subs + 1)]
@@ -366,21 +368,31 @@
     for i in range(1, subs):
         rows = slice(i * SUB, (i + 1) * SUB)
         grow_ref[rows, :] = grow_ref[rows, :] * jnp.exp(starts[i])
-
-
-def levels_part(received, cum, gates, near, own):
+    other = jnp.where(place_ref[0] % 2 == 1, message_state(pair_ref), 0.0)
+    other = jnp.concatenate(halves(other), axis=0)
+    to_lanes = spread(128, 11, LEVELS)
+    for k in range(CHUNK // BLOCK):
+        rows = slice(k * BLOCK, (k + 1) * BLOCK)
+        c = load_c(ref, k * BLOCK, BLOCK)
+        reached = dot(jnp.concatenate([c, c], axis=1), other)
+        out_ref[rows, :] += dot(gate_ref[rows, :], to_lanes) * grow_ref[rows, :] * reached
+
+
+def levels_part(place, received, cum, gates, near, pair, own):
     wide = jax.ShapeDtypeStruct((CHUNK, WIDTH), F32)
     vmem = pl.BlockSpec(memory_space=pltpu.VMEM)
     return pl.pallas_call(
         levels_kernel,
-        in_specs=[vmem] * 4 + [pl.BlockSpec(memory_space=pl.ANY)],
+        in_specs=[pl.BlockSpec(memory_space=pltpu.SMEM)]
+        + [vmem] * 5
+        + [pl.BlockSpec(memory_space=pl.ANY)],
         out_shape=(wide, wide),
         compiler_params=params(),
         cost_estimate=pl.CostEstimate(
             flops=4 * 10**9, bytes_accessed=4 * 1024 * 1024, transcendentals=10**6
         ),
         name="levels_part",
-    )(received, cum, gates, near, own)
+    )(place, received, cum, gates, near, pair, own)
 
 
 def outer_kernel(
@@ -401,19 +413,18 @@
     far_prefix = prefix + jnp.where(three, message_total(shift_ref), 0.0)
     shifted = message_state(shift_ref)
     levels = (
-        jnp.where(in_half, message_state(pair_ref), 0.0),
         jnp.exp(prefix) * (message_state(one_ref) + jnp.where(three, shifted, 0.0)),
         jnp.exp(far_prefix) * (jnp.where(two, shifted, 0.0) + message_state(skip_ref)),
     )
     levels = [jnp.concatenate(halves(value), axis=0) for value in levels]
-    spreads = [spread(128, 11 + bit, LEVELS) for bit in range(3)]
+    spreads = [spread(128, 12 + bit, LEVELS) for bit in range(2)]
     for k in range(CHUNK // BLOCK):
         rows = slice(k * BLOCK, (k + 1) * BLOCK)
         c = load_c(ref, k * BLOCK, BLOCK)
         c = jnp.concatenate([c, c], axis=1)
         gates = gate_ref[rows, :]
         total = jnp.zeros((BLOCK, WIDTH), F32)
-        for bit in range(3):
+        for bit in range(2):
             total += dot(gates, spreads[bit]) * dot(c, levels[bit])
         mixed = inner_ref[rows, :] + grow_ref[rows, :] * total
         out_ref[k * 16 : (k + 1) * 16] = mixed.astype(BF16).reshape(BLOCK // 16, 16, WIDTH)
@@ -472,7 +483,7 @@
         return lax.ppermute(value, "chunk", pairs)
 
     one = up(own, (0, 1))
-    inner, grow = levels_part(received, cum, gates, near, own)
+    inner, grow = levels_part(place, received, cum, gates, near, pair, own)
     joined, shifting = relay(place, own, one, inner)
     shift = up(shifting, (1, 2), (2, 3))
     skip = up(joined, (1, 3))

time: 92.9 us -> 92.9 us (level)
  no operation moved by 1% of the time
where the time goes in v7:
time: 92.9 us; the launch traced here: 92.6 us
  waiting for transfers between devices  35.2 us (38%)
  blocking collectives  24.6 us (26%)
  starting transfers between devices  22.1 us (24%)
  Pallas kernels  10.3 us (11%)
    all_to_all x1, waiting for transfers between devices, per_device(): received = lax.all_to_all(packed, near_axes, 0, 0, tiled=True)  31 us
    all_to_all x1, blocking collectives, per_device(): return unpack(lax.all_to_all(mixed, near_axes, 0, 0, tiled=True))  24.6 us
    all_to_all x1, starting transfers between devices, per_device(): received = lax.all_to_all(packed, near_axes, 0, 0, tiled=True)  11.1 us
    ppermute x3, starting transfers between devices, up(): return lax.ppermute(value, 'chunk', pairs)  7.01 us
    ppermute x3, waiting for transfers between devices, up(): return lax.ppermute(value, 'chunk', pairs)  4.16 us
    ppermute x1, starting transfers between devices, per_device(): lax.ppermute(own, 'chunk', [(source, source ^ 1) for source in range(8)])  4 us
    pallas_call x1, Pallas kernels, pack(): pl.pallas_call(pack_kernel, in_specs=[pl.BlockSpec(memory_space=pltpu.HBM...  2.87 us
    pallas_call x1, Pallas kernels, near_part(): pl.pallas_call(near_kernel, out_shape=(jax.ShapeDtypeStruct((CHUNK, WIDTH...  2.77 us
  transfers between devices with their start and end apart: 5, of which 3 were waited for; matrix products, arithmetic and copies ran while one was open for 0% of the time, Pallas kernels for 5%

profile of v7, /device:TPU:135, one launch (start us, length us, event | category | flops | bytes accessed | tf_op | source)
XLA Modules:
  0.0 92.6 jit_solution(8318309486967390746)
XLA Ops:
  0.0 2.9 %pack_messages.1 = bf16[64,72,128]{2,1,0:T(8,128)(2,1)} custom-call(bf16[4,16,4096]{2,1,0:T(8,128)(2,1)} %refs_0_.1, bf16[4,16,2048]{2,1,0:T(8,128)(2,1)} %refs_1_.1, bf16[4,16,2048]{2,1,0:T(8,128)(2,1)} %refs_2_.1, f32[4,16,64]{2,1,0:T(8,128)} %refs_3_.1, f32[4,16,896]{2,1,0:T(8,128)} %refs_4_.1), custom_call_target="tpu_custom_call" | custom-call | tf_op jit(solution)/shard_map/pack_messages/pallas_call | solution.py:89
  2.9 0.0 copy-start
  2.9 11.1 %all-to-all-start = ((bf16[64,72,128]{2,1,0:T(8,128)(2,1)}), bf16[64,72,128]{2,1,0:T(8,128)(2,1)S(1)}, u32[]{:S(2)}, u32[]{:S(2)}) async-start(bf16[64,72,128]{2,1,0:T(8,128)(2,1)} %pack_messages.1), calls=%async_computation | async-start | bytes 2359296 | tf_op jit(solution)/shard_map/all_to_all | solution.py:474
  14.0 0.0 copy-done
  14.0 0.1 broadcast_in_dim.7
  14.1 0.1 broadcast_in_dim_reshape.3.gain_ref
  14.2 31.0 %all-to-all-done.ref = bf16[64,72,128]{2,1,0:T(8,128)(2,1)S(1)} async-done(((bf16[64,72,128]{2,1,0:T(8,128)(2,1)}), bf16[64,72,128]{2,1,0:T(8,128)(2,1)S(1)}, u32[]{:S(2)}, u32[]{:S(2)}) %all-to-all-start) | async-done | bytes 1179680 | tf_op jit(solution)/shard_map/all_to_all | solution.py:474
  45.2 1.3 %chunk_state.1 = (bf16[144,256]{1,0:T(8,128)(2,1)S(1)}, f32[1024,256]{1,0:T(8,128)S(1)}) custom-call(bf16[64,72,128]{2,1,0:T(8,128)(2,1)S(1)} %all-to-all-done.ref), custom_call_target="tpu_custom_call" | custom-call | tf_op jit(solution)/shard_map/chunk_state/pallas_call | solution.py:206
  46.6 4.0 %collective-permute-start = (bf16[144,256]{1,0:T(8,128)(2,1)S(1)}, bf16[144,256]{1,0:T(8,128)(2,1)S(1)}, u32[]{:S(2)}, u32[]{:S(2)}) collective-permute-start(bf16[144,256]{1,0:T(8,128)(2,1)S(1)} %get-tuple-element.16.own_ref), channel_id=1, source_target_pairs={{0,64},{64,0},{128,192},{192,128},{256,320},{320,256},{384,448},{4... | collective-permute-start | bytes 221192 | tf_op jit(solution)/shard_map/ppermute | solution.py:477
  50.6 2.8 %near_part.1 = (f32[1024,256]{1,0:T(8,128)S(1)}, bf16[1024,128]{1,0:T(8,128)(2,1)S(1)}) custom-call(bf16[64,72,128]{2,1,0:T(8,128)(2,1)S(1)} %all-to-all-done.ref, f32[1024,256]{1,0:T(8,128)S(1)} %get-tuple-element.13.cum_ref, f32[1,256]{1,0:T(1,128)S(1)} %broadcast_in_dim_reshape.3.gain_ref), custom_call_target="tpu_custom_call" | custom-call | flops 4000000000 | bytes 4194304 | tf_op jit(solution)/shard_map/near_part/pallas_call | solution.py:313
  53.4 0.0 collective-permute-done.partner_ref.pair_ref
  53.4 1.3 %collective-permute-start.1 = (bf16[144,256]{1,0:T(8,128)(2,1)S(1)}, bf16[144,256]{1,0:T(8,128)(2,1)S(1)}, u32[]{:S(2)}, u32[]{:S(2)}) collective-permute-start(bf16[144,256]{1,0:T(8,128)(2,1)S(1)} %join_states.1.own_ref), channel_id=1, source_target_pairs={{0,192},{64,128},{1,193},{65,129},{2,194},{66,130},{3,195},{67,131... | collective-permute-start | bytes 221192 | tf_op jit(solution)/shard_map/ppermute | solution.py:483
  54.7 1.7 %levels_part.1 = (f32[1024,256]{1,0:T(8,128)S(1)}, f32[1024,256]{1,0:T(8,128)S(1)}) custom-call(s32[1]{0:T(128)} %bitcast.place_ref, bf16[64,72,128]{2,1,0:T(8,128)(2,1)S(1)} %all-to-all-done.ref, f32[1024,256]{1,0:T(8,128)S(1)} %get-tuple-element.13.cum_ref, bf16[1024,128]{1,0:T(8,128)(2,1)S(1)} %get-tuple-element.14.gate_ref, ...), custom_call_target="tpu_custom_call" | custom-call | flops 4000000000 | bytes 4194304 | tf_op jit(solution)/shard_map/levels_part/pallas_call | solution.py:384
  56.4 2.1 %collective-permute-done.1.before_ref.one_ref = bf16[144,256]{1,0:T(8,128)(2,1)S(1)} collective-permute-done((bf16[144,256]{1,0:T(8,128)(2,1)S(1)}, bf16[144,256]{1,0:T(8,128)(2,1)S(1)}, u32[]{:S(2)}, u32[]{:S(2)}) %collective-permute-start.1) | collective-permute-done | bytes 73760 | tf_op jit(solution)/shard_map/ppermute | solution.py:483
  58.6 3.5 %collective-permute-start.2 = (bf16[144,256]{1,0:T(8,128)(2,1)S(1)}, bf16[144,256]{1,0:T(8,128)(2,1)S(1)}, u32[]{:S(2)}, u32[]{:S(2)}) collective-permute-start(bf16[144,256]{1,0:T(8,128)(2,1)S(1)} %get-tuple-element.19), channel_id=1, source_target_pairs={{128,320},{192,256},{256,448},{320,384},{129,321},{193,257},{257,4... | collective-permute-start | bytes 221192 | tf_op jit(solution)/shard_map/ppermute | solution.py:483
  62.1 2.2 %collective-permute-start.3 = (bf16[144,256]{1,0:T(8,128)(2,1)S(1)}, bf16[144,256]{1,0:T(8,128)(2,1)S(1)}, u32[]{:S(2)}, u32[]{:S(2)}) collective-permute-start(bf16[144,256]{1,0:T(8,128)(2,1)S(1)} %get-tuple-element.20), channel_id=1, source_target_pairs={{128,448},{192,384},{129,449},{193,385},{130,450},{194,386},{131,4... | collective-permute-start | bytes 221192 | tf_op jit(solution)/shard_map/ppermute | solution.py:483
  64.3 0.0 collective-permute-done.2.shift_ref
  64.3 2.1 %collective-permute-done.3.skip_ref = bf16[144,256]{1,0:T(8,128)(2,1)S(1)} collective-permute-done((bf16[144,256]{1,0:T(8,128)(2,1)S(1)}, bf16[144,256]{1,0:T(8,128)(2,1)S(1)}, u32[]{:S(2)}, u32[]{:S(2)}) %collective-permute-start.3) | collective-permute-done | bytes 73760 | tf_op jit(solution)/shard_map/ppermute | solution.py:483
  66.4 0.7 outer_part.1
  67.1 24.6 %all_to_all.10.ref = bf16[64,16,256]{2,1,0:T(8,128)(2,1)S(1)} all-to-all(bf16[64,16,256]{2,1,0:T(8,128)(2,1)S(1)} %outer_part.1), channel_id=1, replica_groups=mesh['chunk'=8,'block'=4,'tp'=16] {'block','tp'}, dimensions={0} | all-to-all | bytes 1048576 | tf_op jit(solution)/shard_map/all_to_all | solution.py:491
  91.8 0.8 unpack_outputs.1
  (2 shorter events, 0.1 us)
Async XLA Ops:
  2.9 11.2 %copy-start = (f32[4]{0:T(128)S(1)}, f32[4]{0:T(128)}, u32[]{:S(2)}) copy-start(f32[4]{0:T(128)} %param.11) | copy-start | bytes 52
  2.9 42.4 %all-to-all-start = ((bf16[64,72,128]{2,1,0:T(8,128)(2,1)}), bf16[64,72,128]{2,1,0:T(8,128)(2,1)S(1)}, u32[]{:S(2)}, u32[]{:S(2)}) async-start(bf16[64,72,128]{2,1,0:T(8,128)(2,1)} %pack_messages.1), calls=%async_computation | async-start | bytes 2359296 | tf_op jit(solution)/shard_map/all_to_all | solution.py:474
  46.6 6.8 %collective-permute-start = (bf16[144,256]{1,0:T(8,128)(2,1)S(1)}, bf16[144,256]{1,0:T(8,128)(2,1)S(1)}, u32[]{:S(2)}, u32[]{:S(2)}) collective-permute-start(bf16[144,256]{1,0:T(8,128)(2,1)S(1)} %get-tuple-element.16.own_ref), channel_id=1, source_target_pairs={{0,64},{64,0},{128,192},{192,128},{256,320},{320,256},{384,448},{4... | collective-permute-start | bytes 221192 | tf_op jit(solution)/shard_map/ppermute | solution.py:477
  53.4 5.1 %collective-permute-start.1 = (bf16[144,256]{1,0:T(8,128)(2,1)S(1)}, bf16[144,256]{1,0:T(8,128)(2,1)S(1)}, u32[]{:S(2)}, u32[]{:S(2)}) collective-permute-start(bf16[144,256]{1,0:T(8,128)(2,1)S(1)} %join_states.1.own_ref), channel_id=1, source_target_pairs={{0,192},{64,128},{1,193},{65,129},{2,194},{66,130},{3,195},{67,131... | collective-permute-start | bytes 221192 | tf_op jit(solution)/shard_map/ppermute | solution.py:483
  58.6 5.7 %collective-permute-start.2 = (bf16[144,256]{1,0:T(8,128)(2,1)S(1)}, bf16[144,256]{1,0:T(8,128)(2,1)S(1)}, u32[]{:S(2)}, u32[]{:S(2)}) collective-permute-start(bf16[144,256]{1,0:T(8,128)(2,1)S(1)} %get-tuple-element.19), channel_id=1, source_target_pairs={{128,320},{192,256},{256,448},{320,384},{129,321},{193,257},{257,4... | collective-permute-start | bytes 221192 | tf_op jit(solution)/shard_map/ppermute | solution.py:483
  62.1 4.3 %collective-permute-start.3 = (bf16[144,256]{1,0:T(8,128)(2,1)S(1)}, bf16[144,256]{1,0:T(8,128)(2,1)S(1)}, u32[]{:S(2)}, u32[]{:S(2)}) collective-permute-start(bf16[144,256]{1,0:T(8,128)(2,1)S(1)} %get-tuple-element.20), channel_id=1, source_target_pairs={{128,448},{192,384},{129,449},{193,385},{130,450},{194,386},{131,4... | collective-permute-start | bytes 221192 | tf_op jit(solution)/shard_map/ppermute | solution.py:483
